TPU v7x, 32 devices: a whole 2x2x4 slice. The times are simulated.
32 devices in a mesh: grp: 2 (over x), comp: 16 (over z, y, core).
Axes of the slice: x: 2, y: 2, z: 4, core: 2. Of those that a mesh axis runs over, the one named last changes fastest.
Arguments:
- spectrum: float32 [1152, 96, 128], P(None, ('grp', 'comp')), parts along dimension 1, may hold values from 0.04 to 14, as said below
- sea_mask: int32 [96, 128], P(('grp', 'comp')), parts along dimension 0, may hold values 0 or 1
- ice_mask: int32 [96, 128], P(('grp', 'comp')), parts along dimension 0, may hold values 0 or 1
- wind: float32 [96, 128], P(('grp', 'comp')), parts along dimension 0, may hold values from 0.2 to 1
- source_matrix: bfloat16 [1152, 1152], replicated, may hold values from -0.1875 to 0.1875
Outputs:
- evolved: float32 [1152, 96, 128], P(None, ('grp', 'comp')), parts along dimension 1
There are 2 independent parts, one for each index of `grp`. A program takes and returns all parts, laid end to end along the dimension named above; an argument that names none is the same for every part. Nothing has to cross between parts.
Inputs may be any that keep to these rules, and one draw needn't show every extreme that they name: `spectrum`: positive spectral densities.
All inputs are finite; a program needn't handle non-finite values. No bound on the sum of `sea_mask` or of `ice_mask` on one device may be relied on, other than what follows from the above.
Results may differ from a plain program's by a relative error of at most 0.0014.
Values sent between devices are 32-bit elements; how exact they have to be, the bound alone decides.
No kernel may reach another device: no remote copies, remote signals or barrier semaphores. Data moves between devices by JAX's collectives and lax.ppermute only.
A program may use at most 64 MiB of HBM per device.

v0:
```python
import jax
import jax.numpy as jnp
from jax import lax
from jax.sharding import PartitionSpec as P

NDIR = 36
NFREQ = 32
K = 1152
STEPS = 2
SUBSTEPS = 3
SRC_SUB = 3


source_rate = 0.5
damping = 0.5


def extended(shard, sides, width):
    for axis, dim in sides:
        size, length = (lax.axis_size(axis), shard.shape[dim])
        up = [(i, (i + 1) % size) for i in range(size - 1)]
        down = [(j, i) for i, j in up]
        last = lax.slice_in_dim(shard, length - width, length, axis=dim)
        leading = lax.slice_in_dim(shard, 0, width, axis=dim)
        before = lax.ppermute(last, axis, up)
        after = lax.ppermute(leading, axis, down)
        shard = jnp.concatenate([before, shard, after], axis=dim)
    return shard


def courant(comp_index):
    direction = (comp_index % NDIR).astype(jnp.float32)
    frequency = (comp_index // NDIR).astype(jnp.float32)
    angles = 2.0 * jnp.pi * (direction + 0.5) / NDIR
    speeds = 0.6 * (0.35 + 0.65 * (NFREQ - 1 - frequency) / (NFREQ - 1))
    return ((speeds * jnp.cos(angles))[:, None, None], (speeds * jnp.sin(angles))[:, None, None])


def advance(spectra, courant_x, courant_y):
    western = jnp.roll(spectra, 1, axis=2)
    eastern = jnp.roll(spectra, -1, axis=2)
    zero_row = jnp.zeros_like(spectra[:, :1])
    southern = jnp.concatenate([zero_row, spectra[:, :-1]], axis=1)
    northern = jnp.concatenate([spectra[:, 1:], zero_row], axis=1)
    staying = 1.0 - jnp.abs(courant_x) - jnp.abs(courant_y)
    return (
        staying * spectra
        + jnp.maximum(courant_x, 0.0) * western
        + jnp.maximum(-courant_x, 0.0) * eastern
        + jnp.maximum(courant_y, 0.0) * southern
        + jnp.maximum(-courant_y, 0.0) * northern
    )


def sources(spectra, sea, wind, source_matrix):
    layout_shape = spectra.shape
    flattened = spectra.reshape(layout_shape[0], -1)
    sea_flat = sea.reshape(1, -1)
    wind_flat = wind.reshape(1, -1)
    for source_step in range(SRC_SUB):
        rounded = flattened.astype(jnp.bfloat16)
        growth = jnp.dot(source_matrix, rounded, preferred_element_type=jnp.float32)
        energy = jnp.mean(flattened * flattened, axis=0, keepdims=True)
        flattened = (
            sea_flat * (flattened + source_rate * wind_flat * growth) / (1.0 + damping * energy)
        )
    return flattened.reshape(layout_shape)


def on_device(spectrum, sea_mask, ice_mask, wind, source_matrix):
    sea_local = sea_mask.astype(jnp.float32)
    thaw = (1.0 - 0.5 * ice_mask.astype(jnp.float32))[None]
    spectra = spectrum
    courant_x, courant_y = courant(jnp.arange(K, dtype=jnp.int32))
    for outer_step in range(STEPS):
        for inner_step in range(SUBSTEPS):
            widened = extended(spectra, (("comp", 1),), 1)
            spectra = sea_local[None] * advance(widened, courant_x, courant_y)[:, 1:-1]
        spectra = sources(spectra, sea_local, wind, source_matrix) * thaw
    return spectra


def solution(mesh):
    return jax.shard_map(
        on_device,
        mesh=mesh,
        in_specs=(
            P(None, ("grp", "comp"), None),
            P(("grp", "comp"), None),
            P(("grp", "comp"), None),
            P(("grp", "comp"), None),
            P(),
        ),
        out_specs=P(None, ("grp", "comp"), None),
        check_vma=False,
    )
```

profile of v0, /device:TPU:1, one launch (start us, length us, event | category | flops | bytes accessed | tf_op | source)
XLA Modules:
  0.0 165.9 jit_solution(6611848075324589240)
XLA Ops:
  0.0 1.5 fusion.134
  1.5 4.7 %collective-permute-start = (f32[1152,1,128]{2,0,1:T(8,128)S(1)}, f32[1152,1,128]{2,0,1:T(8,128)S(1)}, u32[]{:S(2)}, u32[]{:S(2)}) collective-permute-start(f32[1152,1,128]{2,0,1:T(8,128)S(1)} %get-tuple-element.43), channel_id=1, source_target_pairs={{0,1},{1,2},{2,3},{3,4},{4,5},{5,6},{6,7},{7,8},{8,9},{9,10},{10,1... | collective-permute-start | bytes 1769480 | tf_op jit(solution)/shard_map/ppermute | solution.py:25
  6.2 1.9 %collective-permute-start.1 = (f32[1152,1,128]{2,0,1:T(8,128)S(1)}, f32[1152,1,128]{2,0,1:T(8,128)S(1)}, u32[]{:S(2)}, u32[]{:S(2)}) collective-permute-start(f32[1152,1,128]{2,0,1:T(8,128)S(1)} %get-tuple-element.44), channel_id=1, source_target_pairs={{1,0},{2,1},{3,2},{4,3},{5,4},{6,5},{7,6},{8,7},{9,8},{10,9},{11,1... | collective-permute-start | bytes 1769480 | tf_op jit(solution)/shard_map/ppermute | solution.py:26
  8.3 11.0 %collective-permute-done = f32[1152,1,128]{2,0,1:T(8,128)S(1)} collective-permute-done((f32[1152,1,128]{2,0,1:T(8,128)S(1)}, f32[1152,1,128]{2,0,1:T(8,128)S(1)}, u32[]{:S(2)}, u32[]{:S(2)}) %collective-permute-start) | collective-permute-done | bytes 589856 | tf_op jit(solution)/shard_map/ppermute | solution.py:25
  19.4 0.1 constant_dynamic-update-slice_fusion.1
  19.5 1.0 fusion.128
  20.5 1.0 fusion.127
  21.5 2.1 %fusion.82 = f32[1152,3,128]{2,0,1:T(8,128)S(1)} fusion(f32[1152,1,128]{2,0,1:T(8,128)S(1)} %collective-permute-done.1, f32[1152,3,128]{2,0,1:T(8,128)S(1)} %copy-done.1, f32[1152,1,128]{2,0,1:T(8,128)S(1)} %collective-permute-done, f32[1152,5,1]{2,0,1:T(8,128)S(1)} %get-tuple-element.30, f32[1152,5,127]{2,0,1:T(8,128)S(1)} %get-tuple-element.32, ...), kind=kLoop, calls=%fused_computation.129 | loop fusion | flops 9289728 | bytes 12410880 | tf_op jit(solution)/shard_map/mul | solution.py:78
  23.6 0.1 fusion.133
  23.6 4.4 %collective-permute-start.2 = (f32[1152,1,128]{2,0,1:T(8,128)S(1)}, f32[1152,1,128]{2,0,1:T(8,128)S(1)}, u32[]{:S(2)}, u32[]{:S(2)}) collective-permute-start(f32[1152,1,128]{2,0,1:T(8,128)S(1)} %get-tuple-element.41), channel_id=1, source_target_pairs={{0,1},{1,2},{2,3},{3,4},{4,5},{5,6},{6,7},{7,8},{8,9},{9,10},{10,1... | collective-permute-start | bytes 1769480 | tf_op jit(solution)/shard_map/ppermute | solution.py:25
  28.0 1.9 %collective-permute-start.3 = (f32[1152,1,128]{2,0,1:T(8,128)S(1)}, f32[1152,1,128]{2,0,1:T(8,128)S(1)}, u32[]{:S(2)}, u32[]{:S(2)}) collective-permute-start(f32[1152,1,128]{2,0,1:T(8,128)S(1)} %get-tuple-element.42), channel_id=1, source_target_pairs={{1,0},{2,1},{3,2},{4,3},{5,4},{6,5},{7,6},{8,7},{9,8},{10,9},{11,1... | collective-permute-start | bytes 1769480 | tf_op jit(solution)/shard_map/ppermute | solution.py:26
  30.0 11.2 %collective-permute-done.2 = f32[1152,1,128]{2,0,1:T(8,128)S(1)} collective-permute-done((f32[1152,1,128]{2,0,1:T(8,128)S(1)}, f32[1152,1,128]{2,0,1:T(8,128)S(1)}, u32[]{:S(2)}, u32[]{:S(2)}) %collective-permute-start.2) | collective-permute-done | bytes 589856 | tf_op jit(solution)/shard_map/ppermute | solution.py:25
  41.2 0.2 pad_maximum_fusion
  41.4 1.0 fusion.126
  42.3 1.0 fusion.125
  43.3 2.1 %fusion.71 = f32[1152,3,128]{2,0,1:T(8,128)S(1)} fusion(f32[1152,1,128]{2,0,1:T(8,128)S(1)} %collective-permute-done.3, f32[1152,3,128]{2,0,1:T(8,128)S(1)} %fusion.82, f32[1152,1,128]{2,0,1:T(8,128)S(1)} %collective-permute-done.2, f32[1152,5,1]{2,0,1:T(8,128)S(1)} %get-tuple-element.26, f32[1152,5,127]{2,0,1:T(8,128)S(1)} %get-tuple-element.28, ...), kind=kLoop, calls=%fused_computation.111 | loop fusion | flops 9289728 | bytes 12410880 | tf_op jit(solution)/shard_map/mul | solution.py:78
  45.4 0.1 fusion.132
  45.5 4.4 %collective-permute-start.4 = (f32[1152,1,128]{2,0,1:T(8,128)S(1)}, f32[1152,1,128]{2,0,1:T(8,128)S(1)}, u32[]{:S(2)}, u32[]{:S(2)}) collective-permute-start(f32[1152,1,128]{2,0,1:T(8,128)S(1)} %get-tuple-element.39), channel_id=1, source_target_pairs={{0,1},{1,2},{2,3},{3,4},{4,5},{5,6},{6,7},{7,8},{8,9},{9,10},{10,1... | collective-permute-start | bytes 1769480 | tf_op jit(solution)/shard_map/ppermute | solution.py:25
  49.9 2.1 %collective-permute-start.5 = (f32[1152,1,128]{2,0,1:T(8,128)S(1)}, f32[1152,1,128]{2,0,1:T(8,128)S(1)}, u32[]{:S(2)}, u32[]{:S(2)}) collective-permute-start(f32[1152,1,128]{2,0,1:T(8,128)S(1)} %get-tuple-element.40), channel_id=1, source_target_pairs={{1,0},{2,1},{3,2},{4,3},{5,4},{6,5},{7,6},{8,7},{9,8},{10,9},{11,1... | collective-permute-start | bytes 1769480 | tf_op jit(solution)/shard_map/ppermute | solution.py:26
  52.0 11.0 %collective-permute-done.4 = f32[1152,1,128]{2,0,1:T(8,128)S(1)} collective-permute-done((f32[1152,1,128]{2,0,1:T(8,128)S(1)}, f32[1152,1,128]{2,0,1:T(8,128)S(1)}, u32[]{:S(2)}, u32[]{:S(2)}) %collective-permute-start.4) | collective-permute-done | bytes 589856 | tf_op jit(solution)/shard_map/ppermute | solution.py:25
  63.0 0.2 pad_maximum_fusion.1
  63.2 1.0 fusion.124
  64.2 1.0 fusion.123
  65.1 3.0 %multiply_reduce_fusion.5 = (f32[3,128]{1,0:T(4,128)S(1)}, f32[1152,3,128]{2,0,1:T(8,128)}) fusion(f32[1152,1,128]{2,0,1:T(8,128)S(1)} %collective-permute-done.5, f32[1152,3,128]{2,0,1:T(8,128)S(1)} %fusion.71, f32[1152]{0:T(1024)S(1)} %get-tuple-element.55, f32[1152,1,128]{2,0,1:T(8,128)S(1)} %collective-permute-done.4, f32[1152]{0:T(1024)S(1)} %get-tuple-element.58, ...), kind=kLoop, calls=%fused_computation.153 | loop fusion | flops 10174080 | bytes 12412416 | tf_op jit(solution)/shard_map/reduce_sum | solution.py:63
  68.1 2.8 %copy.6 = f32[1152,3,128]{0,2,1:T(8,128)} copy(f32[1152,3,128]{2,0,1:T(8,128)} %get-tuple-element.8) | data formatting | bytes 3538944 | tf_op jit(solution)/shard_map/mul | solution.py:78
  70.9 1.7 %bitcast_convert_fusion.1 = bf16[1152,384]{0,1:T(8,128)(2,1)S(1)} fusion(f32[1152,3,128]{0,2,1:T(8,128)} %copy.6), kind=kLoop, calls=%fused_computation.147 | loop fusion | flops 442368 | bytes 2654208 | tf_op jit(solution)/shard_map/convert_element_type | solution.py:61
  72.6 0.3 copy-done.2
  72.9 1.7 %multiply_reduce_fusion.4 = (f32[384]{0:T(512)S(1)}, f32[1152,384]{0,1:T(8,128)S(1)}) fusion(f32[384]{0:T(512)S(1)} %add_bitcast_fusion.1, f32[1152,384]{0,1:T(8,128)S(1)} %bitcast.70, bf16[1152,384]{0,1:T(8,128)(2,1)S(1)} %bitcast_convert_fusion.1, bf16[1152,1152]{1,0:T(8,128)(2,1)S(1)} %copy-done, f32[384]{0:T(512)S(1)} %multiply_bitcast_fusion, ...), kind=kOutput, calls=%fused_computation.152 | convolution fusion | flops 1021869696 | bytes 7084032 | tf_op jit(solution)/shard_map/dot_general | solution.py:62
  74.6 1.7 %multiply_reduce_fusion.3 = (f32[384]{0:T(512)S(1)}, f32[1152,384]{0,1:T(8,128)S(1)}) fusion(f32[384]{0:T(512)S(1)} %multiply_add_fusion.3, f32[1152,384]{0,1:T(8,128)S(1)} %get-tuple-element.48, bf16[1152,1152]{1,0:T(8,128)(2,1)S(1)} %copy-done, f32[384]{0:T(512)S(1)} %multiply_bitcast_fusion, f32[384]{0:T(512)S(1)} %get-tuple-element.45), kind=kOutput, calls=%fused_computation.151 | convolution fusion | flops 1022312064 | bytes 6199296 | tf_op jit(solution)/shard_map/dot_general | solution.py:62
  76.4 2.7 %fusion.21 = f32[1152,384]{0,1:T(8,128)} fusion(f32[1152,384]{0,1:T(8,128)S(1)} %get-tuple-element.50, bf16[1152,1152]{1,0:T(8,128)(2,1)S(1)} %copy-done, f32[384]{0:T(512)S(1)} %multiply_add_fusion.2, f32[384]{0:T(512)S(1)} %multiply_bitcast_fusion, f32[384]{0:T(512)S(1)} %get-tuple-element.45), kind=kOutput, calls=%fused_computation.32 | convolution fusion | flops 1021427712 | bytes 6197760 | tf_op jit(solution)/shard_map/dot_general | solution.py:62
  79.1 2.8 %copy.7 = f32[1152,3,128]{2,0,1:T(8,128)} copy(f32[1152,3,128]{0,2,1:T(8,128)} %bitcast.73) | data formatting | bytes 3538944 | tf_op jit(solution)/shard_map/reshape | solution.py:67
  81.9 1.6 broadcast_multiply_fusion.1
  83.5 0.1 fusion.131
  83.6 4.4 %collective-permute-start.6 = (f32[1152,1,128]{2,0,1:T(8,128)S(1)}, f32[1152,1,128]{2,0,1:T(8,128)S(1)}, u32[]{:S(2)}, u32[]{:S(2)}) collective-permute-start(f32[1152,1,128]{2,0,1:T(8,128)S(1)} %get-tuple-element.37), channel_id=1, source_target_pairs={{0,1},{1,2},{2,3},{3,4},{4,5},{5,6},{6,7},{7,8},{8,9},{9,10},{10,1... | collective-permute-start | bytes 1769480 | tf_op jit(solution)/shard_map/ppermute | solution.py:25
  88.0 1.9 %collective-permute-start.7 = (f32[1152,1,128]{2,0,1:T(8,128)S(1)}, f32[1152,1,128]{2,0,1:T(8,128)S(1)}, u32[]{:S(2)}, u32[]{:S(2)}) collective-permute-start(f32[1152,1,128]{2,0,1:T(8,128)S(1)} %get-tuple-element.38), channel_id=1, source_target_pairs={{1,0},{2,1},{3,2},{4,3},{5,4},{6,5},{7,6},{8,7},{9,8},{10,9},{11,1... | collective-permute-start | bytes 1769480 | tf_op jit(solution)/shard_map/ppermute | solution.py:26
  89.9 11.2 %collective-permute-done.6 = f32[1152,1,128]{2,0,1:T(8,128)S(1)} collective-permute-done((f32[1152,1,128]{2,0,1:T(8,128)S(1)}, f32[1152,1,128]{2,0,1:T(8,128)S(1)}, u32[]{:S(2)}, u32[]{:S(2)}) %collective-permute-start.6) | collective-permute-done | bytes 589856 | tf_op jit(solution)/shard_map/ppermute | solution.py:25
  101.1 0.2 pad_maximum_fusion.2
  101.3 1.0 fusion.122
  102.3 1.0 fusion.121
  103.2 2.1 %fusion.49 = f32[1152,3,128]{2,0,1:T(8,128)S(1)} fusion(f32[1152,1,128]{2,0,1:T(8,128)S(1)} %collective-permute-done.7, f32[1152,3,128]{2,0,1:T(8,128)S(1)} %broadcast_multiply_fusion.1, f32[1152,1,128]{2,0,1:T(8,128)S(1)} %collective-permute-done.6, f32[1152,5,1]{2,0,1:T(8,128)S(1)} %get-tuple-element.18, f32[1152,5,127]{2,0,1:T(8,128)S(1)} %get-tuple-element.20, ...), kind=kLoop, calls=%fused_computation.75 | loop fusion | flops 9289728 | bytes 12410880 | tf_op jit(solution)/shard_map/mul | solution.py:78
  105.3 0.1 fusion.130
  105.4 4.4 %collective-permute-start.8 = (f32[1152,1,128]{2,0,1:T(8,128)S(1)}, f32[1152,1,128]{2,0,1:T(8,128)S(1)}, u32[]{:S(2)}, u32[]{:S(2)}) collective-permute-start(f32[1152,1,128]{2,0,1:T(8,128)S(1)} %get-tuple-element.35), channel_id=1, source_target_pairs={{0,1},{1,2},{2,3},{3,4},{4,5},{5,6},{6,7},{7,8},{8,9},{9,10},{10,1... | collective-permute-start | bytes 1769480 | tf_op jit(solution)/shard_map/ppermute | solution.py:25
  109.8 2.1 %collective-permute-start.9 = (f32[1152,1,128]{2,0,1:T(8,128)S(1)}, f32[1152,1,128]{2,0,1:T(8,128)S(1)}, u32[]{:S(2)}, u32[]{:S(2)}) collective-permute-start(f32[1152,1,128]{2,0,1:T(8,128)S(1)} %get-tuple-element.36), channel_id=1, source_target_pairs={{1,0},{2,1},{3,2},{4,3},{5,4},{6,5},{7,6},{8,7},{9,8},{10,9},{11,1... | collective-permute-start | bytes 1769480 | tf_op jit(solution)/shard_map/ppermute | solution.py:26
  111.9 11.0 %collective-permute-done.8 = f32[1152,1,128]{2,0,1:T(8,128)S(1)} collective-permute-done((f32[1152,1,128]{2,0,1:T(8,128)S(1)}, f32[1152,1,128]{2,0,1:T(8,128)S(1)}, u32[]{:S(2)}, u32[]{:S(2)}) %collective-permute-start.8) | collective-permute-done | bytes 589856 | tf_op jit(solution)/shard_map/ppermute | solution.py:25
  122.9 0.2 pad_maximum_fusion.3
  123.1 1.0 fusion.120
  124.1 1.0 fusion.119
  125.0 2.1 %fusion.38 = f32[1152,3,128]{2,0,1:T(8,128)S(1)} fusion(f32[1152,1,128]{2,0,1:T(8,128)S(1)} %collective-permute-done.9, f32[1152,3,128]{2,0,1:T(8,128)S(1)} %fusion.49, f32[1152,1,128]{2,0,1:T(8,128)S(1)} %collective-permute-done.8, f32[1152,5,1]{2,0,1:T(8,128)S(1)} %get-tuple-element.14, f32[1152,5,127]{2,0,1:T(8,128)S(1)} %get-tuple-element.16, ...), kind=kLoop, calls=%fused_computation.57 | loop fusion | flops 9289728 | bytes 12410880 | tf_op jit(solution)/shard_map/mul | solution.py:78
  127.1 0.1 fusion.129
  127.2 4.4 %collective-permute-start.10 = (f32[1152,1,128]{2,0,1:T(8,128)S(1)}, f32[1152,1,128]{2,0,1:T(8,128)S(1)}, u32[]{:S(2)}, u32[]{:S(2)}) collective-permute-start(f32[1152,1,128]{2,0,1:T(8,128)S(1)} %get-tuple-element.33), channel_id=1, source_target_pairs={{0,1},{1,2},{2,3},{3,4},{4,5},{5,6},{6,7},{7,8},{8,9},{9,10},{10,1... | collective-permute-start | bytes 1769480 | tf_op jit(solution)/shard_map/ppermute | solution.py:25
  131.6 1.9 %collective-permute-start.11 = (f32[1152,1,128]{2,0,1:T(8,128)S(1)}, f32[1152,1,128]{2,0,1:T(8,128)S(1)}, u32[]{:S(2)}, u32[]{:S(2)}) collective-permute-start(f32[1152,1,128]{2,0,1:T(8,128)S(1)} %get-tuple-element.34), channel_id=1, source_target_pairs={{1,0},{2,1},{3,2},{4,3},{5,4},{6,5},{7,6},{8,7},{9,8},{10,9},{11,1... | collective-permute-start | bytes 1769480 | tf_op jit(solution)/shard_map/ppermute | solution.py:26
  133.5 10.7 %collective-permute-done.10 = f32[1152,1,128]{2,0,1:T(8,128)S(1)} collective-permute-done((f32[1152,1,128]{2,0,1:T(8,128)S(1)}, f32[1152,1,128]{2,0,1:T(8,128)S(1)}, u32[]{:S(2)}, u32[]{:S(2)}) %collective-permute-start.10) | collective-permute-done | bytes 589856 | tf_op jit(solution)/shard_map/ppermute | solution.py:25
  144.2 0.2 pad_maximum_fusion.4
  144.4 1.0 fusion.118
  145.4 1.0 fusion.117
  146.4 3.0 %multiply_reduce_fusion.2 = (f32[3,128]{1,0:T(4,128)S(1)}, f32[1152,3,128]{2,0,1:T(8,128)}) fusion(f32[1152,1,128]{2,0,1:T(8,128)S(1)} %collective-permute-done.11, f32[1152,3,128]{2,0,1:T(8,128)S(1)} %fusion.38, f32[1152]{0:T(1024)S(1)} %get-tuple-element.55, f32[1152,1,128]{2,0,1:T(8,128)S(1)} %collective-permute-done.10, f32[1152]{0:T(1024)S(1)} %get-tuple-element.58, ...), kind=kLoop, calls=%fused_computation.150 | loop fusion | flops 10174080 | bytes 12412416 | tf_op jit(solution)/shard_map/reduce_sum | solution.py:63
  149.3 2.8 %copy.8 = f32[1152,3,128]{0,2,1:T(8,128)} copy(f32[1152,3,128]{2,0,1:T(8,128)} %get-tuple-element.6) | data formatting | bytes 3538944 | tf_op jit(solution)/shard_map/mul | solution.py:78
  152.1 1.7 %bitcast_convert_fusion = bf16[1152,384]{0,1:T(8,128)(2,1)S(1)} fusion(f32[1152,3,128]{0,2,1:T(8,128)} %copy.8), kind=kLoop, calls=%fused_computation.146 | loop fusion | flops 442368 | bytes 2654208 | tf_op jit(solution)/shard_map/convert_element_type | solution.py:61
  153.8 0.3 copy-done.3
  154.2 1.7 %multiply_reduce_fusion.1 = (f32[384]{0:T(512)S(1)}, f32[1152,384]{0,1:T(8,128)S(1)}) fusion(f32[384]{0:T(512)S(1)} %add_bitcast_fusion, f32[1152,384]{0,1:T(8,128)S(1)} %bitcast.71, bf16[1152,384]{0,1:T(8,128)(2,1)S(1)} %bitcast_convert_fusion, bf16[1152,1152]{1,0:T(8,128)(2,1)S(1)} %copy-done, f32[384]{0:T(512)S(1)} %multiply_bitcast_fusion, ...), kind=kOutput, calls=%fused_computation.149 | convolution fusion | flops 1021869696 | bytes 7084032 | tf_op jit(solution)/shard_map/dot_general | solution.py:62
  155.9 1.7 %multiply_reduce_fusion = (f32[384]{0:T(512)S(1)}, f32[1152,384]{0,1:T(8,128)S(1)}) fusion(f32[384]{0:T(512)S(1)} %multiply_add_fusion.1, f32[1152,384]{0,1:T(8,128)S(1)} %get-tuple-element.52, bf16[1152,1152]{1,0:T(8,128)(2,1)S(1)} %copy-done, f32[384]{0:T(512)S(1)} %multiply_bitcast_fusion, f32[384]{0:T(512)S(1)} %get-tuple-element.45), kind=kOutput, calls=%fused_computation.148 | convolution fusion | flops 1022312064 | bytes 6199296 | tf_op jit(solution)/shard_map/dot_general | solution.py:62
  157.6 2.7 %fusion.18 = f32[1152,384]{0,1:T(8,128)} fusion(f32[1152,384]{0,1:T(8,128)S(1)} %get-tuple-element.54, bf16[1152,1152]{1,0:T(8,128)(2,1)S(1)} %copy-done, f32[384]{0:T(512)S(1)} %multiply_add_fusion, f32[384]{0:T(512)S(1)} %multiply_bitcast_fusion, f32[384]{0:T(512)S(1)} %get-tuple-element.45), kind=kOutput, calls=%fused_computation.29 | convolution fusion | flops 1021427712 | bytes 6197760 | tf_op jit(solution)/shard_map/dot_general | solution.py:62
  160.3 2.8 %copy.9 = f32[1152,3,128]{2,0,1:T(8,128)} copy(f32[1152,3,128]{0,2,1:T(8,128)} %bitcast.72) | data formatting | bytes 3538944 | tf_op jit(solution)/shard_map/reshape | solution.py:67
  163.1 2.8 %broadcast_multiply_fusion = f32[1152,3,128]{2,0,1:T(8,128)} fusion(f32[1152,3,128]{2,0,1:T(8,128)} %copy.9, f32[3,128]{1,0:T(4,128)S(1)} %multiply_subtract_fusion), kind=kLoop, calls=%fused_computation.156 | loop fusion | flops 442368 | bytes 3540480 | tf_op jit(solution)/shard_map/mul | solution.py:79
  (32 shorter events, 0.4 us)
Async XLA Ops:
  0.0 72.6 %copy-start = (bf16[1152,1152]{1,0:T(8,128)(2,1)S(1)}, bf16[1152,1152]{1,0:T(8,128)(2,1)}, u32[]{:S(2)}) copy-start(bf16[1152,1152]{1,0:T(8,128)(2,1)} %param.9) | copy-start | bytes 7962628
  0.0 19.3 %copy-start.1 = (f32[1152,3,128]{2,0,1:T(8,128)S(1)}, f32[1152,3,128]{2,0,1:T(8,128)}, u32[]{:S(2)}) copy-start(f32[1152,3,128]{2,0,1:T(8,128)} %param.5) | copy-start | bytes 5308420
  0.0 8.2 %copy-start.4 = (s32[3,128]{1,0:T(4,128)S(1)}, s32[3,128]{1,0:T(4,128)}, u32[]{:S(2)}) copy-start(s32[3,128]{1,0:T(4,128)} %param.6) | copy-start | bytes 4612
  1.5 17.8 %collective-permute-start = (f32[1152,1,128]{2,0,1:T(8,128)S(1)}, f32[1152,1,128]{2,0,1:T(8,128)S(1)}, u32[]{:S(2)}, u32[]{:S(2)}) collective-permute-start(f32[1152,1,128]{2,0,1:T(8,128)S(1)} %get-tuple-element.43), channel_id=1, source_target_pairs={{0,1},{1,2},{2,3},{3,4},{4,5},{5,6},{6,7},{7,8},{8,9},{9,10},{10,1... | collective-permute-start | bytes 1769480 | tf_op jit(solution)/shard_map/ppermute | solution.py:25
  6.2 13.3 %collective-permute-start.1 = (f32[1152,1,128]{2,0,1:T(8,128)S(1)}, f32[1152,1,128]{2,0,1:T(8,128)S(1)}, u32[]{:S(2)}, u32[]{:S(2)}) collective-permute-start(f32[1152,1,128]{2,0,1:T(8,128)S(1)} %get-tuple-element.44), channel_id=1, source_target_pairs={{1,0},{2,1},{3,2},{4,3},{5,4},{6,5},{7,6},{8,7},{9,8},{10,9},{11,1... | collective-permute-start | bytes 1769480 | tf_op jit(solution)/shard_map/ppermute | solution.py:26
  23.6 17.5 %collective-permute-start.2 = (f32[1152,1,128]{2,0,1:T(8,128)S(1)}, f32[1152,1,128]{2,0,1:T(8,128)S(1)}, u32[]{:S(2)}, u32[]{:S(2)}) collective-permute-start(f32[1152,1,128]{2,0,1:T(8,128)S(1)} %get-tuple-element.41), channel_id=1, source_target_pairs={{0,1},{1,2},{2,3},{3,4},{4,5},{5,6},{6,7},{7,8},{8,9},{9,10},{10,1... | collective-permute-start | bytes 1769480 | tf_op jit(solution)/shard_map/ppermute | solution.py:25
  28.0 13.1 %collective-permute-start.3 = (f32[1152,1,128]{2,0,1:T(8,128)S(1)}, f32[1152,1,128]{2,0,1:T(8,128)S(1)}, u32[]{:S(2)}, u32[]{:S(2)}) collective-permute-start(f32[1152,1,128]{2,0,1:T(8,128)S(1)} %get-tuple-element.42), channel_id=1, source_target_pairs={{1,0},{2,1},{3,2},{4,3},{5,4},{6,5},{7,6},{8,7},{9,8},{10,9},{11,1... | collective-permute-start | bytes 1769480 | tf_op jit(solution)/shard_map/ppermute | solution.py:26
  45.4 6.6 %copy-start.5 = (f32[3,128]{1,0:T(4,128)S(1)}, f32[3,128]{1,0:T(4,128)}, u32[]{:S(2)}) copy-start(f32[3,128]{1,0:T(4,128)} %param.8) | copy-start | bytes 4612
  45.4 6.6 %copy-start.6 = (s32[3,128]{1,0:T(4,128)S(1)}, s32[3,128]{1,0:T(4,128)}, u32[]{:S(2)}) copy-start(s32[3,128]{1,0:T(4,128)} %param.7) | copy-start | bytes 4612
  45.5 17.5 %collective-permute-start.4 = (f32[1152,1,128]{2,0,1:T(8,128)S(1)}, f32[1152,1,128]{2,0,1:T(8,128)S(1)}, u32[]{:S(2)}, u32[]{:S(2)}) collective-permute-start(f32[1152,1,128]{2,0,1:T(8,128)S(1)} %get-tuple-element.39), channel_id=1, source_target_pairs={{0,1},{1,2},{2,3},{3,4},{4,5},{5,6},{6,7},{7,8},{8,9},{9,10},{10,1... | collective-permute-start | bytes 1769480 | tf_op jit(solution)/shard_map/ppermute | solution.py:25
  49.9 13.1 %collective-permute-start.5 = (f32[1152,1,128]{2,0,1:T(8,128)S(1)}, f32[1152,1,128]{2,0,1:T(8,128)S(1)}, u32[]{:S(2)}, u32[]{:S(2)}) collective-permute-start(f32[1152,1,128]{2,0,1:T(8,128)S(1)} %get-tuple-element.40), channel_id=1, source_target_pairs={{1,0},{2,1},{3,2},{4,3},{5,4},{6,5},{7,6},{8,7},{9,8},{10,9},{11,1... | collective-permute-start | bytes 1769480 | tf_op jit(solution)/shard_map/ppermute | solution.py:26
  70.9 2.0 %copy-start.2 = (f32[1152,3,128]{0,2,1:T(8,128)S(1)}, f32[1152,3,128]{0,2,1:T(8,128)}, u32[]{:S(2)}) copy-start(f32[1152,3,128]{0,2,1:T(8,128)} %copy.6) | copy-start | bytes 5308420
  83.6 17.5 %collective-permute-start.6 = (f32[1152,1,128]{2,0,1:T(8,128)S(1)}, f32[1152,1,128]{2,0,1:T(8,128)S(1)}, u32[]{:S(2)}, u32[]{:S(2)}) collective-permute-start(f32[1152,1,128]{2,0,1:T(8,128)S(1)} %get-tuple-element.37), channel_id=1, source_target_pairs={{0,1},{1,2},{2,3},{3,4},{4,5},{5,6},{6,7},{7,8},{8,9},{9,10},{10,1... | collective-permute-start | bytes 1769480 | tf_op jit(solution)/shard_map/ppermute | solution.py:25
  88.0 13.1 %collective-permute-start.7 = (f32[1152,1,128]{2,0,1:T(8,128)S(1)}, f32[1152,1,128]{2,0,1:T(8,128)S(1)}, u32[]{:S(2)}, u32[]{:S(2)}) collective-permute-start(f32[1152,1,128]{2,0,1:T(8,128)S(1)} %get-tuple-element.38), channel_id=1, source_target_pairs={{1,0},{2,1},{3,2},{4,3},{5,4},{6,5},{7,6},{8,7},{9,8},{10,9},{11,1... | collective-permute-start | bytes 1769480 | tf_op jit(solution)/shard_map/ppermute | solution.py:26
  105.4 17.5 %collective-permute-start.8 = (f32[1152,1,128]{2,0,1:T(8,128)S(1)}, f32[1152,1,128]{2,0,1:T(8,128)S(1)}, u32[]{:S(2)}, u32[]{:S(2)}) collective-permute-start(f32[1152,1,128]{2,0,1:T(8,128)S(1)} %get-tuple-element.35), channel_id=1, source_target_pairs={{0,1},{1,2},{2,3},{3,4},{4,5},{5,6},{6,7},{7,8},{8,9},{9,10},{10,1... | collective-permute-start | bytes 1769480 | tf_op jit(solution)/shard_map/ppermute | solution.py:25
  109.8 13.1 %collective-permute-start.9 = (f32[1152,1,128]{2,0,1:T(8,128)S(1)}, f32[1152,1,128]{2,0,1:T(8,128)S(1)}, u32[]{:S(2)}, u32[]{:S(2)}) collective-permute-start(f32[1152,1,128]{2,0,1:T(8,128)S(1)} %get-tuple-element.36), channel_id=1, source_target_pairs={{1,0},{2,1},{3,2},{4,3},{5,4},{6,5},{7,6},{8,7},{9,8},{10,9},{11,1... | collective-permute-start | bytes 1769480 | tf_op jit(solution)/shard_map/ppermute | solution.py:26
  127.2 17.0 %collective-permute-start.10 = (f32[1152,1,128]{2,0,1:T(8,128)S(1)}, f32[1152,1,128]{2,0,1:T(8,128)S(1)}, u32[]{:S(2)}, u32[]{:S(2)}) collective-permute-start(f32[1152,1,128]{2,0,1:T(8,128)S(1)} %get-tuple-element.33), channel_id=1, source_target_pairs={{0,1},{1,2},{2,3},{3,4},{4,5},{5,6},{6,7},{7,8},{8,9},{9,10},{10,1... | collective-permute-start | bytes 1769480 | tf_op jit(solution)/shard_map/ppermute | solution.py:25
  131.6 12.6 %collective-permute-start.11 = (f32[1152,1,128]{2,0,1:T(8,128)S(1)}, f32[1152,1,128]{2,0,1:T(8,128)S(1)}, u32[]{:S(2)}, u32[]{:S(2)}) collective-permute-start(f32[1152,1,128]{2,0,1:T(8,128)S(1)} %get-tuple-element.34), channel_id=1, source_target_pairs={{1,0},{2,1},{3,2},{4,3},{5,4},{6,5},{7,6},{8,7},{9,8},{10,9},{11,1... | collective-permute-start | bytes 1769480 | tf_op jit(solution)/shard_map/ppermute | solution.py:26
  152.1 2.0 %copy-start.3 = (f32[1152,3,128]{0,2,1:T(8,128)S(1)}, f32[1152,3,128]{0,2,1:T(8,128)}, u32[]{:S(2)}) copy-start(f32[1152,3,128]{0,2,1:T(8,128)} %copy.8) | copy-start | bytes 5308420
where the time goes:
time: 167 us; the launch traced here: 166 us
  waiting for transfers between devices  66 us (40%)
  starting transfers between devices  38.5 us (23%)
  local copies, waits for them, and re-layouts  25.3 us (15%)
  other arithmetic  23.3 us (14%)
  matrix products  12.3 us (7%)
    ppermute x6, waiting for transfers between devices, extended(): before = lax.ppermute(last, axis, up)  66 us
    ppermute x6, starting transfers between devices, extended(): before = lax.ppermute(last, axis, up)  26.6 us
    dot_general x6, matrix products, sources(): growth = jnp.dot(source_matrix, rounded, preferred_element_type=jnp.float32)  12.3 us
    ppermute x6, starting transfers between devices, extended(): after = lax.ppermute(leading, axis, down)  11.9 us
    slice x12, local copies, waits for them, and re-layouts, advance(): western = jnp.roll(spectra, 1, axis=2)  11.4 us
    mul x4, other arithmetic, on_device(): spectra = sea_local[None] * advance(widened, courant_x, courant_y)[:, 1:-1]  8.34 us
    reduce_sum x2, other arithmetic, sources(): energy = jnp.mean(flattened * flattened, axis=0, keepdims=True)  5.96 us
    reshape x2, local copies, waits for them, and re-layouts, sources(): return flattened.reshape(layout_shape)  5.6 us
  transfers between devices with their start and end apart: 12, of which 6 were waited for; matrix products, arithmetic and copies ran while one was open for 0% of the time, Pallas kernels for 0%

commit v1 on v0

v1 whole, which is shorter than its diff:
```python
import functools

import jax
import jax.numpy as jnp
import numpy as np
from jax import lax
from jax.experimental import pallas as pl
from jax.experimental.pallas import tpu as pltpu
from jax.sharding import PartitionSpec as P

NDIR = 36
NFREQ = 32
K = 1152
STEPS = 2
SUBSTEPS = 3
SRC_SUB = 3

source_rate = 0.5
damping = 0.5

SUB = 8
PERIOD = 2 * NDIR
TILES = PERIOD // SUB
BLOCK = 2 * PERIOD
BLOCKS = K // BLOCK
BTILES = 2 * TILES
HALF = BLOCK // 2
HTILES = BTILES // 2


def split_of(positive, tile):
    rows = [positive((tile * SUB + i) % NDIR) for i in range(SUB)]
    if all(rows):
        return 1
    if not any(rows):
        return -1
    return [i for i in range(SUB) if rows[i]]


def north_going(d):
    return d < NDIR // 2


def east_going(d):
    return d < NDIR // 4 or d >= 3 * NDIR // 4


Y_SPLIT = [split_of(north_going, t % TILES) for t in range(BTILES)]
X_SPLIT = [split_of(east_going, t % TILES) for t in range(BTILES)]


def pattern():
    theta = 2.0 * np.pi * ((np.arange(PERIOD) % NDIR) + 0.5) / NDIR
    both = np.stack([np.abs(np.cos(theta)), np.abs(np.sin(theta))])
    return jnp.broadcast_to(jnp.asarray(both, jnp.float32)[:, :, None], (2, PERIOD, 128))


def sublanes(width):
    return lax.broadcasted_iota(jnp.int32, (SUB, width), 0)


def between(rows, iota):
    return (iota >= rows[0]) & (iota <= rows[-1])


def choose(split, iota, yes, no):
    if split == 1:
        return yes
    if split == -1:
        return no
    return jnp.where(between(split, iota), yes, no)


def tile_coefficients(trig_ref, block, t, iota):
    frequency = (block * (BLOCK // NDIR) + (t * SUB) // NDIR).astype(jnp.float32)
    speed = 0.6 * (0.35 + (0.65 / (NFREQ - 1)) * ((NFREQ - 1) - frequency))
    later = 0.6 * 0.65 / (NFREQ - 1)
    first = SUB - ((t * SUB + SUB) % NDIR)
    speeds = jnp.full(iota.shape, speed, jnp.float32)
    if (t * SUB) // NDIR != (t * SUB + SUB - 1) // NDIR:
        speeds = jnp.where(iota >= first, speeds - later, speeds)
    at = pl.ds((t % TILES) * SUB, SUB)
    along = speeds * trig_ref[0, at, :]
    across = speeds * trig_ref[1, at, :]
    return 1.0 - along - across, along, across


def beside(t, iota, value):
    split = X_SPLIT[t]
    west = pltpu.roll(value, 1, 1) if split != -1 else None
    east = pltpu.roll(value, value.shape[1] - 1, 1) if split != 1 else None
    return choose(split, iota, west, east)


def flow(t, iota, rows):
    return [choose(Y_SPLIT[t], iota, rows[i], rows[len(rows) - 1 - i]) for i in range(len(rows))]


def substep(t, iota, coefficients, rows, seas, before):
    staying, along, across = coefficients
    out = []
    for i, row in enumerate(rows):
        upstream = before if i == 0 else rows[i - 1]
        if upstream is None:
            continue
        out.append(seas[i] * (staying * row + along * beside(t, iota, row) + across * upstream))
    return out


def edges(t, iota, coefficients, rows, seas):
    found = [rows[-1]]
    rows, seas = rows[-SUBSTEPS:], seas[-SUBSTEPS:]
    for _ in range(SUBSTEPS - 1):
        rows = substep(t, iota, coefficients, rows, seas, None)
        seas = seas[1:]
        found.append(rows[-1])
    return found


def pack(tiles, iota):
    a, b = tiles[:TILES], tiles[TILES:]
    roll = lambda value, shift: pltpu.roll(value, shift, 0)
    north = [a[0], a[1], a[5], b[0], b[1], b[5],
             jnp.where(iota < 6, a[6], roll(b[2], 6)),
             jnp.where(iota < 6, b[6], roll(a[2], 6)),
             jnp.where(iota < 4, roll(b[4], 4), a[4])]
    south = [a[3], a[7], a[8], b[3], b[7], b[8],
             jnp.where(iota < 2, roll(a[6], 2), a[2]),
             jnp.where(iota < 2, roll(b[6], 2), b[2]),
             jnp.where(iota < 4, a[4], roll(b[4], 4))]
    return north, south


def unpack(north, south, iota):
    roll = lambda value, shift: pltpu.roll(value, shift, 0)
    a = [north[0], north[1], jnp.where(iota < 2, roll(north[7], 2), south[6]), south[0],
         jnp.where(iota < 4, south[8], north[8]), north[2],
         jnp.where(iota < 6, north[6], roll(south[6], 6)), south[1], south[2]]
    b = [north[3], north[4], jnp.where(iota < 2, roll(north[6], 2), south[7]), south[3],
         jnp.where(iota < 4, roll(south[8], 4), roll(north[8], 4)), north[5],
         jnp.where(iota < 6, north[7], roll(south[7], 6)), south[4], south[5]]
    return a + b


def spread(ref, r):
    row = ref[pl.ds(r, 1), :]
    return jnp.broadcast_to(row.astype(jnp.float32), (SUB, row.shape[1]))


def send_edges(block, found, odd, iota, cross_ref, inner_ref):
    for j in range(SUBSTEPS):
        north, south = pack([f[j] for f in found], iota)
        for i in range(HTILES):
            at = pl.ds(block * HALF + i * SUB, SUB)
            cross_ref[j, at, :] = jnp.where(odd, north[i], south[i])
            inner_ref[j, at, :] = jnp.where(odd, south[i], north[i])


def first_kernel(odd_ref, f_ref, sea_ref, trig_ref, cross_ref, inner_ref):
    rows_here = f_ref.shape[0]
    iota = sublanes(f_ref.shape[2])
    odd = odd_ref[0] == 1
    seas = [spread(sea_ref, r) for r in range(rows_here)]

    def block_step(block, carry):
        found = []
        for t in range(BTILES):
            at = pl.ds(block * BLOCK + t * SUB, SUB)
            rows = flow(t, iota, [f_ref[r, at, :] for r in range(rows_here)])
            coefficients = tile_coefficients(trig_ref, block, t, iota)
            found.append(edges(t, iota, coefficients, rows, flow(t, iota, seas)))
        send_edges(block, found, odd, iota, cross_ref, inner_ref)
        return carry

    lax.fori_loop(0, BLOCKS, block_step, 0)


def step_kernel(last, odd_ref, f_ref, sea_ref, ice_ref, wind_ref, trig_ref, matrix_ref, cross_in, inner_in, *rest):
    if last:
        out_ref, f_acc, b_acc = rest
    else:
        out_ref, cross_ref, inner_ref, f_acc, b_acc = rest
    rows_here, comps, width = f_ref.shape
    iota = sublanes(width)
    odd = odd_ref[0] == 1
    seas = [spread(sea_ref, r) for r in range(rows_here)]

    def advance(block, sums):
        halo = []
        for j in range(SUBSTEPS):
            north, south = [], []
            for i in range(HTILES):
                at = pl.ds(block * HALF + i * SUB, SUB)
                cross, inner = cross_in[j, at, :], inner_in[j, at, :]
                north.append(jnp.where(odd, inner, cross))
                south.append(jnp.where(odd, cross, inner))
            halo.append(unpack(north, south, iota))
        done = []
        for t in range(BTILES):
            at = pl.ds(block * BLOCK + t * SUB, SUB)
            rows = flow(t, iota, [f_ref[r, at, :] for r in range(rows_here)])
            flow_seas = flow(t, iota, seas)
            coefficients = tile_coefficients(trig_ref, block, t, iota)
            for j in range(SUBSTEPS):
                rows = substep(t, iota, coefficients, rows, flow_seas, halo[j][t])
            done.append(flow(t, iota, rows))
        sums = list(sums)
        for r in range(rows_here):
            whole = jnp.concatenate([d[r] for d in done], axis=0)
            at = pl.ds(block * BLOCK, BLOCK)
            f_acc[at, r * width:(r + 1) * width] = whole
            b_acc[0, at, r * width:(r + 1) * width] = whole.astype(jnp.bfloat16)
            for d in done:
                sums[r] = sums[r] + d[r] * d[r]
        return tuple(sums)

    zero = jnp.zeros((SUB, width), jnp.float32)
    sums = lax.fori_loop(0, BLOCKS, advance, (zero,) * rows_here)
    energy = jnp.concatenate([jnp.sum(s, axis=0, keepdims=True) for s in sums], axis=1)
    sea = jnp.concatenate([sea_ref[r:r + 1, :].astype(jnp.float32) for r in range(rows_here)], axis=1)
    gain = source_rate * jnp.concatenate([wind_ref[r:r + 1, :] for r in range(rows_here)], axis=1)

    chunk = 384
    for s in range(SRC_SUB):
        scale = sea / (1.0 + (damping / comps) * energy)
        energy = jnp.zeros_like(energy)
        for c in range(comps // chunk):
            at = pl.ds(c * chunk, chunk)
            growth = jnp.dot(matrix_ref[at, :], b_acc[s % 2], preferred_element_type=jnp.float32)
            value = (f_acc[at, :] + gain * growth) * scale
            f_acc[at, :] = value
            if s + 1 < SRC_SUB:
                b_acc[(s + 1) % 2, at, :] = value.astype(jnp.bfloat16)
                energy = energy + jnp.sum(value * value, axis=0, keepdims=True)

    thaw = [1.0 - 0.5 * spread(ice_ref, r) for r in range(rows_here)]

    def finish(block, carry):
        found = []
        for t in range(BTILES):
            at = pl.ds(block * BLOCK + t * SUB, SUB)
            rows = [f_acc[at, r * width:(r + 1) * width] * thaw[r] for r in range(rows_here)]
            for r in range(rows_here):
                out_ref[r, at, :] = rows[r]
            if not last:
                coefficients = tile_coefficients(trig_ref, block, t, iota)
                found.append(edges(t, iota, coefficients, flow(t, iota, rows), flow(t, iota, seas)))
        if not last:
            send_edges(block, found, odd, iota, cross_ref, inner_ref)
        return carry

    lax.fori_loop(0, BLOCKS, finish, 0)


def on_device(spectrum, sea_mask, ice_mask, wind, source_matrix):
    size = lax.axis_size("comp")
    comps, rows_here, width = spectrum.shape
    assert comps == K and rows_here >= SUBSTEPS and size % 2 == 0
    odd = (lax.axis_index("comp") % 2).astype(jnp.int32).reshape(1)
    f = jnp.transpose(spectrum, (1, 0, 2))
    trig = pattern()
    smem = pl.BlockSpec(memory_space=pltpu.SMEM)
    vmem = pl.BlockSpec(memory_space=pltpu.VMEM)
    params = pltpu.CompilerParams(vmem_limit_bytes=32 * 1024 * 1024)
    message = jax.ShapeDtypeStruct((SUBSTEPS, K // 2, width), jnp.float32)
    whole = jax.ShapeDtypeStruct(f.shape, jnp.float32)
    outer_pairs = [(i, i + 1) for i in range(1, size - 1, 2)]
    inner_pairs = [(i, i + 1) for i in range(0, size, 2)]

    def swap(value, pairs):
        return lax.ppermute(value, "comp", pairs + [(j, i) for i, j in pairs])

    cross, inner = pl.pallas_call(
        first_kernel, out_shape=(message, message), in_specs=[smem, vmem, vmem, vmem],
        out_specs=(vmem, vmem), compiler_params=params, name="edges",
    )(odd, f, sea_mask, trig)
    for step in range(STEPS):
        last = step == STEPS - 1
        cross = swap(cross, outer_pairs)
        inner = swap(inner, inner_pairs)
        result = pl.pallas_call(
            functools.partial(step_kernel, last),
            out_shape=(whole,) if last else (whole, message, message),
            in_specs=[smem] + [vmem] * 8,
            out_specs=(vmem,) if last else (vmem,) * 3,
            scratch_shapes=[pltpu.VMEM((K, rows_here * width), jnp.float32),
                            pltpu.VMEM((2, K, rows_here * width), jnp.bfloat16)],
            compiler_params=params, name="outer_step",
        )(odd, f, sea_mask, ice_mask, wind, trig, source_matrix, cross, inner)
        if last:
            f = result[0]
        else:
            f, cross, inner = result
    return jnp.transpose(f, (1, 0, 2))


def solution(mesh):
    return jax.shard_map(
        on_device,
        mesh=mesh,
        in_specs=(
            P(None, ("grp", "comp"), None),
            P(("grp", "comp"), None),
            P(("grp", "comp"), None),
            P(("grp", "comp"), None),
            P(),
        ),
        out_specs=P(None, ("grp", "comp"), None),
        check_vma=False,
    )
```

time: 167 us -> 68 us (0.41)
  waiting for transfers between devices: 66 us -> 31.2 us
  starting transfers between devices: 38.5 us -> 9.07 us
  other arithmetic: 23.3 us -> 0 us
  Pallas kernels: 0 us -> 22.7 us
  local copies, waits for them, and re-layouts: 25.3 us -> 4.69 us
  matrix products: 12.3 us -> 0 us
    ppermute x12 -> x4, waiting for transfers between devices: 66 us -> 31.2 us  [swap(): return lax.ppermute(value, 'comp', pairs + [(j, i) for i, j in pairs])]
    ppermute x12 -> x4, starting transfers between devices: 38.5 us -> 9.07 us  [swap(): return lax.ppermute(value, 'comp', pairs + [(j, i) for i, j in pairs])]
    pallas_call x0 -> x3, Pallas kernels: none -> 22.7 us  [the longest x2 21.2 us: on_device(): pl.pallas_call(functools.partial(step_kernel, last), out_shape=(whole,) i...]
    slice x18 -> x0, local copies, waits for them, and re-layouts: 13.3 us -> none  [the longest x12 11.4 us: advance(): western = jnp.roll(spectra, 1, axis=2)]
    mul x8 -> x0, other arithmetic: 12.7 us -> none  [the longest x4 8.34 us: on_device(): spectra = sea_local[None] * advance(widened, courant_x, courant_y)[:, 1:-1]]
    dot_general x6 -> x0, matrix products: 12.3 us -> none  [sources(): growth = jnp.dot(source_matrix, rounded, preferred_element_type=jnp.float32)]
    reduce_sum x2 -> x0, other arithmetic: 5.96 us -> none  [sources(): energy = jnp.mean(flattened * flattened, axis=0, keepdims=True)]
    reshape x2 -> x0, local copies, waits for them, and re-layouts: 5.6 us -> none  [sources(): return flattened.reshape(layout_shape)]
  transfers between devices with their start and end apart: 12 -> 4, of which waited for: 6 -> 2; matrix products, arithmetic and copies ran while one was open for 0% -> 0% of each run, Pallas kernels for 0% -> 0%
where the time goes in v1:
time: 68 us; the launch traced here: 67.7 us
  waiting for transfers between devices  31.2 us (46%)
  Pallas kernels  22.7 us (33%)
  starting transfers between devices  9.07 us (13%)
  local copies, waits for them, and re-layouts  4.69 us (7%)
    ppermute x4, waiting for transfers between devices, swap(): return lax.ppermute(value, 'comp', pairs + [(j, i) for i, j in pairs])  31.2 us
    pallas_call x2, Pallas kernels, on_device(): pl.pallas_call(functools.partial(step_kernel, last), out_shape=(whole,) i...  21.2 us
    ppermute x4, starting transfers between devices, swap(): return lax.ppermute(value, 'comp', pairs + [(j, i) for i, j in pairs])  9.07 us
    unnamed x12, local copies, waits for them, and re-layouts  3.91 us
    pallas_call x1, Pallas kernels, on_device(): pl.pallas_call(first_kernel, out_shape=(message, message), in_specs=[smem...  1.52 us
  transfers between devices with their start and end apart: 4, of which 2 were waited for; matrix products, arithmetic and copies ran while one was open for 0% of the time, Pallas kernels for 0%

profile of v1, /device:TPU:1, one launch (start us, length us, event | category | flops | bytes accessed | tf_op | source)
XLA Modules:
  0.0 67.7 jit_solution(14686311867406415788)
XLA Ops:
  0.0 0.0 copy-start.5
  0.0 0.0 copy-start.4
  0.0 0.8 %broadcast_in_dim.2.trig_ref = f32[2,72,128]{2,1,0:T(8,128)S(1)} broadcast(f32[2,72]{1,0:T(2,128)} %constant.19.clone), dimensions={0,1} | broadcast | bytes 74304 | tf_op jit(solution)/shard_map/broadcast_in_dim | solution.py:55
  0.8 0.0 copy-start.2
  0.8 1.5 %copy-done.2 = f32[1152,3,128]{2,0,1:T(8,128)S(1)} copy-done((f32[1152,3,128]{2,0,1:T(8,128)S(1)}, f32[1152,3,128]{2,0,1:T(8,128)}, u32[]{:S(2)}) %copy-start.2) | copy-done | bytes 1769496
  2.3 0.0 copy-start.3
  2.3 0.7 %copy-done.3 = s32[3,128]{1,0:T(4,128)S(1)} copy-done((s32[3,128]{1,0:T(4,128)S(1)}, s32[3,128]{1,0:T(4,128)}, u32[]{:S(2)}) %copy-start.3) | copy-done | bytes 1560
  3.0 1.5 %edges.1 = (f32[3,576,128]{2,1,0:T(8,128)S(1)}, f32[3,576,128]{2,1,0:T(8,128)S(1)}) custom-call(s32[1]{0:T(128)} %bitcast.odd_ref, f32[3,1152,128]{2,1,0:T(8,128)S(1)} %bitcast.3, s32[3,128]{1,0:T(4,128)S(1)} %copy-done.3, f32[2,72,128]{2,1,0:T(8,128)S(1)} %broadcast_in_dim.2.trig_ref), custom_call_target="tpu_custom_call" | custom-call | tf_op jit(solution)/shard_map/edges/pallas_call | solution.py:273
  4.5 4.5 %collective-permute-start = (f32[3,576,128]{2,1,0:T(8,128)S(1)}, f32[3,576,128]{2,1,0:T(8,128)S(1)}, u32[]{:S(2)}, u32[]{:S(2)}) collective-permute-start(f32[3,576,128]{2,1,0:T(8,128)S(1)} %get-tuple-element.10), channel_id=1, source_target_pairs={{1,2},{3,4},{5,6},{7,8},{9,10},{11,12},{13,14},{2,1},{4,3},{6,5},{... | collective-permute-start | bytes 2654216 | tf_op jit(solution)/shard_map/ppermute | solution.py:271
  9.0 0.1 collective-permute-start.1
  9.1 19.4 %collective-permute-done.cross_in = f32[3,576,128]{2,1,0:T(8,128)S(1)} collective-permute-done((f32[3,576,128]{2,1,0:T(8,128)S(1)}, f32[3,576,128]{2,1,0:T(8,128)S(1)}, u32[]{:S(2)}, u32[]{:S(2)}) %collective-permute-start) | collective-permute-done | bytes 884768 | tf_op jit(solution)/shard_map/ppermute | solution.py:271
  28.5 0.0 collective-permute-done.1.inner_in
  28.5 0.0 copy-done.5
  28.5 0.0 copy-done.4
  28.5 0.0 copy-start
  28.5 1.7 %copy-done = bf16[1152,1152]{1,0:T(8,128)(2,1)S(1)} copy-done((bf16[1152,1152]{1,0:T(8,128)(2,1)S(1)}, bf16[1152,1152]{1,0:T(8,128)(2,1)}, u32[]{:S(2)}) %copy-start) | copy-done | bytes 2654232
  30.2 0.0 copy-start.1
  30.2 10.7 %outer_step.2 = (f32[3,1152,128]{2,1,0:T(8,128)S(1)}, f32[3,576,128]{2,1,0:T(8,128)S(1)}, f32[3,576,128]{2,1,0:T(8,128)S(1)}) custom-call(s32[1]{0:T(128)} %bitcast.odd_ref, f32[3,1152,128]{2,1,0:T(8,128)S(1)} %bitcast.4, s32[3,128]{1,0:T(4,128)S(1)} %copy-done.3, s32[3,128]{1,0:T(4,128)S(1)} %copy-done.4, f32[3,128]{1,0:T(4,128)S(1)} %copy-done.5, ...), custom_call_target="tpu_custom_call" | custom-call | tf_op jit(solution)/shard_map/outer_step/pallas_call | solution.py:281
  40.9 4.4 %collective-permute-start.2 = (f32[3,576,128]{2,1,0:T(8,128)S(1)}, f32[3,576,128]{2,1,0:T(8,128)S(1)}, u32[]{:S(2)}, u32[]{:S(2)}) collective-permute-start(f32[3,576,128]{2,1,0:T(8,128)S(1)} %get-tuple-element.13), channel_id=1, source_target_pairs={{1,2},{3,4},{5,6},{7,8},{9,10},{11,12},{13,14},{2,1},{4,3},{6,5},{... | collective-permute-start | bytes 2654216 | tf_op jit(solution)/shard_map/ppermute | solution.py:271
  45.3 0.1 collective-permute-start.3
  45.4 11.8 %collective-permute-done.2.cross_in = f32[3,576,128]{2,1,0:T(8,128)S(1)} collective-permute-done((f32[3,576,128]{2,1,0:T(8,128)S(1)}, f32[3,576,128]{2,1,0:T(8,128)S(1)}, u32[]{:S(2)}, u32[]{:S(2)}) %collective-permute-start.2) | collective-permute-done | bytes 884768 | tf_op jit(solution)/shard_map/ppermute | solution.py:271
  57.2 0.0 collective-permute-done.3.inner_in
  57.2 0.0 copy-done.1
  57.2 10.5 %outer_step.3 = f32[3,1152,128]{2,1,0:T(8,128)} custom-call(s32[1]{0:T(128)} %bitcast.odd_ref, f32[3,1152,128]{2,1,0:T(8,128)S(1)} %get-tuple-element.12.f_ref, s32[3,128]{1,0:T(4,128)S(1)} %copy-done.3, s32[3,128]{1,0:T(4,128)S(1)} %copy-done.4, f32[3,128]{1,0:T(4,128)S(1)} %copy-done.5, f32[2,72,128]{2,1,0:T(8,128)S(1)} %broadcast_in_dim.2.trig_ref, ...), custom_call_target="tpu_custom_call" | custom-call | tf_op jit(solution)/shard_map/outer_step/pallas_call | solution.py:281
Async XLA Ops:
  0.0 28.5 %copy-start.5 = (f32[3,128]{1,0:T(4,128)S(1)}, f32[3,128]{1,0:T(4,128)}, u32[]{:S(2)}) copy-start(f32[3,128]{1,0:T(4,128)} %wind_ref.3) | copy-start | bytes 4612
  0.0 28.5 %copy-start.4 = (s32[3,128]{1,0:T(4,128)S(1)}, s32[3,128]{1,0:T(4,128)}, u32[]{:S(2)}) copy-start(s32[3,128]{1,0:T(4,128)} %ice_ref.3) | copy-start | bytes 4612
  0.8 1.5 %copy-start.2 = (f32[1152,3,128]{2,0,1:T(8,128)S(1)}, f32[1152,3,128]{2,0,1:T(8,128)}, u32[]{:S(2)}) copy-start(f32[1152,3,128]{2,0,1:T(8,128)} %param.6) | copy-start | bytes 5308420
  2.3 0.7 %copy-start.3 = (s32[3,128]{1,0:T(4,128)S(1)}, s32[3,128]{1,0:T(4,128)}, u32[]{:S(2)}) copy-start(s32[3,128]{1,0:T(4,128)} %sea_ref.5) | copy-start | bytes 4612
  4.5 24.0 %collective-permute-start = (f32[3,576,128]{2,1,0:T(8,128)S(1)}, f32[3,576,128]{2,1,0:T(8,128)S(1)}, u32[]{:S(2)}, u32[]{:S(2)}) collective-permute-start(f32[3,576,128]{2,1,0:T(8,128)S(1)} %get-tuple-element.10), channel_id=1, source_target_pairs={{1,2},{3,4},{5,6},{7,8},{9,10},{11,12},{13,14},{2,1},{4,3},{6,5},{... | collective-permute-start | bytes 2654216 | tf_op jit(solution)/shard_map/ppermute | solution.py:271
  9.0 19.4 %collective-permute-start.1 = (f32[3,576,128]{2,1,0:T(8,128)S(1)}, f32[3,576,128]{2,1,0:T(8,128)S(1)}, u32[]{:S(2)}, u32[]{:S(2)}) collective-permute-start(f32[3,576,128]{2,1,0:T(8,128)S(1)} %get-tuple-element.11), channel_id=1, source_target_pairs={{0,1},{2,3},{4,5},{6,7},{8,9},{10,11},{12,13},{14,15},{1,0},{3,2},... | collective-permute-start | bytes 2654216 | tf_op jit(solution)/shard_map/ppermute | solution.py:271
  28.5 1.8 %copy-start = (bf16[1152,1152]{1,0:T(8,128)(2,1)S(1)}, bf16[1152,1152]{1,0:T(8,128)(2,1)}, u32[]{:S(2)}) copy-start(bf16[1152,1152]{1,0:T(8,128)(2,1)} %matrix_ref.3) | copy-start | bytes 7962628
  30.2 27.0 %copy-start.1 = (bf16[1152,1152]{1,0:T(8,128)(2,1)S(1)}, bf16[1152,1152]{1,0:T(8,128)(2,1)}, u32[]{:S(2)}) copy-start(bf16[1152,1152]{1,0:T(8,128)(2,1)} %matrix_ref.3) | copy-start | bytes 7962628
  40.9 16.3 %collective-permute-start.2 = (f32[3,576,128]{2,1,0:T(8,128)S(1)}, f32[3,576,128]{2,1,0:T(8,128)S(1)}, u32[]{:S(2)}, u32[]{:S(2)}) collective-permute-start(f32[3,576,128]{2,1,0:T(8,128)S(1)} %get-tuple-element.13), channel_id=1, source_target_pairs={{1,2},{3,4},{5,6},{7,8},{9,10},{11,12},{13,14},{2,1},{4,3},{6,5},{... | collective-permute-start | bytes 2654216 | tf_op jit(solution)/shard_map/ppermute | solution.py:271
  45.3 11.9 %collective-permute-start.3 = (f32[3,576,128]{2,1,0:T(8,128)S(1)}, f32[3,576,128]{2,1,0:T(8,128)S(1)}, u32[]{:S(2)}, u32[]{:S(2)}) collective-permute-start(f32[3,576,128]{2,1,0:T(8,128)S(1)} %get-tuple-element.14), channel_id=1, source_target_pairs={{0,1},{2,3},{4,5},{6,7},{8,9},{10,11},{12,13},{14,15},{1,0},{3,2},... | collective-permute-start | bytes 2654216 | tf_op jit(solution)/shard_map/ppermute | solution.py:271

commit v2 on v1

v2 whole, which is shorter than its diff:
```python
import functools

import jax
import jax.numpy as jnp
import numpy as np
from jax import lax
from jax.experimental import pallas as pl
from jax.experimental.pallas import tpu as pltpu
from jax.sharding import PartitionSpec as P

NDIR = 36
NFREQ = 32
K = 1152
STEPS = 2
SUBSTEPS = 3
SRC_SUB = 3

source_rate = 0.5
damping = 0.5

SUB = 8
PERIOD = 2 * NDIR
TILES = PERIOD // SUB
BLOCK = 2 * PERIOD
BLOCKS = K // BLOCK
BTILES = 2 * TILES
HALF = BLOCK // 2
HTILES = BTILES // 2


def split_of(positive, tile):
    rows = [positive((tile * SUB + i) % NDIR) for i in range(SUB)]
    if all(rows):
        return 1
    if not any(rows):
        return -1
    return [i for i in range(SUB) if rows[i]]


def north_going(d):
    return d < NDIR // 2


def east_going(d):
    return d < NDIR // 4 or d >= 3 * NDIR // 4


Y_SPLIT = [split_of(north_going, t % TILES) for t in range(BTILES)]
X_SPLIT = [split_of(east_going, t % TILES) for t in range(BTILES)]


def pattern():
    theta = 2.0 * np.pi * ((np.arange(PERIOD) % NDIR) + 0.5) / NDIR
    both = np.stack([np.abs(np.cos(theta)), np.abs(np.sin(theta))]).astype(np.float32)
    return jnp.asarray(np.ascontiguousarray(np.broadcast_to(both[:, :, None], (2, PERIOD, 128))))


def sublanes(width):
    return lax.broadcasted_iota(jnp.int32, (SUB, width), 0)


def between(rows, iota):
    return (iota >= rows[0]) & (iota <= rows[-1])


def choose(split, iota, yes, no):
    if split == 1:
        return yes
    if split == -1:
        return no
    return jnp.where(between(split, iota), yes, no)


def tile_coefficients(trig_ref, block, t, iota):
    frequency = (block * (BLOCK // NDIR) + (t * SUB) // NDIR).astype(jnp.float32)
    speed = 0.6 * (0.35 + (0.65 / (NFREQ - 1)) * ((NFREQ - 1) - frequency))
    later = 0.6 * 0.65 / (NFREQ - 1)
    first = SUB - ((t * SUB + SUB) % NDIR)
    speeds = jnp.full(iota.shape, speed, jnp.float32)
    if (t * SUB) // NDIR != (t * SUB + SUB - 1) // NDIR:
        speeds = jnp.where(iota >= first, speeds - later, speeds)
    at = pl.ds((t % TILES) * SUB, SUB)
    along = speeds * trig_ref[0, at, :]
    across = speeds * trig_ref[1, at, :]
    return 1.0 - along - across, along, across


def beside(t, iota, value):
    split = X_SPLIT[t]
    west = pltpu.roll(value, 1, 1) if split != -1 else None
    east = pltpu.roll(value, value.shape[1] - 1, 1) if split != 1 else None
    return choose(split, iota, west, east)


def flow(t, iota, rows):
    return [choose(Y_SPLIT[t], iota, rows[i], rows[len(rows) - 1 - i]) for i in range(len(rows))]


def substep(t, iota, coefficients, rows, seas, before):
    staying, along, across = coefficients
    out = []
    for i, row in enumerate(rows):
        upstream = before if i == 0 else rows[i - 1]
        if upstream is None:
            continue
        out.append(seas[i] * (staying * row + along * beside(t, iota, row) + across * upstream))
    return out


def edges(t, iota, coefficients, rows, seas, count):
    found = [rows[-1]]
    rows, seas = rows[-count:], seas[-count:]
    for _ in range(count - 1):
        rows = substep(t, iota, coefficients, rows, seas, None)
        seas = seas[1:]
        found.append(rows[-1])
    return found


def pack(tiles, iota):
    a, b = tiles[:TILES], tiles[TILES:]
    roll = lambda value, shift: pltpu.roll(value, shift, 0)
    north = [a[0], a[1], a[5], b[0], b[1], b[5],
             jnp.where(iota < 6, a[6], roll(b[2], 6)),
             jnp.where(iota < 6, b[6], roll(a[2], 6)),
             jnp.where(iota < 4, roll(b[4], 4), a[4])]
    south = [a[3], a[7], a[8], b[3], b[7], b[8],
             jnp.where(iota < 2, roll(a[6], 2), a[2]),
             jnp.where(iota < 2, roll(b[6], 2), b[2]),
             jnp.where(iota < 4, a[4], roll(b[4], 4))]
    return north, south


def unpack(north, south, iota):
    roll = lambda value, shift: pltpu.roll(value, shift, 0)
    a = [north[0], north[1], jnp.where(iota < 2, roll(north[7], 2), south[6]), south[0],
         jnp.where(iota < 4, south[8], north[8]), north[2],
         jnp.where(iota < 6, north[6], roll(south[6], 6)), south[1], south[2]]
    b = [north[3], north[4], jnp.where(iota < 2, roll(north[6], 2), south[7]), south[3],
         jnp.where(iota < 4, roll(south[8], 4), roll(north[8], 4)), north[5],
         jnp.where(iota < 6, north[7], roll(south[7], 6)), south[4], south[5]]
    return a + b


def spread(ref, r):
    row = ref[pl.ds(r, 1), :]
    return jnp.broadcast_to(row.astype(jnp.float32), (SUB, row.shape[1]))


def tile_at(block, t):
    return pl.ds(block * BLOCK + t * SUB, SUB)


def send(block, slot, tiles, odd, iota, cross_ref, inner_ref):
    north, south = pack(tiles, iota)
    for i in range(HTILES):
        at = pl.ds(block * HALF + i * SUB, SUB)
        cross_ref[slot, at, :] = jnp.where(odd, north[i], south[i])
        inner_ref[slot, at, :] = jnp.where(odd, south[i], north[i])


def receive(block, slot, odd, iota, cross_ref, inner_ref):
    north, south = [], []
    for i in range(HTILES):
        at = pl.ds(block * HALF + i * SUB, SUB)
        cross, inner = cross_ref[slot, at, :], inner_ref[slot, at, :]
        north.append(jnp.where(odd, inner, cross))
        south.append(jnp.where(odd, cross, inner))
    return unpack(north, south, iota)


def reader(row_refs):
    if len(row_refs) == 1:
        whole, = row_refs
        return whole.shape, lambda r, at: whole[r, at, :]
    edge, middle = row_refs
    count = middle.shape[0] + 2

    def row(r, at):
        if r == 0:
            return edge[0, at, :]
        if r == count - 1:
            return edge[1, at, :]
        return middle[r - 1, at, :]

    return (count,) + tuple(middle.shape[1:]), row


def edges_kernel(slots, odd_ref, sea_ref, trig_ref, *refs):
    (count, _, width), row = reader(refs[:-2])
    cross_ref, inner_ref = refs[-2:]
    iota = sublanes(width)
    odd = odd_ref[0] == 1
    seas = [spread(sea_ref, r) for r in range(count)]

    def body(block, carry):
        found = []
        for t in range(BTILES):
            rows = flow(t, iota, [row(r, tile_at(block, t)) for r in range(count)])
            coefficients = tile_coefficients(trig_ref, block, t, iota)
            found.append(edges(t, iota, coefficients, rows, flow(t, iota, seas), slots[-1] + 1))
        for i, slot in enumerate(slots):
            send(block, i, [f[slot] for f in found], odd, iota, cross_ref, inner_ref)
        return carry

    lax.fori_loop(0, BLOCKS, body, 0)


def lanes(ref, rows):
    return jnp.concatenate([ref[r:r + 1, :].astype(jnp.float32) for r in rows], axis=1)


def source_steps(rows, sums, sea_ref, wind_ref, matrix_ref, f_acc, b_acc):
    comps = f_acc.shape[0]
    sea, gain = lanes(sea_ref, rows), source_rate * lanes(wind_ref, rows)
    energy = jnp.concatenate([jnp.sum(s, axis=0, keepdims=True) for s in sums], axis=1)
    chunk = comps // 4
    for s in range(SRC_SUB):
        scale = sea / (1.0 + (damping / comps) * energy)
        energy = jnp.zeros_like(energy)
        for c in range(comps // chunk):
            at = pl.ds(c * chunk, chunk)
            growth = jnp.dot(matrix_ref[at, :], b_acc[s % 2], preferred_element_type=jnp.float32)
            value = (f_acc[at, :] + gain * growth) * scale
            f_acc[at, :] = value
            if s + 1 < SRC_SUB:
                b_acc[(s + 1) % 2, at, :] = value.astype(jnp.bfloat16)
                energy = energy + jnp.sum(value * value, axis=0, keepdims=True)


def hold(block, column, tiles, f_acc, b_acc):
    whole = jnp.concatenate(tiles, axis=0)
    width = whole.shape[1]
    at = pl.ds(block * BLOCK, BLOCK)
    f_acc[at, column * width:(column + 1) * width] = whole
    b_acc[0, at, column * width:(column + 1) * width] = whole.astype(jnp.bfloat16)


def middle_kernel(odd_ref, sea_ref, ice_ref, wind_ref, trig_ref, matrix_ref, cross_ref, inner_ref, *refs):
    (count, _, width), row = reader(refs[:-4])
    middle_ref, edge_ref, f_acc, b_acc = refs[-4:]
    iota = sublanes(width)
    odd = odd_ref[0] == 1
    seas = [spread(sea_ref, r) for r in range(count)]
    between_rows = range(1, count - 1)

    def advance(block, sums):
        halo = [receive(block, j, odd, iota, cross_ref, inner_ref) for j in range(SUBSTEPS - 1)]
        done = []
        for t in range(BTILES):
            rows = flow(t, iota, [row(r, tile_at(block, t)) for r in range(count)])
            flow_seas = flow(t, iota, seas)
            coefficients = tile_coefficients(trig_ref, block, t, iota)
            for j in range(SUBSTEPS):
                before = halo[j][t] if j < SUBSTEPS - 1 else jnp.zeros_like(rows[0])
                rows = substep(t, iota, coefficients, rows, flow_seas, before)
            rows = flow(t, iota, rows)
            edge_ref[0, tile_at(block, t), :] = rows[0]
            edge_ref[1, tile_at(block, t), :] = rows[-1]
            done.append(rows)
        sums = list(sums)
        for i, r in enumerate(between_rows):
            hold(block, i, [d[r] for d in done], f_acc, b_acc)
            for d in done:
                sums[i] = sums[i] + d[r] * d[r]
        return tuple(sums)

    zero = jnp.zeros((SUB, width), jnp.float32)
    sums = lax.fori_loop(0, BLOCKS, advance, (zero,) * len(between_rows))
    source_steps(between_rows, sums, sea_ref, wind_ref, matrix_ref, f_acc, b_acc)
    for i, r in enumerate(between_rows):
        middle_ref[i] = f_acc[:, i * width:(i + 1) * width] * (1.0 - 0.5 * ice_ref[r:r + 1, :].astype(jnp.float32))


def edge_kernel(last, odd_ref, sea_ref, ice_ref, wind_ref, trig_ref, matrix_ref, cross_in, inner_in, part_ref, middle_ref, *refs):
    f_acc, b_acc = refs[-2:]
    out_ref = refs[0]
    count, width = middle_ref.shape[0] + 2, middle_ref.shape[2]
    iota = sublanes(width)
    odd = odd_ref[0] == 1
    seas = [spread(sea_ref, r) for r in range(count)]
    edge_rows = (0, count - 1)

    def advance(block, sums):
        halo = receive(block, 0, odd, iota, cross_in, inner_in)
        first, final = [], []
        for t in range(BTILES):
            _, _, across = tile_coefficients(trig_ref, block, t, iota)
            term = flow(t, iota, seas)[0] * (across * halo[t])
            zero = jnp.zeros_like(term)
            at = tile_at(block, t)
            first.append(part_ref[0, at, :] + choose(Y_SPLIT[t], iota, term, zero))
            final.append(part_ref[1, at, :] + choose(Y_SPLIT[t], iota, zero, term))
        sums = list(sums)
        for i, tiles in enumerate((first, final)):
            hold(block, i, tiles, f_acc, b_acc)
            for tile in tiles:
                sums[i] = sums[i] + tile * tile
        return tuple(sums)

    zero = jnp.zeros((SUB, width), jnp.float32)
    sums = lax.fori_loop(0, BLOCKS, advance, (zero, zero))
    source_steps(edge_rows, sums, sea_ref, wind_ref, matrix_ref, f_acc, b_acc)
    thaw = [1.0 - 0.5 * spread(ice_ref, r) for r in edge_rows]
    if last:
        for i, r in enumerate(edge_rows):
            out_ref[r] = f_acc[:, i * width:(i + 1) * width] * thaw[i][:1]
        for r in range(1, count - 1):
            out_ref[r] = middle_ref[r - 1]
        return
    cross_ref, inner_ref = refs[1:3]

    def finish(block, carry):
        found = []
        for t in range(BTILES):
            at = tile_at(block, t)
            ends = [f_acc[at, i * width:(i + 1) * width] * thaw[i] for i in range(2)]
            out_ref[0, at, :], out_ref[1, at, :] = ends
            rows = flow(t, iota, [ends[0]] + [middle_ref[r - 1, at, :] for r in range(1, count - 1)] + [ends[1]])
            coefficients = tile_coefficients(trig_ref, block, t, iota)
            found.append(edges(t, iota, coefficients, rows, flow(t, iota, seas), SUBSTEPS - 1))
        for slot in range(SUBSTEPS - 1):
            send(block, slot, [f[slot] for f in found], odd, iota, cross_ref, inner_ref)
        return carry

    lax.fori_loop(0, BLOCKS, finish, 0)


def on_device(spectrum, sea_mask, ice_mask, wind, source_matrix):
    size = lax.axis_size("comp")
    comps, count, width = spectrum.shape
    assert comps == K and count >= SUBSTEPS and size % 2 == 0
    odd = (lax.axis_index("comp") % 2).astype(jnp.int32).reshape(1)
    f = jnp.transpose(spectrum, (1, 0, 2))
    trig = pattern()
    outer_pairs = [(i, i + 1) for i in range(1, size - 1, 2)]
    inner_pairs = [(i, i + 1) for i in range(0, size, 2)]

    def swap(messages):
        cross, inner = messages
        return tuple(lax.ppermute(value, "comp", pairs + [(j, i) for i, j in pairs])
                     for value, pairs in ((cross, outer_pairs), (inner, inner_pairs)))

    def call(kernel, name, args, outs, scratch_rows=0):
        scratch = []
        if scratch_rows:
            scratch = [pltpu.VMEM((K, scratch_rows * width), jnp.float32),
                       pltpu.VMEM((2, K, scratch_rows * width), jnp.bfloat16)]
        vmem = pl.BlockSpec(memory_space=pltpu.VMEM)
        return pl.pallas_call(
            kernel, out_shape=[jax.ShapeDtypeStruct(s, jnp.float32) for s in outs],
            in_specs=[pl.BlockSpec(memory_space=pltpu.SMEM)] + [vmem] * len(args),
            out_specs=[vmem] * len(outs), scratch_shapes=scratch, name=name,
            compiler_params=pltpu.CompilerParams(vmem_limit_bytes=24 * 1024 * 1024),
        )(odd, *args)

    def message(slots):
        return [(slots, K // 2, width)] * 2

    early, late = tuple(range(SUBSTEPS - 1)), (SUBSTEPS - 1,)
    rows = (f,)
    masks = (sea_mask, ice_mask, wind, trig, source_matrix)
    sent = call(functools.partial(edges_kernel, early), "early_edges", (sea_mask, trig) + rows, message(SUBSTEPS - 1))
    for step in range(STEPS):
        came = swap(sent)
        sent = call(functools.partial(edges_kernel, late), "late_edges", (sea_mask, trig) + rows, message(1))
        came_late = swap(sent)
        middle, part = call(middle_kernel, "middle_rows", masks + came + rows,
                            [(count - 2, K, width), (2, K, width)], count - 2)
        last = step == STEPS - 1
        outs = [(count, K, width)] if last else [(2, K, width)] + message(SUBSTEPS - 1)
        result = call(functools.partial(edge_kernel, last), "edge_rows", masks + came_late + (part, middle), outs, 2)
        if last:
            return jnp.transpose(result[0], (1, 0, 2))
        rows, sent = (result[0], middle), result[1:]


def solution(mesh):
    return jax.shard_map(
        on_device,
        mesh=mesh,
        in_specs=(
            P(None, ("grp", "comp"), None),
            P(("grp", "comp"), None),
            P(("grp", "comp"), None),
            P(("grp", "comp"), None),
            P(),
        ),
        out_specs=P(None, ("grp", "comp"), None),
        check_vma=False,
    )
```

time: 68 us -> 61.6 us (0.906)
  waiting for transfers between devices: 31.2 us -> 17.5 us
  starting transfers between devices: 9.07 us -> 14.7 us
  Pallas kernels: 22.7 us -> 26 us
  local copies, waits for them, and re-layouts: 4.69 us -> 3.05 us
    ppermute x4 -> x8, waiting for transfers between devices: 31.2 us -> 17.5 us  [swap(): lax.ppermute(value, 'comp', pairs + [(j, i) for i, j in pairs])]
    ppermute x4 -> x8, starting transfers between devices: 9.07 us -> 14.7 us  [swap(): lax.ppermute(value, 'comp', pairs + [(j, i) for i, j in pairs])]
    pallas_call x3 -> x7, Pallas kernels: 22.7 us -> 26 us  [call(): pl.pallas_call(kernel, out_shape=[jax.ShapeDtypeStruct(s, jnp.float32) fo...]
    unnamed x12, local copies, waits for them, and re-layouts: 3.91 us -> 3.05 us
    broadcast_in_dim x1 -> x0, local copies, waits for them, and re-layouts: 0.78 us -> none  [pattern(): jnp.broadcast_to(jnp.asarray(both, jnp.float32)[:, :, None], (2, PERIOD,...]
  transfers between devices with their start and end apart: 4 -> 8, of which waited for: 2 -> 2; matrix products, arithmetic and copies ran while one was open for 0% -> 0% of each run, Pallas kernels for 0% -> 28%
where the time goes in v2:
time: 61.6 us; the launch traced here: 61.4 us
  Pallas kernels  26 us (42%)
  waiting for transfers between devices  17.5 us (28%)
  starting transfers between devices  14.7 us (24%)
  local copies, waits for them, and re-layouts  3.05 us (5%)
    pallas_call x7, Pallas kernels, call(): pl.pallas_call(kernel, out_shape=[jax.ShapeDtypeStruct(s, jnp.float32) fo...  26 us
    ppermute x8, waiting for transfers between devices, swap(): lax.ppermute(value, 'comp', pairs + [(j, i) for i, j in pairs])  17.5 us
    ppermute x8, starting transfers between devices, swap(): lax.ppermute(value, 'comp', pairs + [(j, i) for i, j in pairs])  14.7 us
    unnamed x12, local copies, waits for them, and re-layouts  3.05 us
  transfers between devices with their start and end apart: 8, of which 2 were waited for; matrix products, arithmetic and copies ran while one was open for 0% of the time, Pallas kernels for 28%

profile of v2, /device:TPU:1, one launch (start us, length us, event | category | flops | bytes accessed | tf_op | source)
XLA Modules:
  0.0 61.4 jit_solution(10105202525764000029)
XLA Ops:
  0.0 0.0 copy-start.1
  0.0 1.5 %copy-done.1 = f32[1152,3,128]{2,0,1:T(8,128)S(1)} copy-done((f32[1152,3,128]{2,0,1:T(8,128)S(1)}, f32[1152,3,128]{2,0,1:T(8,128)}, u32[]{:S(2)}) %copy-start.1) | copy-done | bytes 1769496
  1.5 0.0 copy-start.2
  1.5 0.9 %copy-done.2 = f32[2,72,128]{2,1,0:T(8,128)S(1)} copy-done((f32[2,72,128]{2,1,0:T(8,128)S(1)}, f32[2,72,128]{2,1,0:T(8,128)}, u32[]{:S(2)}) %copy-start.2) | copy-done | bytes 73752
  2.4 0.0 copy-start.3
  2.4 0.7 %copy-done.3 = s32[3,128]{1,0:T(4,128)S(1)} copy-done((s32[3,128]{1,0:T(4,128)S(1)}, s32[3,128]{1,0:T(4,128)}, u32[]{:S(2)}) %copy-start.3) | copy-done | bytes 1560
  3.0 0.0 copy-start
  3.0 0.0 copy-start.4
  3.0 0.0 copy-start.5
  3.1 0.8 %early_edges.1 = (f32[2,576,128]{2,1,0:T(8,128)S(1)}, f32[2,576,128]{2,1,0:T(8,128)S(1)}) custom-call(s32[1]{0:T(128)} %bitcast.odd_ref, s32[3,128]{1,0:T(4,128)S(1)} %copy-done.3, f32[2,72,128]{2,1,0:T(8,128)S(1)} %copy-done.2, f32[3,1152,128]{2,1,0:T(8,128)S(1)} %bitcast.3), custom_call_target="tpu_custom_call" | custom-call | tf_op jit(solution)/shard_map/early_edges/pallas_call | solution.py:350
  3.9 4.5 %collective-permute-start.2 = (f32[2,576,128]{2,1,0:T(8,128)S(1)}, f32[2,576,128]{2,1,0:T(8,128)S(1)}, u32[]{:S(2)}, u32[]{:S(2)}) collective-permute-start(f32[2,576,128]{2,1,0:T(8,128)S(1)} %get-tuple-element.20), channel_id=1, source_target_pairs={{1,2},{3,4},{5,6},{7,8},{9,10},{11,12},{13,14},{2,1},{4,3},{6,5},{... | collective-permute-start | bytes 1769480 | tf_op jit(solution)/shard_map/ppermute | solution.py:341
  8.4 0.1 collective-permute-start.3
  8.5 1.5 %late_edges.2 = (f32[1,576,128]{2,1,0:T(8,128)S(1)}, f32[1,576,128]{2,1,0:T(8,128)S(1)}) custom-call(s32[1]{0:T(128)} %bitcast.odd_ref, s32[3,128]{1,0:T(4,128)S(1)} %copy-done.3, f32[2,72,128]{2,1,0:T(8,128)S(1)} %copy-done.2, f32[3,1152,128]{2,1,0:T(8,128)S(1)} %bitcast.4), custom_call_target="tpu_custom_call" | custom-call | tf_op jit(solution)/shard_map/late_edges/pallas_call | solution.py:350
  10.0 3.5 %collective-permute-start = (f32[1,576,128]{2,1,0:T(8,128)S(1)}, f32[1,576,128]{2,1,0:T(8,128)S(1)}, u32[]{:S(2)}, u32[]{:S(2)}) collective-permute-start(f32[1,576,128]{2,1,0:T(8,128)S(1)} %get-tuple-element.18), channel_id=1, source_target_pairs={{1,2},{3,4},{5,6},{7,8},{9,10},{11,12},{13,14},{2,1},{4,3},{6,5},{... | collective-permute-start | bytes 884744 | tf_op jit(solution)/shard_map/ppermute | solution.py:341
  13.5 0.1 collective-permute-start.1
  13.6 11.1 %collective-permute-done.2.cross_ref = f32[2,576,128]{2,1,0:T(8,128)S(1)} collective-permute-done((f32[2,576,128]{2,1,0:T(8,128)S(1)}, f32[2,576,128]{2,1,0:T(8,128)S(1)}, u32[]{:S(2)}, u32[]{:S(2)}) %collective-permute-start.2) | collective-permute-done | bytes 589856 | tf_op jit(solution)/shard_map/ppermute | solution.py:341
  24.7 0.0 collective-permute-done.3.inner_ref
  24.7 0.0 copy-done
  24.7 0.0 copy-done.4
  24.7 0.0 copy-done.5
  24.7 7.0 %middle_rows.2 = (f32[1,1152,128]{2,1,0:T(8,128)S(1)}, f32[2,1152,128]{2,1,0:T(8,128)S(1)}) custom-call(s32[1]{0:T(128)} %bitcast.odd_ref, s32[3,128]{1,0:T(4,128)S(1)} %copy-done.3, s32[3,128]{1,0:T(4,128)S(1)} %copy-done.4, f32[3,128]{1,0:T(4,128)S(1)} %copy-done.5, f32[2,72,128]{2,1,0:T(8,128)S(1)} %copy-done.2, bf16[1152,1152]{1,0:T(8,128)(2,1)S(1)} %copy-done, ...), custom_call_target="tpu_custom_call" | custom-call | tf_op jit(solution)/shard_map/middle_rows/pallas_call | solution.py:350
  31.7 0.0 collective-permute-done.cross_in
  31.8 0.0 collective-permute-done.1.inner_in
  31.8 3.8 %edge_rows.2 = (f32[2,1152,128]{2,1,0:T(8,128)S(1)}, f32[2,576,128]{2,1,0:T(8,128)S(1)}, f32[2,576,128]{2,1,0:T(8,128)S(1)}) custom-call(s32[1]{0:T(128)} %bitcast.odd_ref, s32[3,128]{1,0:T(4,128)S(1)} %copy-done.3, s32[3,128]{1,0:T(4,128)S(1)} %copy-done.4, f32[3,128]{1,0:T(4,128)S(1)} %copy-done.5, f32[2,72,128]{2,1,0:T(8,128)S(1)} %copy-done.2, ...), custom_call_target="tpu_custom_call" | custom-call | tf_op jit(solution)/shard_map/edge_rows/pallas_call | solution.py:350
  35.6 4.4 %collective-permute-start.6 = (f32[2,576,128]{2,1,0:T(8,128)S(1)}, f32[2,576,128]{2,1,0:T(8,128)S(1)}, u32[]{:S(2)}, u32[]{:S(2)}) collective-permute-start(f32[2,576,128]{2,1,0:T(8,128)S(1)} %get-tuple-element.27), channel_id=1, source_target_pairs={{1,2},{3,4},{5,6},{7,8},{9,10},{11,12},{13,14},{2,1},{4,3},{6,5},{... | collective-permute-start | bytes 1769480 | tf_op jit(solution)/shard_map/ppermute | solution.py:341
  40.0 0.1 collective-permute-start.7
  40.1 1.5 %late_edges.3 = (f32[1,576,128]{2,1,0:T(8,128)S(1)}, f32[1,576,128]{2,1,0:T(8,128)S(1)}) custom-call(s32[1]{0:T(128)} %bitcast.odd_ref, s32[3,128]{1,0:T(4,128)S(1)} %copy-done.3, f32[2,72,128]{2,1,0:T(8,128)S(1)} %copy-done.2, f32[2,1152,128]{2,1,0:T(8,128)S(1)} %get-tuple-element.24.refs_0_, f32[1,1152,128]{2,1,0:T(8,128)S(1)} %get-tuple-element.23.middle_ref.refs_1_), custom_call_target="tpu_custom_call" | custom-call | tf_op jit(solution)/shard_map/late_edges/pallas_call | solution.py:350
  41.6 1.9 %collective-permute-start.4 = (f32[1,576,128]{2,1,0:T(8,128)S(1)}, f32[1,576,128]{2,1,0:T(8,128)S(1)}, u32[]{:S(2)}, u32[]{:S(2)}) collective-permute-start(f32[1,576,128]{2,1,0:T(8,128)S(1)} %get-tuple-element.25), channel_id=1, source_target_pairs={{1,2},{3,4},{5,6},{7,8},{9,10},{11,12},{13,14},{2,1},{4,3},{6,5},{... | collective-permute-start | bytes 884744 | tf_op jit(solution)/shard_map/ppermute | solution.py:341
  43.5 0.1 collective-permute-start.5
  43.6 6.4 %collective-permute-done.6.cross_ref = f32[2,576,128]{2,1,0:T(8,128)S(1)} collective-permute-done((f32[2,576,128]{2,1,0:T(8,128)S(1)}, f32[2,576,128]{2,1,0:T(8,128)S(1)}, u32[]{:S(2)}, u32[]{:S(2)}) %collective-permute-start.6) | collective-permute-done | bytes 589856 | tf_op jit(solution)/shard_map/ppermute | solution.py:341
  50.0 0.0 collective-permute-done.7.inner_ref
  50.0 7.0 %middle_rows.3 = (f32[1,1152,128]{2,1,0:T(8,128)S(1)}, f32[2,1152,128]{2,1,0:T(8,128)S(1)}) custom-call(s32[1]{0:T(128)} %bitcast.odd_ref, s32[3,128]{1,0:T(4,128)S(1)} %copy-done.3, s32[3,128]{1,0:T(4,128)S(1)} %copy-done.4, f32[3,128]{1,0:T(4,128)S(1)} %copy-done.5, f32[2,72,128]{2,1,0:T(8,128)S(1)} %copy-done.2, bf16[1152,1152]{1,0:T(8,128)(2,1)S(1)} %copy-done, ...), custom_call_target="tpu_custom_call" | custom-call | tf_op jit(solution)/shard_map/middle_rows/pallas_call | solution.py:350
  57.0 0.0 collective-permute-done.4.cross_in
  57.0 0.0 collective-permute-done.5.inner_in
  57.0 4.3 %edge_rows.3 = f32[3,1152,128]{2,1,0:T(8,128)} custom-call(s32[1]{0:T(128)} %bitcast.odd_ref, s32[3,128]{1,0:T(4,128)S(1)} %copy-done.3, s32[3,128]{1,0:T(4,128)S(1)} %copy-done.4, f32[3,128]{1,0:T(4,128)S(1)} %copy-done.5, f32[2,72,128]{2,1,0:T(8,128)S(1)} %copy-done.2, bf16[1152,1152]{1,0:T(8,128)(2,1)S(1)} %copy-done, ...), custom_call_target="tpu_custom_call" | custom-call | tf_op jit(solution)/shard_map/edge_rows/pallas_call | solution.py:350
Async XLA Ops:
  0.0 1.5 %copy-start.1 = (f32[1152,3,128]{2,0,1:T(8,128)S(1)}, f32[1152,3,128]{2,0,1:T(8,128)}, u32[]{:S(2)}) copy-start(f32[1152,3,128]{2,0,1:T(8,128)} %param.6) | copy-start | bytes 5308420
  1.5 0.9 %copy-start.2 = (f32[2,72,128]{2,1,0:T(8,128)S(1)}, f32[2,72,128]{2,1,0:T(8,128)}, u32[]{:S(2)}) copy-start(f32[2,72,128]{2,1,0:T(8,128)} %constant.19.clone.trig_ref) | copy-start | bytes 221188
  2.4 0.7 %copy-start.3 = (s32[3,128]{1,0:T(4,128)S(1)}, s32[3,128]{1,0:T(4,128)}, u32[]{:S(2)}) copy-start(s32[3,128]{1,0:T(4,128)} %sea_ref.13) | copy-start | bytes 4612
  3.0 21.7 %copy-start = (bf16[1152,1152]{1,0:T(8,128)(2,1)S(1)}, bf16[1152,1152]{1,0:T(8,128)(2,1)}, u32[]{:S(2)}) copy-start(bf16[1152,1152]{1,0:T(8,128)(2,1)} %matrix_ref.7) | copy-start | bytes 7962628
  3.0 21.7 %copy-start.4 = (s32[3,128]{1,0:T(4,128)S(1)}, s32[3,128]{1,0:T(4,128)}, u32[]{:S(2)}) copy-start(s32[3,128]{1,0:T(4,128)} %ice_ref.7) | copy-start | bytes 4612
  3.0 21.7 %copy-start.5 = (f32[3,128]{1,0:T(4,128)S(1)}, f32[3,128]{1,0:T(4,128)}, u32[]{:S(2)}) copy-start(f32[3,128]{1,0:T(4,128)} %wind_ref.7) | copy-start | bytes 4612
  3.9 20.8 %collective-permute-start.2 = (f32[2,576,128]{2,1,0:T(8,128)S(1)}, f32[2,576,128]{2,1,0:T(8,128)S(1)}, u32[]{:S(2)}, u32[]{:S(2)}) collective-permute-start(f32[2,576,128]{2,1,0:T(8,128)S(1)} %get-tuple-element.20), channel_id=1, source_target_pairs={{1,2},{3,4},{5,6},{7,8},{9,10},{11,12},{13,14},{2,1},{4,3},{6,5},{... | collective-permute-start | bytes 1769480 | tf_op jit(solution)/shard_map/ppermute | solution.py:341
  8.4 16.3 %collective-permute-start.3 = (f32[2,576,128]{2,1,0:T(8,128)S(1)}, f32[2,576,128]{2,1,0:T(8,128)S(1)}, u32[]{:S(2)}, u32[]{:S(2)}) collective-permute-start(f32[2,576,128]{2,1,0:T(8,128)S(1)} %get-tuple-element.21), channel_id=1, source_target_pairs={{0,1},{2,3},{4,5},{6,7},{8,9},{10,11},{12,13},{14,15},{1,0},{3,2},... | collective-permute-start | bytes 1769480 | tf_op jit(solution)/shard_map/ppermute | solution.py:341
  10.0 21.7 %collective-permute-start = (f32[1,576,128]{2,1,0:T(8,128)S(1)}, f32[1,576,128]{2,1,0:T(8,128)S(1)}, u32[]{:S(2)}, u32[]{:S(2)}) collective-permute-start(f32[1,576,128]{2,1,0:T(8,128)S(1)} %get-tuple-element.18), channel_id=1, source_target_pairs={{1,2},{3,4},{5,6},{7,8},{9,10},{11,12},{13,14},{2,1},{4,3},{6,5},{... | collective-permute-start | bytes 884744 | tf_op jit(solution)/shard_map/ppermute | solution.py:341
  13.5 18.2 %collective-permute-start.1 = (f32[1,576,128]{2,1,0:T(8,128)S(1)}, f32[1,576,128]{2,1,0:T(8,128)S(1)}, u32[]{:S(2)}, u32[]{:S(2)}) collective-permute-start(f32[1,576,128]{2,1,0:T(8,128)S(1)} %get-tuple-element.19), channel_id=1, source_target_pairs={{0,1},{2,3},{4,5},{6,7},{8,9},{10,11},{12,13},{14,15},{1,0},{3,2},... | collective-permute-start | bytes 884744 | tf_op jit(solution)/shard_map/ppermute | solution.py:341
  35.6 14.4 %collective-permute-start.6 = (f32[2,576,128]{2,1,0:T(8,128)S(1)}, f32[2,576,128]{2,1,0:T(8,128)S(1)}, u32[]{:S(2)}, u32[]{:S(2)}) collective-permute-start(f32[2,576,128]{2,1,0:T(8,128)S(1)} %get-tuple-element.27), channel_id=1, source_target_pairs={{1,2},{3,4},{5,6},{7,8},{9,10},{11,12},{13,14},{2,1},{4,3},{6,5},{... | collective-permute-start | bytes 1769480 | tf_op jit(solution)/shard_map/ppermute | solution.py:341
  40.0 10.0 %collective-permute-start.7 = (f32[2,576,128]{2,1,0:T(8,128)S(1)}, f32[2,576,128]{2,1,0:T(8,128)S(1)}, u32[]{:S(2)}, u32[]{:S(2)}) collective-permute-start(f32[2,576,128]{2,1,0:T(8,128)S(1)} %get-tuple-element.28), channel_id=1, source_target_pairs={{0,1},{2,3},{4,5},{6,7},{8,9},{10,11},{12,13},{14,15},{1,0},{3,2},... | collective-permute-start | bytes 1769480 | tf_op jit(solution)/shard_map/ppermute | solution.py:341
  41.6 15.4 %collective-permute-start.4 = (f32[1,576,128]{2,1,0:T(8,128)S(1)}, f32[1,576,128]{2,1,0:T(8,128)S(1)}, u32[]{:S(2)}, u32[]{:S(2)}) collective-permute-start(f32[1,576,128]{2,1,0:T(8,128)S(1)} %get-tuple-element.25), channel_id=1, source_target_pairs={{1,2},{3,4},{5,6},{7,8},{9,10},{11,12},{13,14},{2,1},{4,3},{6,5},{... | collective-permute-start | bytes 884744 | tf_op jit(solution)/shard_map/ppermute | solution.py:341
  43.5 13.5 %collective-permute-start.5 = (f32[1,576,128]{2,1,0:T(8,128)S(1)}, f32[1,576,128]{2,1,0:T(8,128)S(1)}, u32[]{:S(2)}, u32[]{:S(2)}) collective-permute-start(f32[1,576,128]{2,1,0:T(8,128)S(1)} %get-tuple-element.26), channel_id=1, source_target_pairs={{0,1},{2,3},{4,5},{6,7},{8,9},{10,11},{12,13},{14,15},{1,0},{3,2},... | collective-permute-start | bytes 884744 | tf_op jit(solution)/shard_map/ppermute | solution.py:341

commit v3 on v2

--- a/solution.py
+++ b/solution.py
@@ -26,6 +26,7 @@
 BTILES = 2 * TILES
 HALF = BLOCK // 2
 HTILES = BTILES // 2
+CHUNKS = 4
 
 
 def split_of(positive, tile):
@@ -186,6 +187,42 @@
     return (count,) + tuple(middle.shape[1:]), row
 
 
+def edges_body(slots, block, row, count, seas, trig_ref, odd, iota, cross_ref, inner_ref):
+    found = []
+    for t in range(BTILES):
+        rows = flow(t, iota, [row(r, tile_at(block, t)) for r in range(count)])
+        coefficients = tile_coefficients(trig_ref, block, t, iota)
+        found.append(edges(t, iota, coefficients, rows, flow(t, iota, seas), slots[-1] + 1))
+    for i, slot in enumerate(slots):
+        send(block, i, [f[slot] for f in found], odd, iota, cross_ref, inner_ref)
+
+
+def first_kernel(slots, odd_ref, f_hbm, sea_hbm, trig_hbm, f_ref, sea_ref, trig_ref, cross_ref, inner_ref, sem, block_sem):
+    count, _, width = f_ref.shape
+
+    def block_copy(block):
+        at = pl.ds(pl.multiple_of(block * BLOCK, BLOCK), BLOCK)
+        return pltpu.make_async_copy(f_hbm.at[:, at, :], f_ref.at[:, at, :], block_sem.at[block])
+
+    small = [pltpu.make_async_copy(sea_hbm, sea_ref, sem.at[0]), pltpu.make_async_copy(trig_hbm, trig_ref, sem.at[1])]
+    for copy in small:
+        copy.start()
+    for block in range(BLOCKS):
+        block_copy(block).start()
+    for copy in small:
+        copy.wait()
+    iota = sublanes(width)
+    odd = odd_ref[0] == 1
+    seas = [spread(sea_ref, r) for r in range(count)]
+
+    def body(block, carry):
+        block_copy(block).wait()
+        edges_body(slots, block, lambda r, at: f_ref[r, at, :], count, seas, trig_ref, odd, iota, cross_ref, inner_ref)
+        return carry
+
+    lax.fori_loop(0, BLOCKS, body, 0)
+
+
 def edges_kernel(slots, odd_ref, sea_ref, trig_ref, *refs):
     (count, _, width), row = reader(refs[:-2])
     cross_ref, inner_ref = refs[-2:]
@@ -194,30 +231,63 @@
     seas = [spread(sea_ref, r) for r in range(count)]
 
     def body(block, carry):
-        found = []
+        edges_body(slots, block, row, count, seas, trig_ref, odd, iota, cross_ref, inner_ref)
+        return carry
+
+    lax.fori_loop(0, BLOCKS, body, 0)
+
+
+def local_kernel(sea_ref, trig_ref, *refs):
+    (count, _, width), row = reader(refs[:-1])
+    local_ref = refs[-1]
+    iota = sublanes(width)
+    seas = [spread(sea_ref, r) for r in range(count)]
+
+    def body(block, carry):
         for t in range(BTILES):
-            rows = flow(t, iota, [row(r, tile_at(block, t)) for r in range(count)])
+            at = tile_at(block, t)
+            rows = flow(t, iota, [row(r, at) for r in range(count)])
             coefficients = tile_coefficients(trig_ref, block, t, iota)
-            found.append(edges(t, iota, coefficients, rows, flow(t, iota, seas), slots[-1] + 1))
-        for i, slot in enumerate(slots):
-            send(block, i, [f[slot] for f in found], odd, iota, cross_ref, inner_ref)
+            for _ in range(SUBSTEPS):
+                rows = substep(t, iota, coefficients, rows, flow(t, iota, seas), jnp.zeros_like(rows[0]))
+            for r, value in enumerate(flow(t, iota, rows)):
+                local_ref[r, at, :] = value
         return carry
 
     lax.fori_loop(0, BLOCKS, body, 0)
+
+
+def upstream_part(t, iota, coefficients, seas, halo):
+    staying, along, across = coefficients
+    rows = []
+    for j in range(SUBSTEPS):
+        new = []
+        for i in range(j + 1):
+            value = None
+            if i < len(rows):
+                value = staying * rows[i] + along * beside(t, iota, rows[i])
+            upstream = rows[i - 1] if i else (halo[j] if j < len(halo) else None)
+            if upstream is not None:
+                value = across * upstream if value is None else value + across * upstream
+            new.append(seas[i] * value)
+        rows = new
+    return rows
 
 
 def lanes(ref, rows):
     return jnp.concatenate([ref[r:r + 1, :].astype(jnp.float32) for r in rows], axis=1)
 
 
-def source_steps(rows, sums, sea_ref, wind_ref, matrix_ref, f_acc, b_acc):
+def source_steps(rows, sums, sea_ref, ice_ref, wind_ref, matrix_ref, f_acc, b_acc, ready=None):
     comps = f_acc.shape[0]
     sea, gain = lanes(sea_ref, rows), source_rate * lanes(wind_ref, rows)
     energy = jnp.concatenate([jnp.sum(s, axis=0, keepdims=True) for s in sums], axis=1)
-    chunk = comps // 4
+    chunk = comps // CHUNKS
     for s in range(SRC_SUB):
         scale = sea / (1.0 + (damping / comps) * energy)
         energy = jnp.zeros_like(energy)
+        if s + 1 == SRC_SUB:
+            scale = scale * (1.0 - 0.5 * lanes(ice_ref, rows))
         for c in range(comps // chunk):
             at = pl.ds(c * chunk, chunk)
             growth = jnp.dot(matrix_ref[at, :], b_acc[s % 2], preferred_element_type=jnp.float32)
@@ -226,6 +296,8 @@
             if s + 1 < SRC_SUB:
                 b_acc[(s + 1) % 2, at, :] = value.astype(jnp.bfloat16)
                 energy = energy + jnp.sum(value * value, axis=0, keepdims=True)
+            elif ready is not None:
+                ready(c, at)
 
 
 def hold(block, column, tiles, f_acc, b_acc):
@@ -236,9 +308,9 @@
     b_acc[0, at, column * width:(column + 1) * width] = whole.astype(jnp.bfloat16)
 
 
-def middle_kernel(odd_ref, sea_ref, ice_ref, wind_ref, trig_ref, matrix_ref, cross_ref, inner_ref, *refs):
-    (count, _, width), row = reader(refs[:-4])
-    middle_ref, edge_ref, f_acc, b_acc = refs[-4:]
+def middle_kernel(odd_ref, sea_ref, ice_ref, wind_ref, trig_ref, matrix_ref, cross_ref, inner_ref, local_ref,
+                  middle_ref, edge_ref, f_acc, b_acc):
+    count, _, width = local_ref.shape
     iota = sublanes(width)
     odd = odd_ref[0] == 1
     seas = [spread(sea_ref, r) for r in range(count)]
@@ -248,15 +320,13 @@
         halo = [receive(block, j, odd, iota, cross_ref, inner_ref) for j in range(SUBSTEPS - 1)]
         done = []
         for t in range(BTILES):
-            rows = flow(t, iota, [row(r, tile_at(block, t)) for r in range(count)])
-            flow_seas = flow(t, iota, seas)
+            at = tile_at(block, t)
             coefficients = tile_coefficients(trig_ref, block, t, iota)
-            for j in range(SUBSTEPS):
-                before = halo[j][t] if j < SUBSTEPS - 1 else jnp.zeros_like(rows[0])
-                rows = substep(t, iota, coefficients, rows, flow_seas, before)
-            rows = flow(t, iota, rows)
-            edge_ref[0, tile_at(block, t), :] = rows[0]
-            edge_ref[1, tile_at(block, t), :] = rows[-1]
+            rows = upstream_part(t, iota, coefficients, flow(t, iota, seas), [h[t] for h in halo])
+            rows = flow(t, iota, rows + [jnp.zeros_like(rows[0])] * (count - len(rows)))
+            rows = [local_ref[r, at, :] + value for r, value in enumerate(rows)]
+            edge_ref[0, at, :] = rows[0]
+            edge_ref[1, at, :] = rows[-1]
             done.append(rows)
         sums = list(sums)
         for i, r in enumerate(between_rows):
@@ -267,14 +337,16 @@
 
     zero = jnp.zeros((SUB, width), jnp.float32)
     sums = lax.fori_loop(0, BLOCKS, advance, (zero,) * len(between_rows))
-    source_steps(between_rows, sums, sea_ref, wind_ref, matrix_ref, f_acc, b_acc)
-    for i, r in enumerate(between_rows):
-        middle_ref[i] = f_acc[:, i * width:(i + 1) * width] * (1.0 - 0.5 * ice_ref[r:r + 1, :].astype(jnp.float32))
+    source_steps(between_rows, sums, sea_ref, ice_ref, wind_ref, matrix_ref, f_acc, b_acc)
+    for i in range(count - 2):
+        middle_ref[i] = f_acc[:, i * width:(i + 1) * width]
 
 
 def edge_kernel(last, odd_ref, sea_ref, ice_ref, wind_ref, trig_ref, matrix_ref, cross_in, inner_in, part_ref, middle_ref, *refs):
-    f_acc, b_acc = refs[-2:]
-    out_ref = refs[0]
+    if last:
+        out_ref, f_acc, b_acc, sem = refs
+    else:
+        out_ref, cross_ref, inner_ref, f_acc, b_acc = refs
     count, width = middle_ref.shape[0] + 2, middle_ref.shape[2]
     iota = sublanes(width)
     odd = odd_ref[0] == 1
@@ -300,21 +372,28 @@
 
     zero = jnp.zeros((SUB, width), jnp.float32)
     sums = lax.fori_loop(0, BLOCKS, advance, (zero, zero))
-    source_steps(edge_rows, sums, sea_ref, wind_ref, matrix_ref, f_acc, b_acc)
-    thaw = [1.0 - 0.5 * spread(ice_ref, r) for r in edge_rows]
     if last:
-        for i, r in enumerate(edge_rows):
-            out_ref[r] = f_acc[:, i * width:(i + 1) * width] * thaw[i][:1]
-        for r in range(1, count - 1):
-            out_ref[r] = middle_ref[r - 1]
+        copies = [pltpu.make_async_copy(middle_ref, out_ref.at[pl.ds(1, count - 2)], sem.at[2 * CHUNKS])]
+        copies[0].start()
+
+        def ready(c, at):
+            for i, r in enumerate(edge_rows):
+                columns = pl.ds(i * width, width)
+                copy = pltpu.make_async_copy(f_acc.at[at, columns], out_ref.at[r, at, :], sem.at[2 * c + i])
+                copy.start()
+                copies.append(copy)
+
+        source_steps(edge_rows, sums, sea_ref, ice_ref, wind_ref, matrix_ref, f_acc, b_acc, ready)
+        for copy in copies:
+            copy.wait()
         return
-    cross_ref, inner_ref = refs[1:3]
+    source_steps(edge_rows, sums, sea_ref, ice_ref, wind_ref, matrix_ref, f_acc, b_acc)
 
     def finish(block, carry):
         found = []
         for t in range(BTILES):
             at = tile_at(block, t)
-            ends = [f_acc[at, i * width:(i + 1) * width] * thaw[i] for i in range(2)]
+            ends = [f_acc[at, i * width:(i + 1) * width] for i in range(2)]
             out_ref[0, at, :], out_ref[1, at, :] = ends
             rows = flow(t, iota, [ends[0]] + [middle_ref[r - 1, at, :] for r in range(1, count - 1)] + [ends[1]])
             coefficients = tile_coefficients(trig_ref, block, t, iota)
@@ -341,35 +420,43 @@
         return tuple(lax.ppermute(value, "comp", pairs + [(j, i) for i, j in pairs])
                      for value, pairs in ((cross, outer_pairs), (inner, inner_pairs)))
 
-    def call(kernel, name, args, outs, scratch_rows=0):
-        scratch = []
+    vmem = pl.BlockSpec(memory_space=pltpu.VMEM)
+    hbm = pl.BlockSpec(memory_space=pltpu.HBM)
+    dma = pltpu.SemaphoreType.DMA
+
+    def call(kernel, name, args, outs, scratch_rows=0, scratch=(), in_space=vmem, out_space=vmem, scalar=True, limit=24):
+        scratch = list(scratch)
         if scratch_rows:
             scratch = [pltpu.VMEM((K, scratch_rows * width), jnp.float32),
-                       pltpu.VMEM((2, K, scratch_rows * width), jnp.bfloat16)]
-        vmem = pl.BlockSpec(memory_space=pltpu.VMEM)
+                       pltpu.VMEM((2, K, scratch_rows * width), jnp.bfloat16)] + scratch
+        outs = [out if hasattr(out, "dtype") else jax.ShapeDtypeStruct(out, jnp.float32) for out in outs]
         return pl.pallas_call(
-            kernel, out_shape=[jax.ShapeDtypeStruct(s, jnp.float32) for s in outs],
-            in_specs=[pl.BlockSpec(memory_space=pltpu.SMEM)] + [vmem] * len(args),
-            out_specs=[vmem] * len(outs), scratch_shapes=scratch, name=name,
-            compiler_params=pltpu.CompilerParams(vmem_limit_bytes=24 * 1024 * 1024),
-        )(odd, *args)
+            kernel, out_shape=outs, name=name,
+            in_specs=[pl.BlockSpec(memory_space=pltpu.SMEM)] * scalar + [in_space] * len(args),
+            out_specs=[out_space] * len(outs), scratch_shapes=scratch,
+            compiler_params=pltpu.CompilerParams(vmem_limit_bytes=limit * 1024 * 1024),
+        )(*((odd,) if scalar else ()), *args)
 
     def message(slots):
         return [(slots, K // 2, width)] * 2
 
     early, late = tuple(range(SUBSTEPS - 1)), (SUBSTEPS - 1,)
+    f, sea, trig, *sent = call(
+        functools.partial(first_kernel, early), "first_edges", [pltpu.with_memory_space_constraint(x, pltpu.HBM) for x in (f, sea_mask, trig)],
+        [f, sea_mask, trig] + message(SUBSTEPS - 1), scratch=[dma((2,)), dma((BLOCKS,))], in_space=hbm, limit=24)
     rows = (f,)
-    masks = (sea_mask, ice_mask, wind, trig, source_matrix)
-    sent = call(functools.partial(edges_kernel, early), "early_edges", (sea_mask, trig) + rows, message(SUBSTEPS - 1))
+    masks = (sea, ice_mask, wind, trig, source_matrix)
     for step in range(STEPS):
         came = swap(sent)
-        sent = call(functools.partial(edges_kernel, late), "late_edges", (sea_mask, trig) + rows, message(1))
+        sent = call(functools.partial(edges_kernel, late), "late_edges", (sea, trig) + rows, message(1))
         came_late = swap(sent)
-        middle, part = call(middle_kernel, "middle_rows", masks + came + rows,
+        local, = call(local_kernel, "local_rows", (sea, trig) + rows, [(count, K, width)], scalar=False)
+        middle, part = call(middle_kernel, "middle_rows", masks + came + (local,),
                             [(count - 2, K, width), (2, K, width)], count - 2)
         last = step == STEPS - 1
         outs = [(count, K, width)] if last else [(2, K, width)] + message(SUBSTEPS - 1)
-        result = call(functools.partial(edge_kernel, last), "edge_rows", masks + came_late + (part, middle), outs, 2)
+        result = call(functools.partial(edge_kernel, last), "edge_rows", masks + came_late + (part, middle), outs, 2,
+                      scratch=[dma((2 * CHUNKS + 1,))] if last else (), out_space=hbm if last else vmem)
         if last:
             return jnp.transpose(result[0], (1, 0, 2))
         rows, sent = (result[0], middle), result[1:]

time: 61.6 us -> 54.4 us (0.88)
  waiting for transfers between devices: 17.5 us -> 8.18 us
  Pallas kernels: 26 us -> 31.1 us
  local copies, waits for them, and re-layouts: 3.05 us -> 0.02 us
    ppermute x8, waiting for transfers between devices: 17.5 us -> 8.18 us  [swap(): lax.ppermute(value, 'comp', pairs + [(j, i) for i, j in pairs])]
    pallas_call x7 -> x9, Pallas kernels: 26 us -> 31.1 us  [call(): pl.pallas_call(kernel, out_shape=outs, name=name, in_specs=[pl.BlockSpec(...]
    unnamed x12 -> x6, local copies, waits for them, and re-layouts: 3.05 us -> 0.02 us
  transfers between devices with their start and end apart: 8 -> 8, of which waited for: 2 -> 2; matrix products, arithmetic and copies ran while one was open for 0% -> 0% of each run, Pallas kernels for 28% -> 39%
where the time goes in v3:
time: 54.4 us; the launch traced here: 54.2 us
  Pallas kernels  31.1 us (57%)
  starting transfers between devices  14.7 us (27%)
  waiting for transfers between devices  8.18 us (15%)
    pallas_call x9, Pallas kernels, call(): pl.pallas_call(kernel, out_shape=outs, name=name, in_specs=[pl.BlockSpec(...  31.1 us
    ppermute x8, starting transfers between devices, swap(): lax.ppermute(value, 'comp', pairs + [(j, i) for i, j in pairs])  14.7 us
    ppermute x8, waiting for transfers between devices, swap(): lax.ppermute(value, 'comp', pairs + [(j, i) for i, j in pairs])  8.18 us
  transfers between devices with their start and end apart: 8, of which 2 were waited for; matrix products, arithmetic and copies ran while one was open for 0% of the time, Pallas kernels for 39%

profile of v3, /device:TPU:1, one launch (start us, length us, event | category | flops | bytes accessed | tf_op | source)
XLA Modules:
  0.0 54.2 jit_solution(7299604227359702885)
XLA Ops:
  0.0 2.4 %first_edges.1 = (f32[3,1152,128]{2,1,0:T(8,128)S(1)}, s32[3,128]{1,0:T(4,128)S(1)}, f32[2,72,128]{2,1,0:T(8,128)S(1)}, f32[2,576,128]{2,1,0:T(8,128)S(1)}, f32[2,576,128]{2,1,0:T(8,128)S(1)}) custom-call(s32[1]{0:T(128)} %bitcast.odd_ref, f32[3,1152,128]{2,1,0:T(8,128)} %bitcast.3, s32[3,128]{1,0:T(4,128)} %sea_hbm.1, f32[2,72,128]{2,1,0:T(8,128)} %constant.19.clone.trig_hbm), custom_call_target="tpu_custom_call" | custom-call | tf_op jit(solution)/shard_map/first_edges/pallas_call | solution.py:433
  2.4 4.5 %collective-permute-start.2 = (f32[2,576,128]{2,1,0:T(8,128)S(1)}, f32[2,576,128]{2,1,0:T(8,128)S(1)}, u32[]{:S(2)}, u32[]{:S(2)}) collective-permute-start(f32[2,576,128]{2,1,0:T(8,128)S(1)} %get-tuple-element.26), channel_id=1, source_target_pairs={{1,2},{3,4},{5,6},{7,8},{9,10},{11,12},{13,14},{2,1},{4,3},{6,5},{... | collective-permute-start | bytes 1769480 | tf_op jit(solution)/shard_map/ppermute | solution.py:420
  7.0 0.1 collective-permute-start.3
  7.0 1.5 %late_edges.2 = (f32[1,576,128]{2,1,0:T(8,128)S(1)}, f32[1,576,128]{2,1,0:T(8,128)S(1)}) custom-call(s32[1]{0:T(128)} %bitcast.odd_ref, s32[3,128]{1,0:T(4,128)S(1)} %get-tuple-element.21.sea_ref, f32[2,72,128]{2,1,0:T(8,128)S(1)} %get-tuple-element.22.trig_ref, f32[3,1152,128]{2,1,0:T(8,128)S(1)} %get-tuple-element.23.refs_0_), custom_call_target="tpu_custom_call" | custom-call | tf_op jit(solution)/shard_map/late_edges/pallas_call | solution.py:433
  8.6 3.5 %collective-permute-start = (f32[1,576,128]{2,1,0:T(8,128)S(1)}, f32[1,576,128]{2,1,0:T(8,128)S(1)}, u32[]{:S(2)}, u32[]{:S(2)}) collective-permute-start(f32[1,576,128]{2,1,0:T(8,128)S(1)} %get-tuple-element.24), channel_id=1, source_target_pairs={{1,2},{3,4},{5,6},{7,8},{9,10},{11,12},{13,14},{2,1},{4,3},{6,5},{... | collective-permute-start | bytes 884744 | tf_op jit(solution)/shard_map/ppermute | solution.py:420
  12.1 0.0 copy-start
  12.1 0.0 copy-start.1
  12.1 0.0 copy-start.2
  12.1 0.1 collective-permute-start.1
  12.2 4.8 %local_rows.2.local_ref = f32[3,1152,128]{2,1,0:T(8,128)S(1)} custom-call(s32[3,128]{1,0:T(4,128)S(1)} %get-tuple-element.21.sea_ref, f32[2,72,128]{2,1,0:T(8,128)S(1)} %get-tuple-element.22.trig_ref, f32[3,1152,128]{2,1,0:T(8,128)S(1)} %get-tuple-element.23.refs_0_), custom_call_target="tpu_custom_call" | custom-call | tf_op jit(solution)/shard_map/local_rows/pallas_call | solution.py:433
  17.0 6.2 %collective-permute-done.2.cross_ref = f32[2,576,128]{2,1,0:T(8,128)S(1)} collective-permute-done((f32[2,576,128]{2,1,0:T(8,128)S(1)}, f32[2,576,128]{2,1,0:T(8,128)S(1)}, u32[]{:S(2)}, u32[]{:S(2)}) %collective-permute-start.2) | collective-permute-done | bytes 589856 | tf_op jit(solution)/shard_map/ppermute | solution.py:420
  23.2 0.0 collective-permute-done.3.inner_ref
  23.2 0.0 copy-done
  23.2 0.0 copy-done.1
  23.2 0.0 copy-done.2
  23.3 4.2 %middle_rows.2 = (f32[1,1152,128]{2,1,0:T(8,128)S(1)}, f32[2,1152,128]{2,1,0:T(8,128)S(1)}) custom-call(s32[1]{0:T(128)} %bitcast.odd_ref, s32[3,128]{1,0:T(4,128)S(1)} %get-tuple-element.21.sea_ref, s32[3,128]{1,0:T(4,128)S(1)} %copy-done.1, f32[3,128]{1,0:T(4,128)S(1)} %copy-done.2, f32[2,72,128]{2,1,0:T(8,128)S(1)} %get-tuple-element.22.trig_ref, ...), custom_call_target="tpu_custom_call" | custom-call | tf_op jit(solution)/shard_map/middle_rows/pallas_call | solution.py:433
  27.5 0.0 collective-permute-done.cross_in
  27.5 0.0 collective-permute-done.1.inner_in
  27.5 3.8 %edge_rows.2 = (f32[2,1152,128]{2,1,0:T(8,128)S(1)}, f32[2,576,128]{2,1,0:T(8,128)S(1)}, f32[2,576,128]{2,1,0:T(8,128)S(1)}) custom-call(s32[1]{0:T(128)} %bitcast.odd_ref, s32[3,128]{1,0:T(4,128)S(1)} %get-tuple-element.21.sea_ref, s32[3,128]{1,0:T(4,128)S(1)} %copy-done.1, f32[3,128]{1,0:T(4,128)S(1)} %copy-done.2, ...), custom_call_target="tpu_custom_call" | custom-call | tf_op jit(solution)/shard_map/edge_rows/pallas_call | solution.py:433
  31.3 4.4 %collective-permute-start.6 = (f32[2,576,128]{2,1,0:T(8,128)S(1)}, f32[2,576,128]{2,1,0:T(8,128)S(1)}, u32[]{:S(2)}, u32[]{:S(2)}) collective-permute-start(f32[2,576,128]{2,1,0:T(8,128)S(1)} %get-tuple-element.33), channel_id=1, source_target_pairs={{1,2},{3,4},{5,6},{7,8},{9,10},{11,12},{13,14},{2,1},{4,3},{6,5},{... | collective-permute-start | bytes 1769480 | tf_op jit(solution)/shard_map/ppermute | solution.py:420
  35.7 0.1 collective-permute-start.7
  35.8 1.5 %late_edges.3 = (f32[1,576,128]{2,1,0:T(8,128)S(1)}, f32[1,576,128]{2,1,0:T(8,128)S(1)}) custom-call(s32[1]{0:T(128)} %bitcast.odd_ref, s32[3,128]{1,0:T(4,128)S(1)} %get-tuple-element.21.sea_ref, f32[2,72,128]{2,1,0:T(8,128)S(1)} %get-tuple-element.22.trig_ref, f32[2,1152,128]{2,1,0:T(8,128)S(1)} %get-tuple-element.30.refs_0_, ...), custom_call_target="tpu_custom_call" | custom-call | tf_op jit(solution)/shard_map/late_edges/pallas_call | solution.py:433
  37.3 1.9 %collective-permute-start.4 = (f32[1,576,128]{2,1,0:T(8,128)S(1)}, f32[1,576,128]{2,1,0:T(8,128)S(1)}, u32[]{:S(2)}, u32[]{:S(2)}) collective-permute-start(f32[1,576,128]{2,1,0:T(8,128)S(1)} %get-tuple-element.31), channel_id=1, source_target_pairs={{1,2},{3,4},{5,6},{7,8},{9,10},{11,12},{13,14},{2,1},{4,3},{6,5},{... | collective-permute-start | bytes 884744 | tf_op jit(solution)/shard_map/ppermute | solution.py:420
  39.3 0.1 collective-permute-start.5
  39.3 4.8 %local_rows.3.local_ref = f32[3,1152,128]{2,1,0:T(8,128)S(1)} custom-call(s32[3,128]{1,0:T(4,128)S(1)} %get-tuple-element.21.sea_ref, f32[2,72,128]{2,1,0:T(8,128)S(1)} %get-tuple-element.22.trig_ref, f32[2,1152,128]{2,1,0:T(8,128)S(1)} %get-tuple-element.30.refs_0_, f32[1,1152,128]{2,1,0:T(8,128)S(1)} %get-tuple-element.29.middle_ref.refs_1_), custom_call_target="tpu_custom_call" | custom-call | tf_op jit(solution)/shard_map/local_rows/pallas_call | solution.py:433
  44.1 1.9 %collective-permute-done.6.cross_ref = f32[2,576,128]{2,1,0:T(8,128)S(1)} collective-permute-done((f32[2,576,128]{2,1,0:T(8,128)S(1)}, f32[2,576,128]{2,1,0:T(8,128)S(1)}, u32[]{:S(2)}, u32[]{:S(2)}) %collective-permute-start.6) | collective-permute-done | bytes 589856 | tf_op jit(solution)/shard_map/ppermute | solution.py:420
  46.0 0.0 collective-permute-done.7.inner_ref
  46.0 4.2 %middle_rows.3 = (f32[1,1152,128]{2,1,0:T(8,128)S(1)}, f32[2,1152,128]{2,1,0:T(8,128)S(1)}) custom-call(s32[1]{0:T(128)} %bitcast.odd_ref, s32[3,128]{1,0:T(4,128)S(1)} %get-tuple-element.21.sea_ref, s32[3,128]{1,0:T(4,128)S(1)} %copy-done.1, f32[3,128]{1,0:T(4,128)S(1)} %copy-done.2, f32[2,72,128]{2,1,0:T(8,128)S(1)} %get-tuple-element.22.trig_ref, ...), custom_call_target="tpu_custom_call" | custom-call | tf_op jit(solution)/shard_map/middle_rows/pallas_call | solution.py:433
  50.2 0.0 collective-permute-done.4.cross_in
  50.2 0.0 collective-permute-done.5.inner_in
  50.3 3.9 %edge_rows.3 = f32[3,1152,128]{2,1,0:T(8,128)} custom-call(s32[1]{0:T(128)} %bitcast.odd_ref, s32[3,128]{1,0:T(4,128)S(1)} %get-tuple-element.21.sea_ref, s32[3,128]{1,0:T(4,128)S(1)} %copy-done.1, f32[3,128]{1,0:T(4,128)S(1)} %copy-done.2, f32[2,72,128]{2,1,0:T(8,128)S(1)} %get-tuple-element.22.trig_ref, bf16[1152,1152]{1,0:T(8,128)(2,1)S(1)} %copy-done, ...), custom_call_target="tpu_custom_call" | custom-call | tf_op jit(solution)/shard_map/edge_rows/pallas_call | solution.py:433
Async XLA Ops:
  2.4 20.8 %collective-permute-start.2 = (f32[2,576,128]{2,1,0:T(8,128)S(1)}, f32[2,576,128]{2,1,0:T(8,128)S(1)}, u32[]{:S(2)}, u32[]{:S(2)}) collective-permute-start(f32[2,576,128]{2,1,0:T(8,128)S(1)} %get-tuple-element.26), channel_id=1, source_target_pairs={{1,2},{3,4},{5,6},{7,8},{9,10},{11,12},{13,14},{2,1},{4,3},{6,5},{... | collective-permute-start | bytes 1769480 | tf_op jit(solution)/shard_map/ppermute | solution.py:420
  7.0 16.3 %collective-permute-start.3 = (f32[2,576,128]{2,1,0:T(8,128)S(1)}, f32[2,576,128]{2,1,0:T(8,128)S(1)}, u32[]{:S(2)}, u32[]{:S(2)}) collective-permute-start(f32[2,576,128]{2,1,0:T(8,128)S(1)} %get-tuple-element.27), channel_id=1, source_target_pairs={{0,1},{2,3},{4,5},{6,7},{8,9},{10,11},{12,13},{14,15},{1,0},{3,2},... | collective-permute-start | bytes 1769480 | tf_op jit(solution)/shard_map/ppermute | solution.py:420
  8.6 18.9 %collective-permute-start = (f32[1,576,128]{2,1,0:T(8,128)S(1)}, f32[1,576,128]{2,1,0:T(8,128)S(1)}, u32[]{:S(2)}, u32[]{:S(2)}) collective-permute-start(f32[1,576,128]{2,1,0:T(8,128)S(1)} %get-tuple-element.24), channel_id=1, source_target_pairs={{1,2},{3,4},{5,6},{7,8},{9,10},{11,12},{13,14},{2,1},{4,3},{6,5},{... | collective-permute-start | bytes 884744 | tf_op jit(solution)/shard_map/ppermute | solution.py:420
  12.1 11.2 %copy-start = (bf16[1152,1152]{1,0:T(8,128)(2,1)S(1)}, bf16[1152,1152]{1,0:T(8,128)(2,1)}, u32[]{:S(2)}) copy-start(bf16[1152,1152]{1,0:T(8,128)(2,1)} %matrix_ref.7) | copy-start | bytes 7962628
  12.1 11.1 %copy-start.1 = (s32[3,128]{1,0:T(4,128)S(1)}, s32[3,128]{1,0:T(4,128)}, u32[]{:S(2)}) copy-start(s32[3,128]{1,0:T(4,128)} %ice_ref.7) | copy-start | bytes 4612
  12.1 11.1 %copy-start.2 = (f32[3,128]{1,0:T(4,128)S(1)}, f32[3,128]{1,0:T(4,128)}, u32[]{:S(2)}) copy-start(f32[3,128]{1,0:T(4,128)} %wind_ref.7) | copy-start | bytes 4612
  12.1 15.4 %collective-permute-start.1 = (f32[1,576,128]{2,1,0:T(8,128)S(1)}, f32[1,576,128]{2,1,0:T(8,128)S(1)}, u32[]{:S(2)}, u32[]{:S(2)}) collective-permute-start(f32[1,576,128]{2,1,0:T(8,128)S(1)} %get-tuple-element.25), channel_id=1, source_target_pairs={{0,1},{2,3},{4,5},{6,7},{8,9},{10,11},{12,13},{14,15},{1,0},{3,2},... | collective-permute-start | bytes 884744 | tf_op jit(solution)/shard_map/ppermute | solution.py:420
  31.3 14.7 %collective-permute-start.6 = (f32[2,576,128]{2,1,0:T(8,128)S(1)}, f32[2,576,128]{2,1,0:T(8,128)S(1)}, u32[]{:S(2)}, u32[]{:S(2)}) collective-permute-start(f32[2,576,128]{2,1,0:T(8,128)S(1)} %get-tuple-element.33), channel_id=1, source_target_pairs={{1,2},{3,4},{5,6},{7,8},{9,10},{11,12},{13,14},{2,1},{4,3},{6,5},{... | collective-permute-start | bytes 1769480 | tf_op jit(solution)/shard_map/ppermute | solution.py:420
  35.7 10.3 %collective-permute-start.7 = (f32[2,576,128]{2,1,0:T(8,128)S(1)}, f32[2,576,128]{2,1,0:T(8,128)S(1)}, u32[]{:S(2)}, u32[]{:S(2)}) collective-permute-start(f32[2,576,128]{2,1,0:T(8,128)S(1)} %get-tuple-element.34), channel_id=1, source_target_pairs={{0,1},{2,3},{4,5},{6,7},{8,9},{10,11},{12,13},{14,15},{1,0},{3,2},... | collective-permute-start | bytes 1769480 | tf_op jit(solution)/shard_map/ppermute | solution.py:420
  37.3 12.9 %collective-permute-start.4 = (f32[1,576,128]{2,1,0:T(8,128)S(1)}, f32[1,576,128]{2,1,0:T(8,128)S(1)}, u32[]{:S(2)}, u32[]{:S(2)}) collective-permute-start(f32[1,576,128]{2,1,0:T(8,128)S(1)} %get-tuple-element.31), channel_id=1, source_target_pairs={{1,2},{3,4},{5,6},{7,8},{9,10},{11,12},{13,14},{2,1},{4,3},{6,5},{... | collective-permute-start | bytes 884744 | tf_op jit(solution)/shard_map/ppermute | solution.py:420
  39.3 11.0 %collective-permute-start.5 = (f32[1,576,128]{2,1,0:T(8,128)S(1)}, f32[1,576,128]{2,1,0:T(8,128)S(1)}, u32[]{:S(2)}, u32[]{:S(2)}) collective-permute-start(f32[1,576,128]{2,1,0:T(8,128)S(1)} %get-tuple-element.32), channel_id=1, source_target_pairs={{0,1},{2,3},{4,5},{6,7},{8,9},{10,11},{12,13},{14,15},{1,0},{3,2},... | collective-permute-start | bytes 884744 | tf_op jit(solution)/shard_map/ppermute | solution.py:420

commit v4 on v0

v4 whole, which is shorter than its diff:
```python
import functools

import jax
import jax.numpy as jnp
import numpy as np
from jax import lax
from jax.experimental import pallas as pl
from jax.experimental.pallas import tpu as pltpu
from jax.sharding import PartitionSpec as P

NDIR = 36
NFREQ = 32
K = 1152
STEPS = 2
SUBSTEPS = 3
SRC_SUB = 3

source_rate = 0.5
damping = 0.5

SUB = 8
QUADRANTS = 4
ARC = NDIR // QUADRANTS
ARC_ROWS = SUB * ARC
BLOCK = QUADRANTS * ARC_ROWS
BLOCKS = K // BLOCK
HALF = BLOCK // 2
CHUNKS = 4
EAST = (True, False, False, True)
NORTH = (True, True, False, False)


def source_row(row):
    quadrant, rest = divmod(row, ARC_ROWS)
    frequency, direction = divmod(rest, ARC)
    return frequency * NDIR + quadrant * ARC + direction


ORDER = [source_row(row) for row in range(BLOCK)]
INVERSE = [ORDER.index(row) for row in range(BLOCK)]


def reorder(read, order, tile, iota):
    pieces = {}
    for to, row in enumerate(order[tile * SUB:(tile + 1) * SUB]):
        pieces.setdefault((row // SUB, (to - row) % SUB), []).append(to)
    out = None
    for (index, shift), rows in pieces.items():
        value = read(index)
        if shift:
            value = pltpu.roll(value, shift, 0)
        out = value if out is None else jnp.where((iota >= rows[0]) & (iota <= rows[-1]), value, out)
    return out


def pattern():
    row = np.arange(ARC_ROWS)
    theta = 2.0 * np.pi * (row % ARC + 0.5) / NDIR
    slower = 0.6 * 0.65 / (NFREQ - 1) * (row // ARC)
    table = np.stack([np.cos(theta), np.sin(theta), slower]).astype(np.float32)
    return jnp.asarray(np.ascontiguousarray(np.broadcast_to(table[:, :, None], (3, ARC_ROWS, 128))))


def sublanes(width):
    return lax.broadcasted_iota(jnp.int32, (SUB, width), 0)


def arc_coefficients(trig_ref, block, i):
    frequency = (block * SUB).astype(jnp.float32)
    fastest = 0.6 * (0.35 + (0.65 / (NFREQ - 1)) * ((NFREQ - 1) - frequency))
    at = pl.ds(i * SUB, SUB)
    speed = fastest - trig_ref[2, at, :]
    one, other = speed * trig_ref[0, at, :], speed * trig_ref[1, at, :]
    return 1.0 - one - other, one, other


def tiles(trig_ref, block):
    for i in range(ARC):
        staying, one, other = arc_coefficients(trig_ref, block, i)
        for q in range(QUADRANTS):
            at = pl.ds(block * BLOCK + q * ARC_ROWS + i * SUB, SUB)
            yield q, i, at, (staying, one, other) if q % 2 == 0 else (staying, other, one)


def beside(q, value):
    return pltpu.roll(value, 1 if EAST[q] else value.shape[1] - 1, 1)


def flow(q, rows):
    return list(rows) if NORTH[q] else list(rows)[::-1]


def substep(q, coefficients, rows, seas, whole):
    staying, along, across = coefficients
    out = []
    for i, row in enumerate(rows):
        if i == 0 and not whole:
            continue
        value = staying * row + along * beside(q, row)
        if i:
            value = value + across * rows[i - 1]
        out.append(seas[i] * value)
    return out


def edges(q, coefficients, rows, seas, number):
    found = [rows[-1]]
    rows, seas = rows[-number:], seas[-number:]
    for _ in range(number - 1):
        rows = substep(q, coefficients, rows, seas, False)
        seas = seas[1:]
        found.append(rows[-1])
    return found


def upstream_part(q, coefficients, seas, beside_second_sea, halo):
    staying, along, across = coefficients
    first = seas[0] * (across * halo[0])
    beside_first = beside(q, first)
    second = seas[1] * (across * first)
    beside_second = beside_second_sea * (across * beside_first)
    first = seas[0] * (staying * first + along * beside_first + across * halo[1])
    third = seas[2] * (across * second)
    second = seas[1] * (staying * second + along * beside_second + across * first)
    first = seas[0] * (staying * first + along * beside(q, first))
    return [first, second, third]


def half_at(q, i, block):
    return pl.ds(block * HALF + (q % 2) * ARC_ROWS + i * SUB, SUB)


def send(block, slot, found, odd, cross_ref, inner_ref):
    for i in range(ARC):
        for q in range(2):
            at = half_at(q, i, block)
            north, south = found[q, i], found[q + 2, i]
            if cross_ref is not None:
                cross_ref[slot[0], at, :] = jnp.where(odd, north, south)
            if inner_ref is not None:
                inner_ref[slot[1], at, :] = jnp.where(odd, south, north)


def receive(q, i, block, slot, odd, cross_ref, inner_ref):
    at = half_at(q, i, block)
    cross, inner = cross_ref[slot[0], at, :], inner_ref[slot[1], at, :]
    return jnp.where(odd, inner, cross) if NORTH[q] else jnp.where(odd, cross, inner)


def spread(ref, r):
    row = ref[pl.ds(r, 1), :]
    return jnp.broadcast_to(row.astype(jnp.float32), (SUB, row.shape[1]))


def spread_all(ref, count):
    return [spread(ref, r) for r in range(count)]


def reader(row_refs):
    if len(row_refs) == 1:
        whole, = row_refs
        return whole.shape, lambda r, at: whole[r, at, :]
    edge, middle = row_refs
    count = middle.shape[0] + 2

    def row(r, at):
        if r == 0:
            return edge[0, at, :]
        if r == count - 1:
            return edge[1, at, :]
        return middle[r - 1, at, :]

    return (count,) + tuple(middle.shape[1:]), row


def early_messages(block, row, count, seas, trig_ref, odd, cross_ref):
    found = {}
    for q, i, at, coefficients in tiles(trig_ref, block):
        rows = flow(q, [row(r, at) for r in range(count)])
        found[q, i] = edges(q, coefficients, rows, flow(q, seas), SUBSTEPS - 1)
    for j in range(SUBSTEPS - 1):
        send(block, (j,), {key: f[j] for key, f in found.items()}, odd, cross_ref, None)


def first_kernel(odd_ref, f_hbm, sea_hbm, trig_hbm, f_ref, sea_ref, trig_ref, cross_ref, raw_ref, sem, block_sem):
    count, _, width = f_ref.shape

    def block_copy(block):
        at = pl.ds(pl.multiple_of(block * BLOCK, BLOCK), BLOCK)
        return pltpu.make_async_copy(f_hbm.at[:, at, :], raw_ref.at[:, at, :], block_sem.at[block])

    small = [pltpu.make_async_copy(sea_hbm, sea_ref, sem.at[0]), pltpu.make_async_copy(trig_hbm, trig_ref, sem.at[1])]
    for copy in small:
        copy.start()
    for block in range(BLOCKS):
        block_copy(block).start()
    for copy in small:
        copy.wait()
    iota = sublanes(width)
    odd = odd_ref[0] == 1
    seas = spread_all(sea_ref, count)

    def body(block, carry):
        block_copy(block).wait()
        put_in_order(block, lambda r, at: raw_ref[r, at, :], f_ref, range(count), iota)
        early_messages(block, lambda r, at: f_ref[r, at, :], count, seas, trig_ref, odd, cross_ref)
        return carry

    lax.fori_loop(0, BLOCKS, body, 0)


def put_in_order(block, read, out_ref, rows, iota):
    for r in rows:
        for t in range(BLOCK // SUB):
            tile = reorder(lambda index: read(r, pl.ds(block * BLOCK + index * SUB, SUB)), ORDER, t, iota)
            out_ref[r, pl.ds(block * BLOCK + t * SUB, SUB), :] = tile


def late_kernel(odd_ref, sea_ref, trig_ref, *refs):
    (count, _, width), row = reader(refs[:-2])
    cross_ref, inner_ref = refs[-2:]
    odd = odd_ref[0] == 1
    seas = spread_all(sea_ref, count)

    def body(block, carry):
        found = {}
        for q, i, at, coefficients in tiles(trig_ref, block):
            rows = flow(q, [row(r, at) for r in range(count)])
            found[q, i] = edges(q, coefficients, rows, flow(q, seas), SUBSTEPS)
        for j in range(SUBSTEPS):
            last = j == SUBSTEPS - 1
            send(block, (0, j), {key: f[j] for key, f in found.items()}, odd, cross_ref if last else None, inner_ref)
        return carry

    lax.fori_loop(0, BLOCKS, body, 0)


def local_kernel(sea_ref, trig_ref, *refs):
    (count, _, width), row = reader(refs[:-1])
    local_ref = refs[-1]
    seas = spread_all(sea_ref, count)

    def body(block, carry):
        for q, i, at, coefficients in tiles(trig_ref, block):
            rows = flow(q, [row(r, at) for r in range(count)])
            for _ in range(SUBSTEPS):
                rows = substep(q, coefficients, rows, flow(q, seas), True)
            for r, value in enumerate(flow(q, rows)):
                local_ref[r, at, :] = value
        return carry

    lax.fori_loop(0, BLOCKS, body, 0)


def lanes(ref, rows):
    return jnp.concatenate([ref[r:r + 1, :].astype(jnp.float32) for r in rows], axis=1)


def source_steps(rows, sums, sea_ref, ice_ref, wind_ref, matrix_ref, f_acc, b_acc, ready=None):
    comps = f_acc.shape[0]
    sea, gain = lanes(sea_ref, rows), source_rate * lanes(wind_ref, rows)
    energy = jnp.concatenate([jnp.sum(s, axis=0, keepdims=True) for s in sums], axis=1)
    chunk = comps // CHUNKS
    for s in range(SRC_SUB):
        scale = sea / (1.0 + (damping / comps) * energy)
        energy = jnp.zeros_like(energy)
        if s + 1 == SRC_SUB:
            scale = scale * (1.0 - 0.5 * lanes(ice_ref, rows))
        for c in range(comps // chunk):
            at = pl.ds(c * chunk, chunk)
            growth = jnp.dot(matrix_ref[at, :], b_acc[s % 2], preferred_element_type=jnp.float32)
            value = (f_acc[at, :] + gain * growth) * scale
            f_acc[at, :] = value
            if s + 1 < SRC_SUB:
                b_acc[(s + 1) % 2, at, :] = value.astype(jnp.bfloat16)
                energy = energy + jnp.sum(value * value, axis=0, keepdims=True)
            elif ready is not None:
                ready(c, at)


def hold(block, column, read, iota, f_acc, b_acc, total):
    width = iota.shape[1]
    columns = slice(column * width, (column + 1) * width)
    for t in range(0, BLOCK // SUB, 2):
        pair = [reorder(read, INVERSE, t + k, iota) for k in range(2)]
        both = jnp.concatenate(pair, axis=0)
        at = pl.ds(block * BLOCK + t * SUB, 2 * SUB)
        f_acc[at, columns] = both
        b_acc[0, at, columns] = both.astype(jnp.bfloat16)
        total = total + pair[0] * pair[0] + pair[1] * pair[1]
    return total


def middle_kernel(last, odd_ref, sea_ref, ice_ref, wind_ref, trig_ref, matrix_ref, cross_ref, inner_ref, local_ref,
                  middle_ref, edge_ref, f_acc, b_acc, moved):
    count, _, width = local_ref.shape
    iota = sublanes(width)
    odd = odd_ref[0] == 1
    seas = spread_all(sea_ref, count)
    beside_seas = [beside(q, flow(q, seas)[1]) for q in range(QUADRANTS)]
    between_rows = range(1, count - 1)

    def advance(block, sums):
        for q, i, at, coefficients in tiles(trig_ref, block):
            halo = [receive(q, i, block, (j, j), odd, cross_ref, inner_ref) for j in range(SUBSTEPS - 1)]
            rows = upstream_part(q, coefficients, flow(q, seas), beside_seas[q], halo)
            rows = flow(q, rows + [0.0] * (count - len(rows)))
            rows = [local_ref[r, at, :] + value for r, value in enumerate(rows)]
            edge_ref[0, at, :], edge_ref[1, at, :] = rows[0], rows[-1]
            for r in between_rows:
                moved[r - 1, at, :] = rows[r]
        return tuple(
            hold(block, i, lambda t: moved[i, pl.ds(block * BLOCK + t * SUB, SUB), :], iota, f_acc, b_acc, total)
            for i, total in enumerate(sums))

    zero = jnp.zeros((SUB, width), jnp.float32)
    sums = lax.fori_loop(0, BLOCKS, advance, (zero,) * len(between_rows))
    source_steps(between_rows, sums, sea_ref, ice_ref, wind_ref, matrix_ref, f_acc, b_acc)
    if last:
        for i in range(count - 2):
            middle_ref[i] = f_acc[:, i * width:(i + 1) * width]
        return

    def finish(block, carry):
        put_in_order(block, lambda r, at: f_acc[at, r * width:(r + 1) * width], middle_ref, range(count - 2), iota)
        return carry

    lax.fori_loop(0, BLOCKS, finish, 0)


def edge_kernel(last, odd_ref, sea_ref, ice_ref, wind_ref, trig_ref, matrix_ref, cross_in, inner_in, part_ref, middle_ref, *refs):
    if last:
        out_ref, f_acc, b_acc, moved, sem = refs
    else:
        out_ref, cross_ref, f_acc, b_acc, moved = refs
    count, width = middle_ref.shape[0] + 2, middle_ref.shape[2]
    iota = sublanes(width)
    odd = odd_ref[0] == 1
    seas = spread_all(sea_ref, count)
    edge_rows = (0, count - 1)
    if last:
        copies = [pltpu.make_async_copy(middle_ref, out_ref.at[pl.ds(1, count - 2)], sem.at[2 * CHUNKS])]
        copies[0].start()

    def advance(block, sums):
        for q, i, at, (_, _, across) in tiles(trig_ref, block):
            halo = receive(q, i, block, (0, SUBSTEPS - 1), odd, cross_in, inner_in)
            first, other = flow(q, (0, 1))
            moved[first, at, :] = part_ref[first, at, :] + flow(q, seas)[0] * (across * halo)
            moved[other, at, :] = part_ref[other, at, :]
        return tuple(
            hold(block, i, lambda t: moved[i, pl.ds(block * BLOCK + t * SUB, SUB), :], iota, f_acc, b_acc, total)
            for i, total in enumerate(sums))

    zero = jnp.zeros((SUB, width), jnp.float32)
    sums = lax.fori_loop(0, BLOCKS, advance, (zero, zero))
    if last:
        def ready(c, at):
            for i, r in enumerate(edge_rows):
                columns = pl.ds(i * width, width)
                copy = pltpu.make_async_copy(f_acc.at[at, columns], out_ref.at[r, at, :], sem.at[2 * c + i])
                copy.start()
                copies.append(copy)

        source_steps(edge_rows, sums, sea_ref, ice_ref, wind_ref, matrix_ref, f_acc, b_acc, ready)
        for copy in copies:
            copy.wait()
        return
    source_steps(edge_rows, sums, sea_ref, ice_ref, wind_ref, matrix_ref, f_acc, b_acc)
    _, row = reader((out_ref, middle_ref))

    def finish(block, carry):
        put_in_order(block, lambda r, at: f_acc[at, r * width:(r + 1) * width], out_ref, range(2), iota)
        early_messages(block, row, count, seas, trig_ref, odd, cross_ref)
        return carry

    lax.fori_loop(0, BLOCKS, finish, 0)


def on_device(spectrum, sea_mask, ice_mask, wind, source_matrix):
    size = lax.axis_size("comp")
    comps, count, width = spectrum.shape
    assert comps == K and count >= SUBSTEPS and size % 2 == 0
    odd = (lax.axis_index("comp") % 2).astype(jnp.int32).reshape(1)
    f = jnp.transpose(spectrum, (1, 0, 2))
    trig = pattern()
    outer_pairs = [(i, i + 1) for i in range(1, size - 1, 2)]
    inner_pairs = [(i, i + 1) for i in range(0, size, 2)]

    def swap(value, pairs):
        return lax.ppermute(value, "comp", pairs + [(j, i) for i, j in pairs])

    vmem = pl.BlockSpec(memory_space=pltpu.VMEM)
    hbm = pl.BlockSpec(memory_space=pltpu.HBM)
    dma = pltpu.SemaphoreType.DMA

    def call(kernel, name, args, outs, scratch_rows=0, scratch=(), in_space=vmem, out_space=vmem, scalar=True, cost=0):
        scratch = list(scratch)
        if scratch_rows:
            scratch = [pltpu.VMEM((K, scratch_rows * width), jnp.float32),
                       pltpu.VMEM((2, K, scratch_rows * width), jnp.bfloat16),
                       pltpu.VMEM((scratch_rows, K, width), jnp.float32)] + scratch
        outs = [out if hasattr(out, "dtype") else jax.ShapeDtypeStruct(out, jnp.float32) for out in outs]
        return pl.pallas_call(
            kernel, out_shape=outs, name=name,
            in_specs=[pl.BlockSpec(memory_space=pltpu.SMEM)] * scalar + [in_space] * len(args),
            out_specs=[out_space] * len(outs), scratch_shapes=scratch,
            cost_estimate=pl.CostEstimate(flops=cost, bytes_accessed=0, transcendentals=0) if cost else None,
            compiler_params=pltpu.CompilerParams(vmem_limit_bytes=24 * 1024 * 1024),
        )(*((odd,) if scalar else ()), *args)

    def message(slots):
        return (slots, K // 2, width)

    whole = jax.ShapeDtypeStruct((count, K, width), jnp.float32)
    operands = [pltpu.with_memory_space_constraint(x, pltpu.HBM) for x in (f, sea_mask, trig)]
    f, sea, trig, cross = call(
        first_kernel, "first_edges", operands, [whole, sea_mask, trig, message(SUBSTEPS - 1)],
        scratch=[pltpu.VMEM(whole.shape, jnp.float32), dma((2,)), dma((BLOCKS,))], in_space=hbm)
    rows = (f,)
    masks = (sea, ice_mask, wind, trig, source_matrix)
    for step in range(STEPS):
        last = step == STEPS - 1
        cross = swap(cross, outer_pairs)
        cross_late, inner = call(late_kernel, "late_edges", (sea, trig) + rows, [message(1), message(SUBSTEPS)])
        cross_late = swap(cross_late, outer_pairs)
        inner = swap(inner, inner_pairs)
        local, = call(local_kernel, "local_rows", (sea, trig) + rows, [whole], scalar=False, cost=30000000000)
        middle, part = call(functools.partial(middle_kernel, last), "middle_rows", masks + (cross, inner, local),
                            [(count - 2, K, width), (2, K, width)], count - 2)
        outs = [whole] if last else [(2, K, width), message(SUBSTEPS - 1)]
        result = call(functools.partial(edge_kernel, last), "edge_rows", masks + (cross_late, inner, part, middle), outs, 2,
                      scratch=[dma((2 * CHUNKS + 1,))] if last else (), out_space=hbm if last else vmem)
        if last:
            return jnp.transpose(result[0], (1, 0, 2))
        rows, cross = (result[0], middle), result[1]


def solution(mesh):
    return jax.shard_map(
        on_device,
        mesh=mesh,
        in_specs=(
            P(None, ("grp", "comp"), None),
            P(("grp", "comp"), None),
            P(("grp", "comp"), None),
            P(("grp", "comp"), None),
            P(),
        ),
        out_specs=P(None, ("grp", "comp"), None),
        check_vma=False,
    )
```

time: 167 us -> 54.2 us (0.32)
  waiting for transfers between devices: 66 us -> 6.58 us
  Pallas kernels: 0 us -> 34.3 us
  starting transfers between devices: 38.5 us -> 12.9 us
  local copies, waits for them, and re-layouts: 25.3 us -> 0.02 us
  other arithmetic: 23.3 us -> 0 us
  matrix products: 12.3 us -> 0 us
    ppermute x12 -> x6, waiting for transfers between devices: 66 us -> 6.58 us  [swap(): return lax.ppermute(value, 'comp', pairs + [(j, i) for i, j in pairs])]
    pallas_call x0 -> x9, Pallas kernels: none -> 34.3 us  [call(): pl.pallas_call(kernel, out_shape=outs, name=name, in_specs=[pl.BlockSpec(...]
    ppermute x12 -> x6, starting transfers between devices: 38.5 us -> 12.9 us  [swap(): return lax.ppermute(value, 'comp', pairs + [(j, i) for i, j in pairs])]
    slice x18 -> x0, local copies, waits for them, and re-layouts: 13.3 us -> none  [the longest x12 11.4 us: advance(): western = jnp.roll(spectra, 1, axis=2)]
    mul x8 -> x0, other arithmetic: 12.7 us -> none  [the longest x4 8.34 us: on_device(): spectra = sea_local[None] * advance(widened, courant_x, courant_y)[:, 1:-1]]
    dot_general x6 -> x0, matrix products: 12.3 us -> none  [sources(): growth = jnp.dot(source_matrix, rounded, preferred_element_type=jnp.float32)]
    reduce_sum x2 -> x0, other arithmetic: 5.96 us -> none  [sources(): energy = jnp.mean(flattened * flattened, axis=0, keepdims=True)]
    reshape x2 -> x0, local copies, waits for them, and re-layouts: 5.6 us -> none  [sources(): return flattened.reshape(layout_shape)]
  transfers between devices with their start and end apart: 12 -> 6, of which waited for: 6 -> 2; matrix products, arithmetic and copies ran while one was open for 0% -> 0% of each run, Pallas kernels for 0% -> 46%
where the time goes in v4:
time: 54.2 us; the launch traced here: 54 us
  Pallas kernels  34.3 us (63%)
  starting transfers between devices  12.9 us (24%)
  waiting for transfers between devices  6.58 us (12%)
    pallas_call x9, Pallas kernels, call(): pl.pallas_call(kernel, out_shape=outs, name=name, in_specs=[pl.BlockSpec(...  34.3 us
    ppermute x6, starting transfers between devices, swap(): return lax.ppermute(value, 'comp', pairs + [(j, i) for i, j in pairs])  12.9 us
    ppermute x6, waiting for transfers between devices, swap(): return lax.ppermute(value, 'comp', pairs + [(j, i) for i, j in pairs])  6.58 us
  transfers between devices with their start and end apart: 6, of which 2 were waited for; matrix products, arithmetic and copies ran while one was open for 0% of the time, Pallas kernels for 46%

profile of v4, /device:TPU:1, one launch (start us, length us, event | category | flops | bytes accessed | tf_op | source)
XLA Modules:
  0.0 54.0 jit_solution(4071746943004183935)
XLA Ops:
  0.0 1.8 %first_edges.1 = (f32[3,1152,128]{2,1,0:T(8,128)S(1)}, s32[3,128]{1,0:T(4,128)S(1)}, f32[3,72,128]{2,1,0:T(8,128)S(1)}, f32[2,576,128]{2,1,0:T(8,128)S(1)}) custom-call(s32[1]{0:T(128)} %bitcast.odd_ref, f32[3,1152,128]{2,1,0:T(8,128)} %bitcast.3, s32[3,128]{1,0:T(4,128)} %sea_hbm.1, f32[3,72,128]{2,1,0:T(8,128)} %constant.19.clone.trig_hbm), custom_call_target="tpu_custom_call" | custom-call | tf_op jit(solution)/shard_map/first_edges/pallas_call | solution.py:404
  1.9 4.5 %collective-permute-start.2 = (f32[2,576,128]{2,1,0:T(8,128)S(1)}, f32[2,576,128]{2,1,0:T(8,128)S(1)}, u32[]{:S(2)}, u32[]{:S(2)}) collective-permute-start(f32[2,576,128]{2,1,0:T(8,128)S(1)} %get-tuple-element.24), channel_id=1, source_target_pairs={{1,2},{3,4},{5,6},{7,8},{9,10},{11,12},{13,14},{2,1},{4,3},{6,5},{... | collective-permute-start | bytes 1769480 | tf_op jit(solution)/shard_map/ppermute | solution.py:391
  6.4 0.9 %late_edges.2 = (f32[1,576,128]{2,1,0:T(8,128)S(1)}, f32[3,576,128]{2,1,0:T(8,128)S(1)}) custom-call(s32[1]{0:T(128)} %bitcast.odd_ref, s32[3,128]{1,0:T(4,128)S(1)} %get-tuple-element.19.sea_ref, f32[3,72,128]{2,1,0:T(8,128)S(1)} %get-tuple-element.20.trig_ref, f32[3,1152,128]{2,1,0:T(8,128)S(1)} %get-tuple-element.21.refs_0_), custom_call_target="tpu_custom_call" | custom-call | tf_op jit(solution)/shard_map/late_edges/pallas_call | solution.py:404
  7.3 1.9 %collective-permute-start = (f32[1,576,128]{2,1,0:T(8,128)S(1)}, f32[1,576,128]{2,1,0:T(8,128)S(1)}, u32[]{:S(2)}, u32[]{:S(2)}) collective-permute-start(f32[1,576,128]{2,1,0:T(8,128)S(1)} %get-tuple-element.22), channel_id=1, source_target_pairs={{1,2},{3,4},{5,6},{7,8},{9,10},{11,12},{13,14},{2,1},{4,3},{6,5},{... | collective-permute-start | bytes 884744 | tf_op jit(solution)/shard_map/ppermute | solution.py:391
  9.2 0.0 copy-start.1
  9.2 0.0 copy-start.2
  9.2 0.1 collective-permute-start.1
  9.3 0.0 copy-start
  9.3 7.9 %local_rows.2.local_ref = f32[3,1152,128]{2,1,0:T(8,128)S(1)} custom-call(s32[3,128]{1,0:T(4,128)S(1)} %get-tuple-element.19.sea_ref, f32[3,72,128]{2,1,0:T(8,128)S(1)} %get-tuple-element.20.trig_ref, f32[3,1152,128]{2,1,0:T(8,128)S(1)} %get-tuple-element.21.refs_0_), custom_call_target="tpu_custom_call" | custom-call | flops 30000001024 | tf_op jit(solution)/shard_map/local_rows/pallas_call | solution.py:404
  17.2 5.5 %collective-permute-done.2.cross_ref = f32[2,576,128]{2,1,0:T(8,128)S(1)} collective-permute-done((f32[2,576,128]{2,1,0:T(8,128)S(1)}, f32[2,576,128]{2,1,0:T(8,128)S(1)}, u32[]{:S(2)}, u32[]{:S(2)}) %collective-permute-start.2) | collective-permute-done | bytes 589856 | tf_op jit(solution)/shard_map/ppermute | solution.py:391
  22.7 0.0 collective-permute-done.1.inner_ref.inner_in
  22.7 0.0 copy-done.1
  22.7 0.0 copy-done.2
  22.7 0.0 copy-done
  22.7 3.7 %middle_rows.2 = (f32[1,1152,128]{2,1,0:T(8,128)S(1)}, f32[2,1152,128]{2,1,0:T(8,128)S(1)}) custom-call(s32[1]{0:T(128)} %bitcast.odd_ref, s32[3,128]{1,0:T(4,128)S(1)} %get-tuple-element.19.sea_ref, s32[3,128]{1,0:T(4,128)S(1)} %copy-done.1, f32[3,128]{1,0:T(4,128)S(1)} %copy-done.2, f32[3,72,128]{2,1,0:T(8,128)S(1)} %get-tuple-element.20.trig_ref, ...), custom_call_target="tpu_custom_call" | custom-call | tf_op jit(solution)/shard_map/middle_rows/pallas_call | solution.py:404
  26.4 0.0 collective-permute-done.cross_in
  26.4 3.6 %edge_rows.2 = (f32[2,1152,128]{2,1,0:T(8,128)S(1)}, f32[2,576,128]{2,1,0:T(8,128)S(1)}) custom-call(s32[1]{0:T(128)} %bitcast.odd_ref, s32[3,128]{1,0:T(4,128)S(1)} %get-tuple-element.19.sea_ref, s32[3,128]{1,0:T(4,128)S(1)} %copy-done.1, f32[3,128]{1,0:T(4,128)S(1)} %copy-done.2, f32[3,72,128]{2,1,0:T(8,128)S(1)} %get-tuple-element.20.trig_ref, ...), custom_call_target="tpu_custom_call" | custom-call | tf_op jit(solution)/shard_map/edge_rows/pallas_call | solution.py:404
  30.0 4.4 %collective-permute-start.5 = (f32[2,576,128]{2,1,0:T(8,128)S(1)}, f32[2,576,128]{2,1,0:T(8,128)S(1)}, u32[]{:S(2)}, u32[]{:S(2)}) collective-permute-start(f32[2,576,128]{2,1,0:T(8,128)S(1)} %get-tuple-element.30), channel_id=1, source_target_pairs={{1,2},{3,4},{5,6},{7,8},{9,10},{11,12},{13,14},{2,1},{4,3},{6,5},{... | collective-permute-start | bytes 1769480 | tf_op jit(solution)/shard_map/ppermute | solution.py:391
  34.4 0.9 %late_edges.3 = (f32[1,576,128]{2,1,0:T(8,128)S(1)}, f32[3,576,128]{2,1,0:T(8,128)S(1)}) custom-call(s32[1]{0:T(128)} %bitcast.odd_ref, s32[3,128]{1,0:T(4,128)S(1)} %get-tuple-element.19.sea_ref, f32[3,72,128]{2,1,0:T(8,128)S(1)} %get-tuple-element.20.trig_ref, f32[2,1152,128]{2,1,0:T(8,128)S(1)} %get-tuple-element.27.refs_0_, ...), custom_call_target="tpu_custom_call" | custom-call | tf_op jit(solution)/shard_map/late_edges/pallas_call | solution.py:404
  35.3 1.9 %collective-permute-start.3 = (f32[1,576,128]{2,1,0:T(8,128)S(1)}, f32[1,576,128]{2,1,0:T(8,128)S(1)}, u32[]{:S(2)}, u32[]{:S(2)}) collective-permute-start(f32[1,576,128]{2,1,0:T(8,128)S(1)} %get-tuple-element.28), channel_id=1, source_target_pairs={{1,2},{3,4},{5,6},{7,8},{9,10},{11,12},{13,14},{2,1},{4,3},{6,5},{... | collective-permute-start | bytes 884744 | tf_op jit(solution)/shard_map/ppermute | solution.py:391
  37.3 0.1 collective-permute-start.4
  37.3 7.9 %local_rows.3.local_ref = f32[3,1152,128]{2,1,0:T(8,128)S(1)} custom-call(s32[3,128]{1,0:T(4,128)S(1)} %get-tuple-element.19.sea_ref, f32[3,72,128]{2,1,0:T(8,128)S(1)} %get-tuple-element.20.trig_ref, f32[2,1152,128]{2,1,0:T(8,128)S(1)} %get-tuple-element.27.refs_0_, f32[1,1152,128]{2,1,0:T(8,128)S(1)} %get-tuple-element.26.middle_ref.refs_1_), custom_call_target="tpu_custom_call" | custom-call | flops 30000001024 | tf_op jit(solution)/shard_map/local_rows/pallas_call | solution.py:404
  45.2 1.1 %collective-permute-done.5.cross_ref = f32[2,576,128]{2,1,0:T(8,128)S(1)} collective-permute-done((f32[2,576,128]{2,1,0:T(8,128)S(1)}, f32[2,576,128]{2,1,0:T(8,128)S(1)}, u32[]{:S(2)}, u32[]{:S(2)}) %collective-permute-start.5) | collective-permute-done | bytes 589856 | tf_op jit(solution)/shard_map/ppermute | solution.py:391
  46.4 0.0 collective-permute-done.4.inner_ref.inner_in
  46.4 3.6 %middle_rows.3 = (f32[1,1152,128]{2,1,0:T(8,128)S(1)}, f32[2,1152,128]{2,1,0:T(8,128)S(1)}) custom-call(s32[1]{0:T(128)} %bitcast.odd_ref, s32[3,128]{1,0:T(4,128)S(1)} %get-tuple-element.19.sea_ref, s32[3,128]{1,0:T(4,128)S(1)} %copy-done.1, f32[3,128]{1,0:T(4,128)S(1)} %copy-done.2, f32[3,72,128]{2,1,0:T(8,128)S(1)} %get-tuple-element.20.trig_ref, ...), custom_call_target="tpu_custom_call" | custom-call | tf_op jit(solution)/shard_map/middle_rows/pallas_call | solution.py:404
  50.0 0.0 collective-permute-done.3.cross_in
  50.0 4.0 %edge_rows.3 = f32[3,1152,128]{2,1,0:T(8,128)} custom-call(s32[1]{0:T(128)} %bitcast.odd_ref, s32[3,128]{1,0:T(4,128)S(1)} %get-tuple-element.19.sea_ref, s32[3,128]{1,0:T(4,128)S(1)} %copy-done.1, f32[3,128]{1,0:T(4,128)S(1)} %copy-done.2, f32[3,72,128]{2,1,0:T(8,128)S(1)} %get-tuple-element.20.trig_ref, bf16[1152,1152]{1,0:T(8,128)(2,1)S(1)} %copy-done, ...), custom_call_target="tpu_custom_call" | custom-call | tf_op jit(solution)/shard_map/edge_rows/pallas_call | solution.py:404
Async XLA Ops:
  1.9 20.8 %collective-permute-start.2 = (f32[2,576,128]{2,1,0:T(8,128)S(1)}, f32[2,576,128]{2,1,0:T(8,128)S(1)}, u32[]{:S(2)}, u32[]{:S(2)}) collective-permute-start(f32[2,576,128]{2,1,0:T(8,128)S(1)} %get-tuple-element.24), channel_id=1, source_target_pairs={{1,2},{3,4},{5,6},{7,8},{9,10},{11,12},{13,14},{2,1},{4,3},{6,5},{... | collective-permute-start | bytes 1769480 | tf_op jit(solution)/shard_map/ppermute | solution.py:391
  7.3 19.1 %collective-permute-start = (f32[1,576,128]{2,1,0:T(8,128)S(1)}, f32[1,576,128]{2,1,0:T(8,128)S(1)}, u32[]{:S(2)}, u32[]{:S(2)}) collective-permute-start(f32[1,576,128]{2,1,0:T(8,128)S(1)} %get-tuple-element.22), channel_id=1, source_target_pairs={{1,2},{3,4},{5,6},{7,8},{9,10},{11,12},{13,14},{2,1},{4,3},{6,5},{... | collective-permute-start | bytes 884744 | tf_op jit(solution)/shard_map/ppermute | solution.py:391
  9.2 13.5 %copy-start.1 = (s32[3,128]{1,0:T(4,128)S(1)}, s32[3,128]{1,0:T(4,128)}, u32[]{:S(2)}) copy-start(s32[3,128]{1,0:T(4,128)} %ice_ref.7) | copy-start | bytes 4612
  9.2 13.5 %copy-start.2 = (f32[3,128]{1,0:T(4,128)S(1)}, f32[3,128]{1,0:T(4,128)}, u32[]{:S(2)}) copy-start(f32[3,128]{1,0:T(4,128)} %wind_ref.7) | copy-start | bytes 4612
  9.2 13.5 %collective-permute-start.1 = (f32[3,576,128]{2,1,0:T(8,128)S(1)}, f32[3,576,128]{2,1,0:T(8,128)S(1)}, u32[]{:S(2)}, u32[]{:S(2)}) collective-permute-start(f32[3,576,128]{2,1,0:T(8,128)S(1)} %get-tuple-element.23), channel_id=1, source_target_pairs={{0,1},{2,3},{4,5},{6,7},{8,9},{10,11},{12,13},{14,15},{1,0},{3,2},... | collective-permute-start | bytes 2654216 | tf_op jit(solution)/shard_map/ppermute | solution.py:391
  9.3 13.4 %copy-start = (bf16[1152,1152]{1,0:T(8,128)(2,1)S(1)}, bf16[1152,1152]{1,0:T(8,128)(2,1)}, u32[]{:S(2)}) copy-start(bf16[1152,1152]{1,0:T(8,128)(2,1)} %matrix_ref.7) | copy-start | bytes 7962628
  30.0 16.3 %collective-permute-start.5 = (f32[2,576,128]{2,1,0:T(8,128)S(1)}, f32[2,576,128]{2,1,0:T(8,128)S(1)}, u32[]{:S(2)}, u32[]{:S(2)}) collective-permute-start(f32[2,576,128]{2,1,0:T(8,128)S(1)} %get-tuple-element.30), channel_id=1, source_target_pairs={{1,2},{3,4},{5,6},{7,8},{9,10},{11,12},{13,14},{2,1},{4,3},{6,5},{... | collective-permute-start | bytes 1769480 | tf_op jit(solution)/shard_map/ppermute | solution.py:391
  35.3 14.7 %collective-permute-start.3 = (f32[1,576,128]{2,1,0:T(8,128)S(1)}, f32[1,576,128]{2,1,0:T(8,128)S(1)}, u32[]{:S(2)}, u32[]{:S(2)}) collective-permute-start(f32[1,576,128]{2,1,0:T(8,128)S(1)} %get-tuple-element.28), channel_id=1, source_target_pairs={{1,2},{3,4},{5,6},{7,8},{9,10},{11,12},{13,14},{2,1},{4,3},{6,5},{... | collective-permute-start | bytes 884744 | tf_op jit(solution)/shard_map/ppermute | solution.py:391
  37.3 9.1 %collective-permute-start.4 = (f32[3,576,128]{2,1,0:T(8,128)S(1)}, f32[3,576,128]{2,1,0:T(8,128)S(1)}, u32[]{:S(2)}, u32[]{:S(2)}) collective-permute-start(f32[3,576,128]{2,1,0:T(8,128)S(1)} %get-tuple-element.29), channel_id=1, source_target_pairs={{0,1},{2,3},{4,5},{6,7},{8,9},{10,11},{12,13},{14,15},{1,0},{3,2},... | collective-permute-start | bytes 2654216 | tf_op jit(solution)/shard_map/ppermute | solution.py:391

commit v5 on v4

--- a/solution.py
+++ b/solution.py
@@ -65,25 +65,28 @@
     return lax.broadcasted_iota(jnp.int32, (SUB, width), 0)
 
 
-def arc_coefficients(trig_ref, block, i):
+def block_parts(trig_ref, block):
     frequency = (block * SUB).astype(jnp.float32)
     fastest = 0.6 * (0.35 + (0.65 / (NFREQ - 1)) * ((NFREQ - 1) - frequency))
-    at = pl.ds(i * SUB, SUB)
-    speed = fastest - trig_ref[2, at, :]
-    one, other = speed * trig_ref[0, at, :], speed * trig_ref[1, at, :]
-    return 1.0 - one - other, one, other
-
-
-def tiles(trig_ref, block):
-    for i in range(ARC):
-        staying, one, other = arc_coefficients(trig_ref, block, i)
-        for q in range(QUADRANTS):
-            at = pl.ds(block * BLOCK + q * ARC_ROWS + i * SUB, SUB)
-            yield q, i, at, (staying, one, other) if q % 2 == 0 else (staying, other, one)
+    cosine, sine, slower = (trig_ref[i].reshape(ARC, SUB, -1) for i in range(3))
+    one, other = (fastest - slower) * cosine, (fastest - slower) * sine
+    staying = 1.0 - one - other
+    for q in range(QUADRANTS):
+        at = pl.ds(block * BLOCK + q * ARC_ROWS, ARC_ROWS)
+        yield q, at, (staying, one, other) if q % 2 == 0 else (staying, other, one)
+
+
+def get(ref, r, at):
+    return ref[r, at, :].reshape(ARC, SUB, -1)
+
+
+def put(ref, r, at, value):
+    ref[r, at, :] = value.reshape(ARC_ROWS, -1)
 
 
 def beside(q, value):
-    return pltpu.roll(value, 1 if EAST[q] else value.shape[1] - 1, 1)
+    last = value.ndim - 1
+    return pltpu.roll(value, 1 if EAST[q] else value.shape[last] - 1, last)
 
 
 def flow(q, rows):
@@ -126,24 +129,22 @@
     return [first, second, third]
 
 
-def half_at(q, i, block):
-    return pl.ds(block * HALF + (q % 2) * ARC_ROWS + i * SUB, SUB)
+def half_at(q, block):
+    return pl.ds(block * HALF + (q % 2) * ARC_ROWS, ARC_ROWS)
 
 
 def send(block, slot, found, odd, cross_ref, inner_ref):
-    for i in range(ARC):
-        for q in range(2):
-            at = half_at(q, i, block)
-            north, south = found[q, i], found[q + 2, i]
-            if cross_ref is not None:
-                cross_ref[slot[0], at, :] = jnp.where(odd, north, south)
-            if inner_ref is not None:
-                inner_ref[slot[1], at, :] = jnp.where(odd, south, north)
-
-
-def receive(q, i, block, slot, odd, cross_ref, inner_ref):
-    at = half_at(q, i, block)
-    cross, inner = cross_ref[slot[0], at, :], inner_ref[slot[1], at, :]
+    for q in range(2):
+        north, south = found[q], found[q + 2]
+        if cross_ref is not None:
+            put(cross_ref, slot[0], half_at(q, block), jnp.where(odd, north, south))
+        if inner_ref is not None:
+            put(inner_ref, slot[1], half_at(q, block), jnp.where(odd, south, north))
+
+
+def receive(q, block, slot, odd, cross_ref, inner_ref):
+    at = half_at(q, block)
+    cross, inner = get(cross_ref, slot[0], at), get(inner_ref, slot[1], at)
     return jnp.where(odd, inner, cross) if NORTH[q] else jnp.where(odd, cross, inner)
 
 
@@ -159,27 +160,27 @@
 def reader(row_refs):
     if len(row_refs) == 1:
         whole, = row_refs
-        return whole.shape, lambda r, at: whole[r, at, :]
+        return whole.shape, lambda r, at: get(whole, r, at)
     edge, middle = row_refs
     count = middle.shape[0] + 2
 
     def row(r, at):
         if r == 0:
-            return edge[0, at, :]
+            return get(edge, 0, at)
         if r == count - 1:
-            return edge[1, at, :]
-        return middle[r - 1, at, :]
+            return get(edge, 1, at)
+        return get(middle, r - 1, at)
 
     return (count,) + tuple(middle.shape[1:]), row
 
 
 def early_messages(block, row, count, seas, trig_ref, odd, cross_ref):
-    found = {}
-    for q, i, at, coefficients in tiles(trig_ref, block):
+    found = []
+    for q, at, coefficients in block_parts(trig_ref, block):
         rows = flow(q, [row(r, at) for r in range(count)])
-        found[q, i] = edges(q, coefficients, rows, flow(q, seas), SUBSTEPS - 1)
+        found.append(edges(q, coefficients, rows, flow(q, seas), SUBSTEPS - 1))
     for j in range(SUBSTEPS - 1):
-        send(block, (j,), {key: f[j] for key, f in found.items()}, odd, cross_ref, None)
+        send(block, (j,), [f[j] for f in found], odd, cross_ref, None)
 
 
 def first_kernel(odd_ref, f_hbm, sea_hbm, trig_hbm, f_ref, sea_ref, trig_ref, cross_ref, raw_ref, sem, block_sem):
@@ -203,7 +204,7 @@
     def body(block, carry):
         block_copy(block).wait()
         put_in_order(block, lambda r, at: raw_ref[r, at, :], f_ref, range(count), iota)
-        early_messages(block, lambda r, at: f_ref[r, at, :], count, seas, trig_ref, odd, cross_ref)
+        early_messages(block, lambda r, at: get(f_ref, r, at), count, seas, trig_ref, odd, cross_ref)
         return carry
 
     lax.fori_loop(0, BLOCKS, body, 0)
@@ -223,13 +224,13 @@
     seas = spread_all(sea_ref, count)
 
     def body(block, carry):
-        found = {}
-        for q, i, at, coefficients in tiles(trig_ref, block):
+        found = []
+        for q, at, coefficients in block_parts(trig_ref, block):
             rows = flow(q, [row(r, at) for r in range(count)])
-            found[q, i] = edges(q, coefficients, rows, flow(q, seas), SUBSTEPS)
+            found.append(edges(q, coefficients, rows, flow(q, seas), SUBSTEPS))
         for j in range(SUBSTEPS):
             last = j == SUBSTEPS - 1
-            send(block, (0, j), {key: f[j] for key, f in found.items()}, odd, cross_ref if last else None, inner_ref)
+            send(block, (0, j), [f[j] for f in found], odd, cross_ref if last else None, inner_ref)
         return carry
 
     lax.fori_loop(0, BLOCKS, body, 0)
@@ -241,12 +242,12 @@
     seas = spread_all(sea_ref, count)
 
     def body(block, carry):
-        for q, i, at, coefficients in tiles(trig_ref, block):
+        for q, at, coefficients in block_parts(trig_ref, block):
             rows = flow(q, [row(r, at) for r in range(count)])
             for _ in range(SUBSTEPS):
                 rows = substep(q, coefficients, rows, flow(q, seas), True)
             for r, value in enumerate(flow(q, rows)):
-                local_ref[r, at, :] = value
+                put(local_ref, r, at, value)
         return carry
 
     lax.fori_loop(0, BLOCKS, body, 0)
@@ -301,14 +302,15 @@
     between_rows = range(1, count - 1)
 
     def advance(block, sums):
-        for q, i, at, coefficients in tiles(trig_ref, block):
-            halo = [receive(q, i, block, (j, j), odd, cross_ref, inner_ref) for j in range(SUBSTEPS - 1)]
+        for q, at, coefficients in block_parts(trig_ref, block):
+            halo = [receive(q, block, (j, j), odd, cross_ref, inner_ref) for j in range(SUBSTEPS - 1)]
             rows = upstream_part(q, coefficients, flow(q, seas), beside_seas[q], halo)
             rows = flow(q, rows + [0.0] * (count - len(rows)))
-            rows = [local_ref[r, at, :] + value for r, value in enumerate(rows)]
-            edge_ref[0, at, :], edge_ref[1, at, :] = rows[0], rows[-1]
+            rows = [get(local_ref, r, at) + value for r, value in enumerate(rows)]
+            put(edge_ref, 0, at, rows[0])
+            put(edge_ref, 1, at, rows[-1])
             for r in between_rows:
-                moved[r - 1, at, :] = rows[r]
+                put(moved, r - 1, at, rows[r])
         return tuple(
             hold(block, i, lambda t: moved[i, pl.ds(block * BLOCK + t * SUB, SUB), :], iota, f_acc, b_acc, total)
             for i, total in enumerate(sums))
@@ -343,11 +345,11 @@
         copies[0].start()
 
     def advance(block, sums):
-        for q, i, at, (_, _, across) in tiles(trig_ref, block):
-            halo = receive(q, i, block, (0, SUBSTEPS - 1), odd, cross_in, inner_in)
+        for q, at, (_, _, across) in block_parts(trig_ref, block):
+            halo = receive(q, block, (0, SUBSTEPS - 1), odd, cross_in, inner_in)
             first, other = flow(q, (0, 1))
-            moved[first, at, :] = part_ref[first, at, :] + flow(q, seas)[0] * (across * halo)
-            moved[other, at, :] = part_ref[other, at, :]
+            put(moved, first, at, get(part_ref, first, at) + flow(q, seas)[0] * (across * halo))
+            put(moved, other, at, get(part_ref, other, at))
         return tuple(
             hold(block, i, lambda t: moved[i, pl.ds(block * BLOCK + t * SUB, SUB), :], iota, f_acc, b_acc, total)
             for i, total in enumerate(sums))

time: 54.2 us -> 51.1 us (0.943)
  Pallas kernels: 34.3 us -> 23.4 us
  waiting for transfers between devices: 6.58 us -> 14.4 us
    pallas_call x9, Pallas kernels: 34.3 us -> 23.4 us  [call(): pl.pallas_call(kernel, out_shape=outs, name=name, in_specs=[pl.BlockSpec(...]
    ppermute x6, waiting for transfers between devices: 6.58 us -> 14.4 us  [swap(): return lax.ppermute(value, 'comp', pairs + [(j, i) for i, j in pairs])]
  transfers between devices with their start and end apart: 6 -> 6, of which waited for: 2 -> 2; matrix products, arithmetic and copies ran while one was open for 0% -> 0% of each run, Pallas kernels for 46% -> 27%
where the time goes in v5:
time: 51.1 us; the launch traced here: 50.9 us
  Pallas kernels  23.4 us (46%)
  waiting for transfers between devices  14.4 us (28%)
  starting transfers between devices  12.9 us (25%)
    pallas_call x9, Pallas kernels, call(): pl.pallas_call(kernel, out_shape=outs, name=name, in_specs=[pl.BlockSpec(...  23.4 us
    ppermute x6, waiting for transfers between devices, swap(): return lax.ppermute(value, 'comp', pairs + [(j, i) for i, j in pairs])  14.4 us
    ppermute x6, starting transfers between devices, swap(): return lax.ppermute(value, 'comp', pairs + [(j, i) for i, j in pairs])  12.9 us
  transfers between devices with their start and end apart: 6, of which 2 were waited for; matrix products, arithmetic and copies ran while one was open for 0% of the time, Pallas kernels for 27%

profile of v5, /device:TPU:1, one launch (start us, length us, event | category | flops | bytes accessed | tf_op | source)
XLA Modules:
  0.0 50.9 jit_solution(51250072889353723)
XLA Ops:
  0.0 1.9 %first_edges.1 = (f32[3,1152,128]{2,1,0:T(8,128)S(1)}, s32[3,128]{1,0:T(4,128)S(1)}, f32[3,72,128]{2,1,0:T(8,128)S(1)}, f32[2,576,128]{2,1,0:T(8,128)S(1)}) custom-call(s32[1]{0:T(128)} %bitcast.odd_ref, f32[3,1152,128]{2,1,0:T(8,128)} %bitcast.3, s32[3,128]{1,0:T(4,128)} %sea_hbm.1, f32[3,72,128]{2,1,0:T(8,128)} %constant.19.clone.trig_hbm), custom_call_target="tpu_custom_call" | custom-call | tf_op jit(solution)/shard_map/first_edges/pallas_call | solution.py:406
  1.9 4.5 %collective-permute-start.2 = (f32[2,576,128]{2,1,0:T(8,128)S(1)}, f32[2,576,128]{2,1,0:T(8,128)S(1)}, u32[]{:S(2)}, u32[]{:S(2)}) collective-permute-start(f32[2,576,128]{2,1,0:T(8,128)S(1)} %get-tuple-element.24), channel_id=1, source_target_pairs={{1,2},{3,4},{5,6},{7,8},{9,10},{11,12},{13,14},{2,1},{4,3},{6,5},{... | collective-permute-start | bytes 1769480 | tf_op jit(solution)/shard_map/ppermute | solution.py:393
  6.4 0.9 %late_edges.2 = (f32[1,576,128]{2,1,0:T(8,128)S(1)}, f32[3,576,128]{2,1,0:T(8,128)S(1)}) custom-call(s32[1]{0:T(128)} %bitcast.odd_ref, s32[3,128]{1,0:T(4,128)S(1)} %get-tuple-element.19.sea_ref, f32[3,72,128]{2,1,0:T(8,128)S(1)} %get-tuple-element.20.trig_ref, f32[3,1152,128]{2,1,0:T(8,128)S(1)} %get-tuple-element.21.refs_0_), custom_call_target="tpu_custom_call" | custom-call | tf_op jit(solution)/shard_map/late_edges/pallas_call | solution.py:406
  7.3 1.9 %collective-permute-start = (f32[1,576,128]{2,1,0:T(8,128)S(1)}, f32[1,576,128]{2,1,0:T(8,128)S(1)}, u32[]{:S(2)}, u32[]{:S(2)}) collective-permute-start(f32[1,576,128]{2,1,0:T(8,128)S(1)} %get-tuple-element.22), channel_id=1, source_target_pairs={{1,2},{3,4},{5,6},{7,8},{9,10},{11,12},{13,14},{2,1},{4,3},{6,5},{... | collective-permute-start | bytes 884744 | tf_op jit(solution)/shard_map/ppermute | solution.py:393
  9.2 0.0 copy-start.1
  9.2 0.0 copy-start.2
  9.3 0.1 collective-permute-start.1
  9.3 0.0 copy-start
  9.3 2.4 %local_rows.2.local_ref = f32[3,1152,128]{2,1,0:T(8,128)S(1)} custom-call(s32[3,128]{1,0:T(4,128)S(1)} %get-tuple-element.19.sea_ref, f32[3,72,128]{2,1,0:T(8,128)S(1)} %get-tuple-element.20.trig_ref, f32[3,1152,128]{2,1,0:T(8,128)S(1)} %get-tuple-element.21.refs_0_), custom_call_target="tpu_custom_call" | custom-call | flops 30000001024 | tf_op jit(solution)/shard_map/local_rows/pallas_call | solution.py:406
  11.7 11.0 %collective-permute-done.2.cross_ref = f32[2,576,128]{2,1,0:T(8,128)S(1)} collective-permute-done((f32[2,576,128]{2,1,0:T(8,128)S(1)}, f32[2,576,128]{2,1,0:T(8,128)S(1)}, u32[]{:S(2)}, u32[]{:S(2)}) %collective-permute-start.2) | collective-permute-done | bytes 589856 | tf_op jit(solution)/shard_map/ppermute | solution.py:393
  22.7 0.0 collective-permute-done.1.inner_ref.inner_in
  22.7 0.0 copy-done.1
  22.7 0.0 copy-done.2
  22.7 0.0 copy-done
  22.7 3.7 %middle_rows.2 = (f32[1,1152,128]{2,1,0:T(8,128)S(1)}, f32[2,1152,128]{2,1,0:T(8,128)S(1)}) custom-call(s32[1]{0:T(128)} %bitcast.odd_ref, s32[3,128]{1,0:T(4,128)S(1)} %get-tuple-element.19.sea_ref, s32[3,128]{1,0:T(4,128)S(1)} %copy-done.1, f32[3,128]{1,0:T(4,128)S(1)} %copy-done.2, f32[3,72,128]{2,1,0:T(8,128)S(1)} %get-tuple-element.20.trig_ref, ...), custom_call_target="tpu_custom_call" | custom-call | tf_op jit(solution)/shard_map/middle_rows/pallas_call | solution.py:406
  26.4 0.0 collective-permute-done.cross_in
  26.4 3.7 %edge_rows.2 = (f32[2,1152,128]{2,1,0:T(8,128)S(1)}, f32[2,576,128]{2,1,0:T(8,128)S(1)}) custom-call(s32[1]{0:T(128)} %bitcast.odd_ref, s32[3,128]{1,0:T(4,128)S(1)} %get-tuple-element.19.sea_ref, s32[3,128]{1,0:T(4,128)S(1)} %copy-done.1, f32[3,128]{1,0:T(4,128)S(1)} %copy-done.2, f32[3,72,128]{2,1,0:T(8,128)S(1)} %get-tuple-element.20.trig_ref, ...), custom_call_target="tpu_custom_call" | custom-call | tf_op jit(solution)/shard_map/edge_rows/pallas_call | solution.py:406
  30.1 4.4 %collective-permute-start.5 = (f32[2,576,128]{2,1,0:T(8,128)S(1)}, f32[2,576,128]{2,1,0:T(8,128)S(1)}, u32[]{:S(2)}, u32[]{:S(2)}) collective-permute-start(f32[2,576,128]{2,1,0:T(8,128)S(1)} %get-tuple-element.30), channel_id=1, source_target_pairs={{1,2},{3,4},{5,6},{7,8},{9,10},{11,12},{13,14},{2,1},{4,3},{6,5},{... | collective-permute-start | bytes 1769480 | tf_op jit(solution)/shard_map/ppermute | solution.py:393
  34.5 0.9 %late_edges.3 = (f32[1,576,128]{2,1,0:T(8,128)S(1)}, f32[3,576,128]{2,1,0:T(8,128)S(1)}) custom-call(s32[1]{0:T(128)} %bitcast.odd_ref, s32[3,128]{1,0:T(4,128)S(1)} %get-tuple-element.19.sea_ref, f32[3,72,128]{2,1,0:T(8,128)S(1)} %get-tuple-element.20.trig_ref, f32[2,1152,128]{2,1,0:T(8,128)S(1)} %get-tuple-element.27.refs_0_, ...), custom_call_target="tpu_custom_call" | custom-call | tf_op jit(solution)/shard_map/late_edges/pallas_call | solution.py:406
  35.4 1.9 %collective-permute-start.3 = (f32[1,576,128]{2,1,0:T(8,128)S(1)}, f32[1,576,128]{2,1,0:T(8,128)S(1)}, u32[]{:S(2)}, u32[]{:S(2)}) collective-permute-start(f32[1,576,128]{2,1,0:T(8,128)S(1)} %get-tuple-element.28), channel_id=1, source_target_pairs={{1,2},{3,4},{5,6},{7,8},{9,10},{11,12},{13,14},{2,1},{4,3},{6,5},{... | collective-permute-start | bytes 884744 | tf_op jit(solution)/shard_map/ppermute | solution.py:393
  37.3 0.1 collective-permute-start.4
  37.4 2.4 %local_rows.3.local_ref = f32[3,1152,128]{2,1,0:T(8,128)S(1)} custom-call(s32[3,128]{1,0:T(4,128)S(1)} %get-tuple-element.19.sea_ref, f32[3,72,128]{2,1,0:T(8,128)S(1)} %get-tuple-element.20.trig_ref, f32[2,1152,128]{2,1,0:T(8,128)S(1)} %get-tuple-element.27.refs_0_, f32[1,1152,128]{2,1,0:T(8,128)S(1)} %get-tuple-element.26.middle_ref.refs_1_), custom_call_target="tpu_custom_call" | custom-call | flops 30000001024 | tf_op jit(solution)/shard_map/local_rows/pallas_call | solution.py:406
  39.8 3.4 %collective-permute-done.5.cross_ref = f32[2,576,128]{2,1,0:T(8,128)S(1)} collective-permute-done((f32[2,576,128]{2,1,0:T(8,128)S(1)}, f32[2,576,128]{2,1,0:T(8,128)S(1)}, u32[]{:S(2)}, u32[]{:S(2)}) %collective-permute-start.5) | collective-permute-done | bytes 589856 | tf_op jit(solution)/shard_map/ppermute | solution.py:393
  43.2 0.0 collective-permute-done.4.inner_ref.inner_in
  43.2 3.6 %middle_rows.3 = (f32[1,1152,128]{2,1,0:T(8,128)S(1)}, f32[2,1152,128]{2,1,0:T(8,128)S(1)}) custom-call(s32[1]{0:T(128)} %bitcast.odd_ref, s32[3,128]{1,0:T(4,128)S(1)} %get-tuple-element.19.sea_ref, s32[3,128]{1,0:T(4,128)S(1)} %copy-done.1, f32[3,128]{1,0:T(4,128)S(1)} %copy-done.2, f32[3,72,128]{2,1,0:T(8,128)S(1)} %get-tuple-element.20.trig_ref, ...), custom_call_target="tpu_custom_call" | custom-call | tf_op jit(solution)/shard_map/middle_rows/pallas_call | solution.py:406
  46.8 0.0 collective-permute-done.3.cross_in
  46.8 4.0 %edge_rows.3 = f32[3,1152,128]{2,1,0:T(8,128)} custom-call(s32[1]{0:T(128)} %bitcast.odd_ref, s32[3,128]{1,0:T(4,128)S(1)} %get-tuple-element.19.sea_ref, s32[3,128]{1,0:T(4,128)S(1)} %copy-done.1, f32[3,128]{1,0:T(4,128)S(1)} %copy-done.2, f32[3,72,128]{2,1,0:T(8,128)S(1)} %get-tuple-element.20.trig_ref, bf16[1152,1152]{1,0:T(8,128)(2,1)S(1)} %copy-done, ...), custom_call_target="tpu_custom_call" | custom-call | tf_op jit(solution)/shard_map/edge_rows/pallas_call | solution.py:406
Async XLA Ops:
  1.9 20.8 %collective-permute-start.2 = (f32[2,576,128]{2,1,0:T(8,128)S(1)}, f32[2,576,128]{2,1,0:T(8,128)S(1)}, u32[]{:S(2)}, u32[]{:S(2)}) collective-permute-start(f32[2,576,128]{2,1,0:T(8,128)S(1)} %get-tuple-element.24), channel_id=1, source_target_pairs={{1,2},{3,4},{5,6},{7,8},{9,10},{11,12},{13,14},{2,1},{4,3},{6,5},{... | collective-permute-start | bytes 1769480 | tf_op jit(solution)/shard_map/ppermute | solution.py:393
  7.3 19.1 %collective-permute-start = (f32[1,576,128]{2,1,0:T(8,128)S(1)}, f32[1,576,128]{2,1,0:T(8,128)S(1)}, u32[]{:S(2)}, u32[]{:S(2)}) collective-permute-start(f32[1,576,128]{2,1,0:T(8,128)S(1)} %get-tuple-element.22), channel_id=1, source_target_pairs={{1,2},{3,4},{5,6},{7,8},{9,10},{11,12},{13,14},{2,1},{4,3},{6,5},{... | collective-permute-start | bytes 884744 | tf_op jit(solution)/shard_map/ppermute | solution.py:393
  9.2 13.5 %copy-start.1 = (s32[3,128]{1,0:T(4,128)S(1)}, s32[3,128]{1,0:T(4,128)}, u32[]{:S(2)}) copy-start(s32[3,128]{1,0:T(4,128)} %ice_ref.7) | copy-start | bytes 4612
  9.2 13.5 %copy-start.2 = (f32[3,128]{1,0:T(4,128)S(1)}, f32[3,128]{1,0:T(4,128)}, u32[]{:S(2)}) copy-start(f32[3,128]{1,0:T(4,128)} %wind_ref.7) | copy-start | bytes 4612
  9.3 13.4 %collective-permute-start.1 = (f32[3,576,128]{2,1,0:T(8,128)S(1)}, f32[3,576,128]{2,1,0:T(8,128)S(1)}, u32[]{:S(2)}, u32[]{:S(2)}) collective-permute-start(f32[3,576,128]{2,1,0:T(8,128)S(1)} %get-tuple-element.23), channel_id=1, source_target_pairs={{0,1},{2,3},{4,5},{6,7},{8,9},{10,11},{12,13},{14,15},{1,0},{3,2},... | collective-permute-start | bytes 2654216 | tf_op jit(solution)/shard_map/ppermute | solution.py:393
  9.3 13.4 %copy-start = (bf16[1152,1152]{1,0:T(8,128)(2,1)S(1)}, bf16[1152,1152]{1,0:T(8,128)(2,1)}, u32[]{:S(2)}) copy-start(bf16[1152,1152]{1,0:T(8,128)(2,1)} %matrix_ref.7) | copy-start | bytes 7962628
  30.1 13.1 %collective-permute-start.5 = (f32[2,576,128]{2,1,0:T(8,128)S(1)}, f32[2,576,128]{2,1,0:T(8,128)S(1)}, u32[]{:S(2)}, u32[]{:S(2)}) collective-permute-start(f32[2,576,128]{2,1,0:T(8,128)S(1)} %get-tuple-element.30), channel_id=1, source_target_pairs={{1,2},{3,4},{5,6},{7,8},{9,10},{11,12},{13,14},{2,1},{4,3},{6,5},{... | collective-permute-start | bytes 1769480 | tf_op jit(solution)/shard_map/ppermute | solution.py:393
  35.4 11.4 %collective-permute-start.3 = (f32[1,576,128]{2,1,0:T(8,128)S(1)}, f32[1,576,128]{2,1,0:T(8,128)S(1)}, u32[]{:S(2)}, u32[]{:S(2)}) collective-permute-start(f32[1,576,128]{2,1,0:T(8,128)S(1)} %get-tuple-element.28), channel_id=1, source_target_pairs={{1,2},{3,4},{5,6},{7,8},{9,10},{11,12},{13,14},{2,1},{4,3},{6,5},{... | collective-permute-start | bytes 884744 | tf_op jit(solution)/shard_map/ppermute | solution.py:393
  37.3 5.9 %collective-permute-start.4 = (f32[3,576,128]{2,1,0:T(8,128)S(1)}, f32[3,576,128]{2,1,0:T(8,128)S(1)}, u32[]{:S(2)}, u32[]{:S(2)}) collective-permute-start(f32[3,576,128]{2,1,0:T(8,128)S(1)} %get-tuple-element.29), channel_id=1, source_target_pairs={{0,1},{2,3},{4,5},{6,7},{8,9},{10,11},{12,13},{14,15},{1,0},{3,2},... | collective-permute-start | bytes 2654216 | tf_op jit(solution)/shard_map/ppermute | solution.py:393

commit v6 on v5

v6 whole, which is shorter than its diff:
```python
import functools

import jax
import jax.numpy as jnp
import numpy as np
from jax import lax
from jax.experimental import pallas as pl
from jax.experimental.pallas import tpu as pltpu
from jax.sharding import PartitionSpec as P

NDIR = 36
NFREQ = 32
K = 1152
STEPS = 2
SUBSTEPS = 3
SRC_SUB = 3

source_rate = 0.5
damping = 0.5

SUB = 8
QUADRANTS = 4
ARC = NDIR // QUADRANTS
ARC_ROWS = SUB * ARC
BLOCK = QUADRANTS * ARC_ROWS
BLOCKS = K // BLOCK
HALF = BLOCK // 2
CHUNKS = 4
EAST = (True, False, False, True)
INWARD = (True, True, False, False)
NEAR = SUBSTEPS - 1


def source_row(row):
    quadrant, rest = divmod(row, ARC_ROWS)
    frequency, direction = divmod(rest, ARC)
    return frequency * NDIR + quadrant * ARC + direction


ORDER = [source_row(row) for row in range(BLOCK)]
INVERSE = [ORDER.index(row) for row in range(BLOCK)]


def reorder(read, order, tile, iota):
    pieces = {}
    for to, row in enumerate(order[tile * SUB:(tile + 1) * SUB]):
        pieces.setdefault((row // SUB, (to - row) % SUB), []).append(to)
    out = None
    for (index, shift), rows in pieces.items():
        value = read(index)
        if shift:
            value = pltpu.roll(value, shift, 0)
        out = value if out is None else jnp.where((iota >= rows[0]) & (iota <= rows[-1]), value, out)
    return out


def pattern():
    row = np.arange(ARC_ROWS)
    theta = 2.0 * np.pi * (row % ARC + 0.5) / NDIR
    slower = 0.6 * 0.65 / (NFREQ - 1) * (row // ARC)
    table = np.stack([np.cos(theta), np.sin(theta), slower]).astype(np.float32)
    return jnp.asarray(np.ascontiguousarray(np.broadcast_to(table[:, :, None], (3, ARC_ROWS, 128))))


def sublanes(width):
    return lax.broadcasted_iota(jnp.int32, (SUB, width), 0)


def counted(odd, i, count):
    return odd * (count - 1) + (1 - 2 * odd) * i


def tile_at(odd, block, index):
    q, i = divmod(index, ARC)
    return pl.ds(pl.multiple_of(block * BLOCK + counted(odd, q, QUADRANTS) * ARC_ROWS + i * SUB, SUB), SUB)


def quadrant_at(block, q):
    return pl.ds(block * BLOCK + q * ARC_ROWS, ARC_ROWS)


def half_at(block, q):
    return pl.ds(block * HALF + (q if INWARD[q] else QUADRANTS - 1 - q) * ARC_ROWS, ARC_ROWS)


def block_coefficients(trig_ref, block):
    frequency = (block * SUB).astype(jnp.float32)
    fastest = 0.6 * (0.35 + (0.65 / (NFREQ - 1)) * ((NFREQ - 1) - frequency))
    cosine, sine, slower = (trig_ref[i].reshape(ARC, SUB, -1) for i in range(3))
    one, other = (fastest - slower) * cosine, (fastest - slower) * sine
    staying = 1.0 - one - other
    return [(staying, one, other) if q % 2 == 0 else (staying, other, one) for q in range(QUADRANTS)]


def get(ref, r, at):
    return ref[r, at, :].reshape(ARC, SUB, -1)


def put(ref, r, at, value):
    ref[r, at, :] = value.reshape(ARC_ROWS, -1)


def beside(q, value):
    last = value.ndim - 1
    return pltpu.roll(value, 1 if EAST[q] else value.shape[last] - 1, last)


def flow(q, rows):
    return list(rows) if INWARD[q] else list(rows)[::-1]


def substep(q, coefficients, rows, seas, whole):
    staying, along, across = coefficients
    out = []
    for i, row in enumerate(rows):
        if i == 0 and not whole:
            continue
        value = staying * row + along * beside(q, row)
        if i:
            value = value + across * rows[i - 1]
        out.append(seas[i] * value)
    return out


def edges(q, coefficients, rows, seas):
    found = [rows[-1]]
    rows, seas = rows[-SUBSTEPS:], seas[-SUBSTEPS:]
    for _ in range(SUBSTEPS - 1):
        rows = substep(q, coefficients, rows, seas, False)
        seas = seas[1:]
        found.append(rows[-1])
    return found


def first_two(q, coefficients, seas, halo):
    staying, along, across = coefficients
    first = seas[0] * (across * halo[0])
    beside_first = beside(q, first)
    second = seas[1] * (across * first)
    beside_second = beside(q, seas[1]) * (across * beside_first)
    first = seas[0] * (staying * first + along * beside_first + across * halo[1])
    after_two = second
    second = seas[1] * (staying * second + along * beside_second + across * first)
    first = seas[0] * (staying * first + along * beside(q, first) + across * halo[2])
    return first, second, after_two


def reader(row_refs):
    if len(row_refs) == 1:
        whole, = row_refs
        return whole.shape, lambda r, at: get(whole, r, at)
    near, far = row_refs
    shape = (NEAR + far.shape[0],) + tuple(far.shape[1:])
    return shape, lambda r, at: get(near, r, at) if r < NEAR else get(far, r - NEAR, at)


def spread_all(ref, count):
    return [jnp.broadcast_to(ref[r:r + 1, :].astype(jnp.float32), (SUB, ref.shape[1])) for r in range(count)]


def put_in_order(odd, block, read, out_ref, rows, iota):
    for r in rows:
        for t in range(BLOCK // SUB):
            tile = reorder(lambda index: read(r, pl.ds(block * BLOCK + index * SUB, SUB)), ORDER, t, iota)
            out_ref[r, tile_at(odd, block, t), :] = tile


def first_message(block, near_ref, cross_ref):
    for q in range(QUADRANTS):
        if not INWARD[q]:
            cross_ref[0, half_at(block, q), :] = near_ref[0, quadrant_at(block, q), :]


def first_kernel(odd_ref, f_hbm, sea_hbm, trig_hbm, f_ref, sea_ref, trig_ref, cross_ref, f_raw, sea_raw, trig_raw, sem, block_sem):
    count, _, width = f_ref.shape
    odd = odd_ref[0]

    def block_copy(block):
        at = pl.ds(pl.multiple_of(block * BLOCK, BLOCK), BLOCK)
        return pltpu.make_async_copy(f_hbm.at[:, at, :], f_raw.at[:, at, :], block_sem.at[block])

    small = [pltpu.make_async_copy(sea_hbm, sea_raw, sem.at[0]), pltpu.make_async_copy(trig_hbm, trig_raw, sem.at[1])]
    for block in range(BLOCKS):
        block_copy(block).start()
    for copy in small:
        copy.start()
    iota = sublanes(width)

    def body(block, carry):
        block_copy(block).wait()
        put_in_order(odd, block, lambda r, at: f_raw[counted(odd, r, count), at, :], f_ref, range(count), iota)
        first_message(block, f_ref, cross_ref)
        return carry

    lax.fori_loop(0, BLOCKS, body, 0)
    for copy in small:
        copy.wait()
    for r in range(count):
        sea_ref[r:r + 1, :] = sea_raw[pl.ds(counted(odd, r, count), 1), :]
    for i in range(2):
        trig_ref[i] = trig_raw[counted(odd, i, 2)]
    trig_ref[2] = trig_raw[2]


def late_kernel(sea_ref, trig_ref, *refs):
    cross_ref, inner_ref = refs[-2:]
    (count, _, _), row = reader(refs[:-2])
    seas = spread_all(sea_ref, count)

    def body(block, carry):
        for q, coefficients in enumerate(block_coefficients(trig_ref, block)):
            rows = flow(q, [row(r, quadrant_at(block, q)) for r in range(count)])
            found = edges(q, coefficients, rows, flow(q, seas))
            if INWARD[q]:
                for j in range(SUBSTEPS):
                    put(inner_ref, j, half_at(block, q), found[j])
            else:
                for j in range(1, SUBSTEPS):
                    put(cross_ref, j - 1, half_at(block, q), found[j])
        return carry

    lax.fori_loop(0, BLOCKS, body, 0)


def local_kernel(sea_ref, trig_ref, *refs):
    (count, _, _), row = reader(refs[:-1])
    local_ref = refs[-1]
    seas = spread_all(sea_ref, count)

    def body(block, carry):
        for q, coefficients in enumerate(block_coefficients(trig_ref, block)):
            at = quadrant_at(block, q)
            rows = flow(q, [row(r, at) for r in range(count)])
            for _ in range(SUBSTEPS):
                rows = substep(q, coefficients, rows, flow(q, seas), True)
            for r, value in enumerate(flow(q, rows)):
                put(local_ref, r, at, value)
        return carry

    lax.fori_loop(0, BLOCKS, body, 0)


def lanes(ref, rows):
    return jnp.concatenate([ref[pl.ds(r, 1), :].astype(jnp.float32) for r in rows], axis=1)


def source_steps(odd, rows, sums, sea_ref, ice_ref, wind_ref, matrix_ref, f_acc, b_acc, ready=None):
    comps, count = f_acc.shape[0], sea_ref.shape[0]
    there = [counted(odd, r, count) for r in rows]
    sea, gain, thaw = lanes(sea_ref, rows), source_rate * lanes(wind_ref, there), 1.0 - 0.5 * lanes(ice_ref, there)
    energy = jnp.concatenate([jnp.sum(s, axis=0, keepdims=True) for s in sums], axis=1)
    chunk = comps // CHUNKS
    for s in range(SRC_SUB):
        scale = sea / (1.0 + (damping / comps) * energy)
        energy = jnp.zeros_like(energy)
        if s + 1 == SRC_SUB:
            scale = scale * thaw
        for c in range(CHUNKS):
            at = pl.ds(c * chunk, chunk)
            growth = jnp.dot(matrix_ref[at, :], b_acc[s % 2], preferred_element_type=jnp.float32)
            value = (f_acc[at, :] + gain * growth) * scale
            f_acc[at, :] = value
            if s + 1 < SRC_SUB:
                b_acc[(s + 1) % 2, at, :] = value.astype(jnp.bfloat16)
                energy = energy + jnp.sum(value * value, axis=0, keepdims=True)
            elif ready is not None:
                ready(c, at)


def hold(odd, block, column, moved, f_acc, b_acc, iota, total):
    width = iota.shape[1]
    columns = slice(column * width, (column + 1) * width)
    for t in range(0, BLOCK // SUB, 2):
        pair = [reorder(lambda index: moved[column, tile_at(odd, block, index), :], INVERSE, t + k, iota) for k in range(2)]
        both = jnp.concatenate(pair, axis=0)
        at = pl.ds(block * BLOCK + t * SUB, 2 * SUB)
        f_acc[at, columns] = both
        b_acc[0, at, columns] = both.astype(jnp.bfloat16)
        total = total + pair[0] * pair[0] + pair[1] * pair[1]
    return total


def far_kernel(last, odd_ref, sea_ref, ice_ref, wind_ref, trig_ref, matrix_ref, cross_ref, inner_ref, local_ref,
               far_ref, near_ref, f_acc, b_acc, moved):
    count, _, width = local_ref.shape
    iota = sublanes(width)
    odd = odd_ref[0]
    seas = spread_all(sea_ref, count)
    rows = range(NEAR, count)

    def advance(block, sums):
        for q, coefficients in enumerate(block_coefficients(trig_ref, block)):
            at = quadrant_at(block, q)
            across = coefficients[2]
            if INWARD[q]:
                value = get(cross_ref, 0, half_at(block, q))
                for r in range(SUBSTEPS):
                    value = seas[r] * (across * value)
                for r in rows:
                    put(moved, r - NEAR, at, get(local_ref, r, at) + value if r == NEAR else get(local_ref, r, at))
            else:
                halo = [get(inner_ref, j, half_at(block, q)) for j in range(SUBSTEPS)]
                first, second, after_two = first_two(q, coefficients, flow(q, seas), halo)
                third = seas[count - 3] * (across * after_two)
                for r, value in enumerate([None] * (count - 3) + [third, second, first]):
                    value = get(local_ref, r, at) if value is None else get(local_ref, r, at) + value
                    if r < NEAR:
                        put(near_ref, r, half_at(block, q), value)
                    else:
                        put(moved, r - NEAR, at, value)
        return tuple(hold(odd, block, i, moved, f_acc, b_acc, iota, total) for i, total in enumerate(sums))

    zero = jnp.zeros((SUB, width), jnp.float32)
    sums = lax.fori_loop(0, BLOCKS, advance, (zero,) * len(rows))
    source_steps(odd, rows, sums, sea_ref, ice_ref, wind_ref, matrix_ref, f_acc, b_acc)
    if last:
        for i in range(len(rows)):
            far_ref[i] = f_acc[:, i * width:(i + 1) * width]
        return

    def finish(block, carry):
        put_in_order(odd, block, lambda r, at: f_acc[at, r * width:(r + 1) * width], far_ref, range(len(rows)), iota)
        return carry

    lax.fori_loop(0, BLOCKS, finish, 0)


def near_kernel(last, odd_ref, sea_ref, ice_ref, wind_ref, trig_ref, matrix_ref, cross_in, late_in, local_ref, part_ref, far_ref, *refs):
    if last:
        out_ref, f_acc, b_acc, moved, sem = refs
    else:
        out_ref, cross_ref, f_acc, b_acc, moved = refs
    count, _, width = local_ref.shape
    iota = sublanes(width)
    odd = odd_ref[0]
    seas = spread_all(sea_ref, count)
    if last:
        copies = [pltpu.make_async_copy(far_ref.at[i], out_ref.at[counted(odd, NEAR + i, count)], sem.at[NEAR * CHUNKS + i])
                  for i in range(count - NEAR)]
        for copy in copies:
            copy.start()

    def advance(block, sums):
        for q, coefficients in enumerate(block_coefficients(trig_ref, block)):
            at, half = quadrant_at(block, q), half_at(block, q)
            if INWARD[q]:
                halo = [get(cross_in, 0, half)] + [get(late_in, j, half) for j in range(SUBSTEPS - 1)]
                for r, value in enumerate(first_two(q, coefficients, seas, halo)[:NEAR]):
                    put(moved, r, at, get(local_ref, r, at) + value)
            else:
                for r in range(NEAR):
                    put(moved, r, at, get(part_ref, r, half))
        return tuple(hold(odd, block, i, moved, f_acc, b_acc, iota, total) for i, total in enumerate(sums))

    zero = jnp.zeros((SUB, width), jnp.float32)
    sums = lax.fori_loop(0, BLOCKS, advance, (zero,) * NEAR)
    if last:
        def ready(c, at):
            for r in range(NEAR):
                copy = pltpu.make_async_copy(f_acc.at[at, pl.ds(r * width, width)], out_ref.at[counted(odd, r, count), at, :],
                                             sem.at[NEAR * c + r])
                copy.start()
                copies.append(copy)

        source_steps(odd, range(NEAR), sums, sea_ref, ice_ref, wind_ref, matrix_ref, f_acc, b_acc, ready)
        for copy in copies:
            copy.wait()
        return
    source_steps(odd, range(NEAR), sums, sea_ref, ice_ref, wind_ref, matrix_ref, f_acc, b_acc)

    def finish(block, carry):
        put_in_order(odd, block, lambda r, at: f_acc[at, r * width:(r + 1) * width], out_ref, range(NEAR), iota)
        first_message(block, out_ref, cross_ref)
        return carry

    lax.fori_loop(0, BLOCKS, finish, 0)


def on_device(spectrum, sea_mask, ice_mask, wind, source_matrix):
    size = lax.axis_size("comp")
    comps, count, width = spectrum.shape
    assert comps == K and count >= SUBSTEPS and size % 2 == 0
    odd = (lax.axis_index("comp") % 2).astype(jnp.int32).reshape(1)
    f = jnp.transpose(spectrum, (1, 0, 2))
    trig = pattern()
    outer_pairs = [(i, i + 1) for i in range(1, size - 1, 2)]
    inner_pairs = [(i, i + 1) for i in range(0, size, 2)]

    def swap(value, pairs):
        return lax.ppermute(value, "comp", pairs + [(j, i) for i, j in pairs])

    vmem = pl.BlockSpec(memory_space=pltpu.VMEM)
    hbm = pl.BlockSpec(memory_space=pltpu.HBM)
    dma = pltpu.SemaphoreType.DMA

    def call(kernel, name, args, outs, scratch_rows=0, scratch=(), in_space=vmem, out_space=vmem, scalar=True, cost=0):
        scratch = list(scratch)
        if scratch_rows:
            scratch = [pltpu.VMEM((K, scratch_rows * width), jnp.float32),
                       pltpu.VMEM((2, K, scratch_rows * width), jnp.bfloat16),
                       pltpu.VMEM((scratch_rows, K, width), jnp.float32)] + scratch
        outs = [out if hasattr(out, "dtype") else jax.ShapeDtypeStruct(out, jnp.float32) for out in outs]
        return pl.pallas_call(
            kernel, out_shape=outs, name=name,
            in_specs=[pl.BlockSpec(memory_space=pltpu.SMEM)] * scalar + [in_space] * len(args),
            out_specs=[out_space] * len(outs), scratch_shapes=scratch,
            cost_estimate=pl.CostEstimate(flops=cost, bytes_accessed=0, transcendentals=0) if cost else None,
            compiler_params=pltpu.CompilerParams(vmem_limit_bytes=24 * 1024 * 1024),
        )(*((odd,) if scalar else ()), *args)

    def half(number):
        return (number, K // 2, width)

    whole = jax.ShapeDtypeStruct((count, K, width), jnp.float32)
    operands = [pltpu.with_memory_space_constraint(x, pltpu.HBM) for x in (f, sea_mask, trig)]
    f, sea, trig, cross = call(
        first_kernel, "first_edges", operands, [whole, sea_mask, trig, half(1)],
        scratch=[pltpu.VMEM(x.shape, x.dtype) for x in (f, sea_mask, trig)] + [dma((2,)), dma((BLOCKS,))], in_space=hbm)
    rows = (f,)
    masks = (sea, ice_mask, wind, trig, source_matrix)
    for step in range(STEPS):
        last = step == STEPS - 1
        cross = swap(cross, outer_pairs)
        late, inner = call(late_kernel, "late_edges", (sea, trig) + rows, [half(SUBSTEPS - 1), half(SUBSTEPS)], scalar=False)
        late = swap(late, outer_pairs)
        inner = swap(inner, inner_pairs)
        local, = call(local_kernel, "local_rows", (sea, trig) + rows, [whole], scalar=False, cost=30000000000)
        far, part = call(functools.partial(far_kernel, last), "far_rows", masks + (cross, inner, local),
                         [(count - NEAR, K, width), half(NEAR)], count - NEAR)
        outs = [whole] if last else [(NEAR, K, width), half(1)]
        result = call(functools.partial(near_kernel, last), "near_rows", masks + (cross, late, local, part, far), outs, NEAR,
                      scratch=[dma((NEAR * CHUNKS + count - NEAR,))] if last else (), out_space=hbm if last else vmem)
        if last:
            return jnp.transpose(result[0], (1, 0, 2))
        rows, cross = (result[0], far), result[1]


def solution(mesh):
    return jax.shard_map(
        on_device,
        mesh=mesh,
        in_specs=(
            P(None, ("grp", "comp"), None),
            P(("grp", "comp"), None),
            P(("grp", "comp"), None),
            P(("grp", "comp"), None),
            P(),
        ),
        out_specs=P(None, ("grp", "comp"), None),
        check_vma=False,
    )
```

time: 51.1 us -> 52.6 us (1.029)
  waiting for transfers between devices: 14.4 us -> 15.5 us
    ppermute x6, waiting for transfers between devices: 14.4 us -> 15.5 us  [swap(): return lax.ppermute(value, 'comp', pairs + [(j, i) for i, j in pairs])]
  transfers between devices with their start and end apart: 6 -> 6, of which waited for: 2 -> 4; matrix products, arithmetic and copies ran while one was open for 0% -> 0% of each run, Pallas kernels for 27% -> 26%
where the time goes in v6:
time: 52.6 us; the launch traced here: 52.4 us
  Pallas kernels  23.8 us (45%)
  waiting for transfers between devices  15.5 us (29%)
  starting transfers between devices  12.9 us (25%)
    pallas_call x9, Pallas kernels, call(): pl.pallas_call(kernel, out_shape=outs, name=name, in_specs=[pl.BlockSpec(...  23.8 us
    ppermute x6, waiting for transfers between devices, swap(): return lax.ppermute(value, 'comp', pairs + [(j, i) for i, j in pairs])  15.5 us
    ppermute x6, starting transfers between devices, swap(): return lax.ppermute(value, 'comp', pairs + [(j, i) for i, j in pairs])  12.9 us
  transfers between devices with their start and end apart: 6, of which 4 were waited for; matrix products, arithmetic and copies ran while one was open for 0% of the time, Pallas kernels for 26%

profile of v6, /device:TPU:1, one launch (start us, length us, event | category | flops | bytes accessed | tf_op | source)
XLA Modules:
  0.0 52.4 jit_solution(490854332122538780)
XLA Ops:
  0.0 1.6 %first_edges.1 = (f32[3,1152,128]{2,1,0:T(8,128)S(1)}, s32[3,128]{1,0:T(4,128)S(1)}, f32[3,72,128]{2,1,0:T(8,128)S(1)}, f32[1,576,128]{2,1,0:T(8,128)S(1)}) custom-call(s32[1]{0:T(128)} %bitcast.odd_ref, f32[3,1152,128]{2,1,0:T(8,128)} %bitcast.3, s32[3,128]{1,0:T(4,128)} %sea_hbm.1, f32[3,72,128]{2,1,0:T(8,128)} %constant.19.clone.trig_hbm), custom_call_target="tpu_custom_call" | custom-call | tf_op jit(solution)/shard_map/first_edges/pallas_call | solution.py:403
  1.6 4.5 %collective-permute-start = (f32[1,576,128]{2,1,0:T(8,128)S(1)}, f32[1,576,128]{2,1,0:T(8,128)S(1)}, u32[]{:S(2)}, u32[]{:S(2)}) collective-permute-start(f32[1,576,128]{2,1,0:T(8,128)S(1)} %get-tuple-element.21), channel_id=1, source_target_pairs={{1,2},{3,4},{5,6},{7,8},{9,10},{11,12},{13,14},{2,1},{4,3},{6,5},{... | collective-permute-start | bytes 884744 | tf_op jit(solution)/shard_map/ppermute | solution.py:390
  6.1 0.9 %late_edges.2 = (f32[2,576,128]{2,1,0:T(8,128)S(1)}, f32[3,576,128]{2,1,0:T(8,128)S(1)}) custom-call(s32[3,128]{1,0:T(4,128)S(1)} %get-tuple-element.19.sea_ref, f32[3,72,128]{2,1,0:T(8,128)S(1)} %get-tuple-element.20.trig_ref, f32[3,1152,128]{2,1,0:T(8,128)S(1)} %get-tuple-element.22.refs_0_), custom_call_target="tpu_custom_call" | custom-call | tf_op jit(solution)/shard_map/late_edges/pallas_call | solution.py:403
  7.0 1.9 %collective-permute-start.1 = (f32[2,576,128]{2,1,0:T(8,128)S(1)}, f32[2,576,128]{2,1,0:T(8,128)S(1)}, u32[]{:S(2)}, u32[]{:S(2)}) collective-permute-start(f32[2,576,128]{2,1,0:T(8,128)S(1)} %get-tuple-element.23), channel_id=1, source_target_pairs={{1,2},{3,4},{5,6},{7,8},{9,10},{11,12},{13,14},{2,1},{4,3},{6,5},{... | collective-permute-start | bytes 1769480 | tf_op jit(solution)/shard_map/ppermute | solution.py:390
  8.9 0.0 copy-start.1
  8.9 0.0 copy-start.2
  9.0 0.1 collective-permute-start.2
  9.0 0.0 copy-start
  9.0 2.4 %local_rows.2.local_ref = f32[3,1152,128]{2,1,0:T(8,128)S(1)} custom-call(s32[3,128]{1,0:T(4,128)S(1)} %get-tuple-element.19.sea_ref, f32[3,72,128]{2,1,0:T(8,128)S(1)} %get-tuple-element.20.trig_ref, f32[3,1152,128]{2,1,0:T(8,128)S(1)} %get-tuple-element.22.refs_0_), custom_call_target="tpu_custom_call" | custom-call | flops 30000001024 | tf_op jit(solution)/shard_map/local_rows/pallas_call | solution.py:403
  11.4 7.8 %collective-permute-done.cross_ref.cross_in = f32[1,576,128]{2,1,0:T(8,128)S(1)} collective-permute-done((f32[1,576,128]{2,1,0:T(8,128)S(1)}, f32[1,576,128]{2,1,0:T(8,128)S(1)}, u32[]{:S(2)}, u32[]{:S(2)}) %collective-permute-start) | collective-permute-done | bytes 294944 | tf_op jit(solution)/shard_map/ppermute | solution.py:390
  19.2 0.0 collective-permute-done.2.inner_ref
  19.2 0.0 copy-done.1
  19.2 0.0 copy-done.2
  19.2 0.0 copy-done
  19.3 3.6 %far_rows.2 = (f32[1,1152,128]{2,1,0:T(8,128)S(1)}, f32[2,576,128]{2,1,0:T(8,128)S(1)}) custom-call(s32[1]{0:T(128)} %bitcast.odd_ref, s32[3,128]{1,0:T(4,128)S(1)} %get-tuple-element.19.sea_ref, s32[3,128]{1,0:T(4,128)S(1)} %copy-done.1, f32[3,128]{1,0:T(4,128)S(1)} %copy-done.2, f32[3,72,128]{2,1,0:T(8,128)S(1)} %get-tuple-element.20.trig_ref, ...), custom_call_target="tpu_custom_call" | custom-call | tf_op jit(solution)/shard_map/far_rows/pallas_call | solution.py:403
  22.8 2.7 %collective-permute-done.1.late_in = f32[2,576,128]{2,1,0:T(8,128)S(1)} collective-permute-done((f32[2,576,128]{2,1,0:T(8,128)S(1)}, f32[2,576,128]{2,1,0:T(8,128)S(1)}, u32[]{:S(2)}, u32[]{:S(2)}) %collective-permute-start.1) | collective-permute-done | bytes 589856 | tf_op jit(solution)/shard_map/ppermute | solution.py:390
  25.6 4.0 %near_rows.2 = (f32[2,1152,128]{2,1,0:T(8,128)S(1)}, f32[1,576,128]{2,1,0:T(8,128)S(1)}) custom-call(s32[1]{0:T(128)} %bitcast.odd_ref, s32[3,128]{1,0:T(4,128)S(1)} %get-tuple-element.19.sea_ref, s32[3,128]{1,0:T(4,128)S(1)} %copy-done.1, f32[3,128]{1,0:T(4,128)S(1)} %copy-done.2, f32[3,72,128]{2,1,0:T(8,128)S(1)} %get-tuple-element.20.trig_ref, ...), custom_call_target="tpu_custom_call" | custom-call | tf_op jit(solution)/shard_map/near_rows/pallas_call | solution.py:403
  29.5 4.4 %collective-permute-start.3 = (f32[1,576,128]{2,1,0:T(8,128)S(1)}, f32[1,576,128]{2,1,0:T(8,128)S(1)}, u32[]{:S(2)}, u32[]{:S(2)}) collective-permute-start(f32[1,576,128]{2,1,0:T(8,128)S(1)} %get-tuple-element.27), channel_id=1, source_target_pairs={{1,2},{3,4},{5,6},{7,8},{9,10},{11,12},{13,14},{2,1},{4,3},{6,5},{... | collective-permute-start | bytes 884744 | tf_op jit(solution)/shard_map/ppermute | solution.py:390
  33.9 0.9 %late_edges.3 = (f32[2,576,128]{2,1,0:T(8,128)S(1)}, f32[3,576,128]{2,1,0:T(8,128)S(1)}) custom-call(s32[3,128]{1,0:T(4,128)S(1)} %get-tuple-element.19.sea_ref, f32[3,72,128]{2,1,0:T(8,128)S(1)} %get-tuple-element.20.trig_ref, f32[2,1152,128]{2,1,0:T(8,128)S(1)} %get-tuple-element.28.refs_0_, f32[1,1152,128]{2,1,0:T(8,128)S(1)} %get-tuple-element.26.far_ref.refs_1_), custom_call_target="tpu_custom_call" | custom-call | tf_op jit(solution)/shard_map/late_edges/pallas_call | solution.py:403
  34.8 1.9 %collective-permute-start.4 = (f32[2,576,128]{2,1,0:T(8,128)S(1)}, f32[2,576,128]{2,1,0:T(8,128)S(1)}, u32[]{:S(2)}, u32[]{:S(2)}) collective-permute-start(f32[2,576,128]{2,1,0:T(8,128)S(1)} %get-tuple-element.29), channel_id=1, source_target_pairs={{1,2},{3,4},{5,6},{7,8},{9,10},{11,12},{13,14},{2,1},{4,3},{6,5},{... | collective-permute-start | bytes 1769480 | tf_op jit(solution)/shard_map/ppermute | solution.py:390
  36.8 0.1 collective-permute-start.5
  36.8 2.4 %local_rows.3.local_ref = f32[3,1152,128]{2,1,0:T(8,128)S(1)} custom-call(s32[3,128]{1,0:T(4,128)S(1)} %get-tuple-element.19.sea_ref, f32[3,72,128]{2,1,0:T(8,128)S(1)} %get-tuple-element.20.trig_ref, f32[2,1152,128]{2,1,0:T(8,128)S(1)} %get-tuple-element.28.refs_0_, f32[1,1152,128]{2,1,0:T(8,128)S(1)} %get-tuple-element.26.far_ref.refs_1_), custom_call_target="tpu_custom_call" | custom-call | flops 30000001024 | tf_op jit(solution)/shard_map/local_rows/pallas_call | solution.py:403
  39.2 2.1 %collective-permute-done.3.cross_ref.cross_in = f32[1,576,128]{2,1,0:T(8,128)S(1)} collective-permute-done((f32[1,576,128]{2,1,0:T(8,128)S(1)}, f32[1,576,128]{2,1,0:T(8,128)S(1)}, u32[]{:S(2)}, u32[]{:S(2)}) %collective-permute-start.3) | collective-permute-done | bytes 294944 | tf_op jit(solution)/shard_map/ppermute | solution.py:390
  41.4 0.0 collective-permute-done.5.inner_ref
  41.4 3.5 %far_rows.3 = (f32[1,1152,128]{2,1,0:T(8,128)S(1)}, f32[2,576,128]{2,1,0:T(8,128)S(1)}) custom-call(s32[1]{0:T(128)} %bitcast.odd_ref, s32[3,128]{1,0:T(4,128)S(1)} %get-tuple-element.19.sea_ref, s32[3,128]{1,0:T(4,128)S(1)} %copy-done.1, f32[3,128]{1,0:T(4,128)S(1)} %copy-done.2, f32[3,72,128]{2,1,0:T(8,128)S(1)} %get-tuple-element.20.trig_ref, ...), custom_call_target="tpu_custom_call" | custom-call | tf_op jit(solution)/shard_map/far_rows/pallas_call | solution.py:403
  44.9 2.8 %collective-permute-done.4.late_in = f32[2,576,128]{2,1,0:T(8,128)S(1)} collective-permute-done((f32[2,576,128]{2,1,0:T(8,128)S(1)}, f32[2,576,128]{2,1,0:T(8,128)S(1)}, u32[]{:S(2)}, u32[]{:S(2)}) %collective-permute-start.4) | collective-permute-done | bytes 589856 | tf_op jit(solution)/shard_map/ppermute | solution.py:390
  47.7 4.6 %near_rows.3 = f32[3,1152,128]{2,1,0:T(8,128)} custom-call(s32[1]{0:T(128)} %bitcast.odd_ref, s32[3,128]{1,0:T(4,128)S(1)} %get-tuple-element.19.sea_ref, s32[3,128]{1,0:T(4,128)S(1)} %copy-done.1, f32[3,128]{1,0:T(4,128)S(1)} %copy-done.2, f32[3,72,128]{2,1,0:T(8,128)S(1)} %get-tuple-element.20.trig_ref, bf16[1152,1152]{1,0:T(8,128)(2,1)S(1)} %copy-done, ...), custom_call_target="tpu_custom_call" | custom-call | tf_op jit(solution)/shard_map/near_rows/pallas_call | solution.py:403
Async XLA Ops:
  1.6 17.7 %collective-permute-start = (f32[1,576,128]{2,1,0:T(8,128)S(1)}, f32[1,576,128]{2,1,0:T(8,128)S(1)}, u32[]{:S(2)}, u32[]{:S(2)}) collective-permute-start(f32[1,576,128]{2,1,0:T(8,128)S(1)} %get-tuple-element.21), channel_id=1, source_target_pairs={{1,2},{3,4},{5,6},{7,8},{9,10},{11,12},{13,14},{2,1},{4,3},{6,5},{... | collective-permute-start | bytes 884744 | tf_op jit(solution)/shard_map/ppermute | solution.py:390
  7.0 18.6 %collective-permute-start.1 = (f32[2,576,128]{2,1,0:T(8,128)S(1)}, f32[2,576,128]{2,1,0:T(8,128)S(1)}, u32[]{:S(2)}, u32[]{:S(2)}) collective-permute-start(f32[2,576,128]{2,1,0:T(8,128)S(1)} %get-tuple-element.23), channel_id=1, source_target_pairs={{1,2},{3,4},{5,6},{7,8},{9,10},{11,12},{13,14},{2,1},{4,3},{6,5},{... | collective-permute-start | bytes 1769480 | tf_op jit(solution)/shard_map/ppermute | solution.py:390
  8.9 10.3 %copy-start.1 = (s32[3,128]{1,0:T(4,128)S(1)}, s32[3,128]{1,0:T(4,128)}, u32[]{:S(2)}) copy-start(s32[3,128]{1,0:T(4,128)} %ice_ref.7) | copy-start | bytes 4612
  8.9 10.3 %copy-start.2 = (f32[3,128]{1,0:T(4,128)S(1)}, f32[3,128]{1,0:T(4,128)}, u32[]{:S(2)}) copy-start(f32[3,128]{1,0:T(4,128)} %wind_ref.7) | copy-start | bytes 4612
  9.0 10.3 %collective-permute-start.2 = (f32[3,576,128]{2,1,0:T(8,128)S(1)}, f32[3,576,128]{2,1,0:T(8,128)S(1)}, u32[]{:S(2)}, u32[]{:S(2)}) collective-permute-start(f32[3,576,128]{2,1,0:T(8,128)S(1)} %get-tuple-element.24), channel_id=1, source_target_pairs={{0,1},{2,3},{4,5},{6,7},{8,9},{10,11},{12,13},{14,15},{1,0},{3,2},... | collective-permute-start | bytes 2654216 | tf_op jit(solution)/shard_map/ppermute | solution.py:390
  9.0 10.2 %copy-start = (bf16[1152,1152]{1,0:T(8,128)(2,1)S(1)}, bf16[1152,1152]{1,0:T(8,128)(2,1)}, u32[]{:S(2)}) copy-start(bf16[1152,1152]{1,0:T(8,128)(2,1)} %matrix_ref.7) | copy-start | bytes 7962628
  29.5 11.9 %collective-permute-start.3 = (f32[1,576,128]{2,1,0:T(8,128)S(1)}, f32[1,576,128]{2,1,0:T(8,128)S(1)}, u32[]{:S(2)}, u32[]{:S(2)}) collective-permute-start(f32[1,576,128]{2,1,0:T(8,128)S(1)} %get-tuple-element.27), channel_id=1, source_target_pairs={{1,2},{3,4},{5,6},{7,8},{9,10},{11,12},{13,14},{2,1},{4,3},{6,5},{... | collective-permute-start | bytes 884744 | tf_op jit(solution)/shard_map/ppermute | solution.py:390
  34.8 12.9 %collective-permute-start.4 = (f32[2,576,128]{2,1,0:T(8,128)S(1)}, f32[2,576,128]{2,1,0:T(8,128)S(1)}, u32[]{:S(2)}, u32[]{:S(2)}) collective-permute-start(f32[2,576,128]{2,1,0:T(8,128)S(1)} %get-tuple-element.29), channel_id=1, source_target_pairs={{1,2},{3,4},{5,6},{7,8},{9,10},{11,12},{13,14},{2,1},{4,3},{6,5},{... | collective-permute-start | bytes 1769480 | tf_op jit(solution)/shard_map/ppermute | solution.py:390
  36.8 4.6 %collective-permute-start.5 = (f32[3,576,128]{2,1,0:T(8,128)S(1)}, f32[3,576,128]{2,1,0:T(8,128)S(1)}, u32[]{:S(2)}, u32[]{:S(2)}) collective-permute-start(f32[3,576,128]{2,1,0:T(8,128)S(1)} %get-tuple-element.30), channel_id=1, source_target_pairs={{0,1},{2,3},{4,5},{6,7},{8,9},{10,11},{12,13},{14,15},{1,0},{3,2},... | collective-permute-start | bytes 2654216 | tf_op jit(solution)/shard_map/ppermute | solution.py:390

commit v7 on v6

--- a/solution.py
+++ b/solution.py
@@ -132,17 +132,24 @@
     return found
 
 
-def first_two(q, coefficients, seas, halo):
+def from_first(q, coefficients, seas, halo):
     staying, along, across = coefficients
-    first = seas[0] * (across * halo[0])
+    first = seas[0] * (across * halo)
     beside_first = beside(q, first)
     second = seas[1] * (across * first)
     beside_second = beside(q, seas[1]) * (across * beside_first)
-    first = seas[0] * (staying * first + along * beside_first + across * halo[1])
-    after_two = second
+    third = seas[2] * (across * second)
+    first = seas[0] * (staying * first + along * beside_first)
     second = seas[1] * (staying * second + along * beside_second + across * first)
-    first = seas[0] * (staying * first + along * beside(q, first) + across * halo[2])
-    return first, second, after_two
+    first = seas[0] * (staying * first + along * beside(q, first))
+    return first, second, third
+
+
+def from_later(q, coefficients, seas, halo):
+    staying, along, across = coefficients
+    first = seas[0] * (across * halo[0])
+    second = seas[1] * (across * first)
+    return seas[0] * (staying * first + along * beside(q, first) + across * halo[1]), second
 
 
 def reader(row_refs):
@@ -165,31 +172,31 @@
             out_ref[r, tile_at(odd, block, t), :] = tile
 
 
-def first_message(block, near_ref, cross_ref):
-    for q in range(QUADRANTS):
-        if not INWARD[q]:
-            cross_ref[0, half_at(block, q), :] = near_ref[0, quadrant_at(block, q), :]
-
-
-def first_kernel(odd_ref, f_hbm, sea_hbm, trig_hbm, f_ref, sea_ref, trig_ref, cross_ref, f_raw, sea_raw, trig_raw, sem, block_sem):
+def first_kernel(odd_ref, f_hbm, sea_hbm, trig_hbm, f_ref, sea_ref, trig_ref, cross_ref, sea_raw, trig_raw, sem, block_sem):
     count, _, width = f_ref.shape
     odd = odd_ref[0]
 
-    def block_copy(block):
+    def row_copy(block, r):
         at = pl.ds(pl.multiple_of(block * BLOCK, BLOCK), BLOCK)
-        return pltpu.make_async_copy(f_hbm.at[:, at, :], f_raw.at[:, at, :], block_sem.at[block])
+        return pltpu.make_async_copy(f_hbm.at[counted(odd, r, count), at, :], f_ref.at[r, at, :], block_sem.at[r, block])
 
     small = [pltpu.make_async_copy(sea_hbm, sea_raw, sem.at[0]), pltpu.make_async_copy(trig_hbm, trig_raw, sem.at[1])]
-    for block in range(BLOCKS):
-        block_copy(block).start()
+    for r in range(count):
+        for block in range(BLOCKS):
+            row_copy(block, r).start()
     for copy in small:
         copy.start()
     iota = sublanes(width)
 
     def body(block, carry):
-        block_copy(block).wait()
-        put_in_order(odd, block, lambda r, at: f_raw[counted(odd, r, count), at, :], f_ref, range(count), iota)
-        first_message(block, f_ref, cross_ref)
+        row_copy(block, 0).wait()
+        for t in range(BLOCK // SUB):
+            q, i = divmod(t, ARC)
+            read = lambda index: f_ref[0, pl.ds(block * BLOCK + index * SUB, SUB), :]
+            if not INWARD[q]:
+                at = pl.ds(half_at(block, q).start + i * SUB, SUB)
+                there = (QUADRANTS - 1 - q) * ARC + i
+                cross_ref[0, at, :] = jnp.where(odd == 1, reorder(read, ORDER, there, iota), reorder(read, ORDER, t, iota))
         return carry
 
     lax.fori_loop(0, BLOCKS, body, 0)
@@ -200,22 +207,31 @@
     for i in range(2):
         trig_ref[i] = trig_raw[counted(odd, i, 2)]
     trig_ref[2] = trig_raw[2]
-
-
-def late_kernel(sea_ref, trig_ref, *refs):
-    cross_ref, inner_ref = refs[-2:]
-    (count, _, _), row = reader(refs[:-2])
+    for r in range(1, count):
+        for block in range(BLOCKS):
+            row_copy(block, r).wait()
+
+
+def late_kernel(first, odd_ref, sea_ref, trig_ref, *refs):
+    if first:
+        raw_ref, cross_ref, inner_ref, f_ref = refs
+        (count, _, width), row = reader((f_ref,))
+        iota = sublanes(width)
+    else:
+        cross_ref, inner_ref = refs[-2:]
+        (count, _, _), row = reader(refs[:-2])
     seas = spread_all(sea_ref, count)
 
     def body(block, carry):
+        if first:
+            put_in_order(odd_ref[0], block, lambda r, at: raw_ref[r, at, :], f_ref, range(count), iota)
         for q, coefficients in enumerate(block_coefficients(trig_ref, block)):
             rows = flow(q, [row(r, quadrant_at(block, q)) for r in range(count)])
             found = edges(q, coefficients, rows, flow(q, seas))
-            if INWARD[q]:
-                for j in range(SUBSTEPS):
+            for j in range(SUBSTEPS):
+                if INWARD[q]:
                     put(inner_ref, j, half_at(block, q), found[j])
-            else:
-                for j in range(1, SUBSTEPS):
+                elif j:
                     put(cross_ref, j - 1, half_at(block, q), found[j])
         return carry
 
@@ -290,24 +306,21 @@
 
     def advance(block, sums):
         for q, coefficients in enumerate(block_coefficients(trig_ref, block)):
-            at = quadrant_at(block, q)
-            across = coefficients[2]
-            if INWARD[q]:
-                value = get(cross_ref, 0, half_at(block, q))
-                for r in range(SUBSTEPS):
-                    value = seas[r] * (across * value)
-                for r in rows:
-                    put(moved, r - NEAR, at, get(local_ref, r, at) + value if r == NEAR else get(local_ref, r, at))
-            else:
-                halo = [get(inner_ref, j, half_at(block, q)) for j in range(SUBSTEPS)]
-                first, second, after_two = first_two(q, coefficients, flow(q, seas), halo)
-                third = seas[count - 3] * (across * after_two)
-                for r, value in enumerate([None] * (count - 3) + [third, second, first]):
-                    value = get(local_ref, r, at) if value is None else get(local_ref, r, at) + value
-                    if r < NEAR:
-                        put(near_ref, r, half_at(block, q), value)
-                    else:
-                        put(moved, r - NEAR, at, value)
+            at, half = quadrant_at(block, q), half_at(block, q)
+            values = [get(local_ref, r, at) for r in range(count)]
+            halo = cross_ref if INWARD[q] else inner_ref
+            shares = [from_first(q, coefficients, flow(q, seas), get(halo, 0, half))]
+            if not INWARD[q]:
+                shares.append(from_later(q, coefficients, flow(q, seas), [get(halo, j, half) for j in range(1, SUBSTEPS)]))
+            for share in shares:
+                for i, value in enumerate(share):
+                    r = i if INWARD[q] else count - 1 - i
+                    values[r] = values[r] + value
+            for r, value in enumerate(values):
+                if r < NEAR:
+                    put(near_ref, r, at, value)
+                else:
+                    put(moved, r - NEAR, at, value)
         return tuple(hold(odd, block, i, moved, f_acc, b_acc, iota, total) for i, total in enumerate(sums))
 
     zero = jnp.zeros((SUB, width), jnp.float32)
@@ -325,12 +338,12 @@
     lax.fori_loop(0, BLOCKS, finish, 0)
 
 
-def near_kernel(last, odd_ref, sea_ref, ice_ref, wind_ref, trig_ref, matrix_ref, cross_in, late_in, local_ref, part_ref, far_ref, *refs):
+def near_kernel(last, odd_ref, sea_ref, ice_ref, wind_ref, trig_ref, matrix_ref, late_ref, part_ref, far_ref, *refs):
     if last:
         out_ref, f_acc, b_acc, moved, sem = refs
     else:
         out_ref, cross_ref, f_acc, b_acc, moved = refs
-    count, _, width = local_ref.shape
+    count, width = NEAR + far_ref.shape[0], far_ref.shape[2]
     iota = sublanes(width)
     odd = odd_ref[0]
     seas = spread_all(sea_ref, count)
@@ -342,14 +355,13 @@
 
     def advance(block, sums):
         for q, coefficients in enumerate(block_coefficients(trig_ref, block)):
-            at, half = quadrant_at(block, q), half_at(block, q)
+            at = quadrant_at(block, q)
+            values = [get(part_ref, r, at) for r in range(NEAR)]
             if INWARD[q]:
-                halo = [get(cross_in, 0, half)] + [get(late_in, j, half) for j in range(SUBSTEPS - 1)]
-                for r, value in enumerate(first_two(q, coefficients, seas, halo)[:NEAR]):
-                    put(moved, r, at, get(local_ref, r, at) + value)
-            else:
-                for r in range(NEAR):
-                    put(moved, r, at, get(part_ref, r, half))
+                halo = [get(late_ref, j, half_at(block, q)) for j in range(SUBSTEPS - 1)]
+                values = [v + share for v, share in zip(values, from_later(q, coefficients, seas, halo))]
+            for r, value in enumerate(values):
+                put(moved, r, at, value)
         return tuple(hold(odd, block, i, moved, f_acc, b_acc, iota, total) for i, total in enumerate(sums))
 
     zero = jnp.zeros((SUB, width), jnp.float32)
@@ -370,7 +382,9 @@
 
     def finish(block, carry):
         put_in_order(odd, block, lambda r, at: f_acc[at, r * width:(r + 1) * width], out_ref, range(NEAR), iota)
-        first_message(block, out_ref, cross_ref)
+        for q in range(QUADRANTS):
+            if not INWARD[q]:
+                cross_ref[0, half_at(block, q), :] = out_ref[0, quadrant_at(block, q), :]
         return carry
 
     lax.fori_loop(0, BLOCKS, finish, 0)
@@ -414,21 +428,23 @@
     whole = jax.ShapeDtypeStruct((count, K, width), jnp.float32)
     operands = [pltpu.with_memory_space_constraint(x, pltpu.HBM) for x in (f, sea_mask, trig)]
     f, sea, trig, cross = call(
-        first_kernel, "first_edges", operands, [whole, sea_mask, trig, half(1)],
-        scratch=[pltpu.VMEM(x.shape, x.dtype) for x in (f, sea_mask, trig)] + [dma((2,)), dma((BLOCKS,))], in_space=hbm)
+        first_kernel, "first_edge", operands, [whole, sea_mask, trig, half(1)],
+        scratch=[pltpu.VMEM(x.shape, x.dtype) for x in (sea_mask, trig)] + [dma((2,)), dma((count, BLOCKS))], in_space=hbm)
     rows = (f,)
     masks = (sea, ice_mask, wind, trig, source_matrix)
     for step in range(STEPS):
-        last = step == STEPS - 1
+        first, last = step == 0, step == STEPS - 1
         cross = swap(cross, outer_pairs)
-        late, inner = call(late_kernel, "late_edges", (sea, trig) + rows, [half(SUBSTEPS - 1), half(SUBSTEPS)], scalar=False)
+        late, inner, *ordered = call(functools.partial(late_kernel, first), "late_edges", (sea, trig) + rows,
+                                     [half(SUBSTEPS - 1), half(SUBSTEPS)] + [whole] * first)
+        rows = tuple(ordered) or rows
         late = swap(late, outer_pairs)
         inner = swap(inner, inner_pairs)
         local, = call(local_kernel, "local_rows", (sea, trig) + rows, [whole], scalar=False, cost=30000000000)
         far, part = call(functools.partial(far_kernel, last), "far_rows", masks + (cross, inner, local),
-                         [(count - NEAR, K, width), half(NEAR)], count - NEAR)
+                         [(count - NEAR, K, width), (NEAR, K, width)], count - NEAR)
         outs = [whole] if last else [(NEAR, K, width), half(1)]
-        result = call(functools.partial(near_kernel, last), "near_rows", masks + (cross, late, local, part, far), outs, NEAR,
+        result = call(functools.partial(near_kernel, last), "near_rows", masks + (late, part, far), outs, NEAR,
                       scratch=[dma((NEAR * CHUNKS + count - NEAR,))] if last else (), out_space=hbm if last else vmem)
         if last:
             return jnp.transpose(result[0], (1, 0, 2))

time: 52.6 us -> 52.2 us (level)
  waiting for transfers between devices: 15.5 us -> 14.7 us
    ppermute x6, waiting for transfers between devices: 15.5 us -> 14.7 us  [swap(): return lax.ppermute(value, 'comp', pairs + [(j, i) for i, j in pairs])]
  transfers between devices with their start and end apart: 6 -> 6, of which waited for: 4 -> 4; matrix products, arithmetic and copies ran while one was open for 0% -> 0% of each run, Pallas kernels for 26% -> 28%
where the time goes in v7:
time: 52.2 us; the launch traced here: 52 us
  Pallas kernels  24.2 us (46%)
  waiting for transfers between devices  14.7 us (28%)
  starting transfers between devices  12.9 us (25%)
    pallas_call x9, Pallas kernels, call(): pl.pallas_call(kernel, out_shape=outs, name=name, in_specs=[pl.BlockSpec(...  24.2 us
    ppermute x6, waiting for transfers between devices, swap(): return lax.ppermute(value, 'comp', pairs + [(j, i) for i, j in pairs])  14.7 us
    ppermute x6, starting transfers between devices, swap(): return lax.ppermute(value, 'comp', pairs + [(j, i) for i, j in pairs])  12.9 us
  transfers between devices with their start and end apart: 6, of which 4 were waited for; matrix products, arithmetic and copies ran while one was open for 0% of the time, Pallas kernels for 28%

profile of v7, /device:TPU:1, one launch (start us, length us, event | category | flops | bytes accessed | tf_op | source)
XLA Modules:
  0.0 52.0 jit_solution(8897955174893194858)
XLA Ops:
  0.0 1.7 %first_edge.1 = (f32[3,1152,128]{2,1,0:T(8,128)S(1)}, s32[3,128]{1,0:T(4,128)S(1)}, f32[3,72,128]{2,1,0:T(8,128)S(1)}, f32[1,576,128]{2,1,0:T(8,128)S(1)}) custom-call(s32[1]{0:T(128)} %bitcast.odd_ref, f32[3,1152,128]{2,1,0:T(8,128)} %bitcast.3, s32[3,128]{1,0:T(4,128)} %sea_hbm.1, f32[3,72,128]{2,1,0:T(8,128)} %constant.19.clone.trig_hbm), custom_call_target="tpu_custom_call" | custom-call | tf_op jit(solution)/shard_map/first_edge/pallas_call | solution.py:417
  1.7 4.5 %collective-permute-start.1 = (f32[1,576,128]{2,1,0:T(8,128)S(1)}, f32[1,576,128]{2,1,0:T(8,128)S(1)}, u32[]{:S(2)}, u32[]{:S(2)}) collective-permute-start(f32[1,576,128]{2,1,0:T(8,128)S(1)} %get-tuple-element.24), channel_id=1, source_target_pairs={{1,2},{3,4},{5,6},{7,8},{9,10},{11,12},{13,14},{2,1},{4,3},{6,5},{... | collective-permute-start | bytes 884744 | tf_op jit(solution)/shard_map/ppermute | solution.py:404
  6.2 1.1 %late_edges.2 = (f32[2,576,128]{2,1,0:T(8,128)S(1)}, f32[3,576,128]{2,1,0:T(8,128)S(1)}, f32[3,1152,128]{2,1,0:T(8,128)S(1)}) custom-call(s32[1]{0:T(128)} %bitcast.odd_ref, s32[3,128]{1,0:T(4,128)S(1)} %get-tuple-element.20.sea_ref, f32[3,72,128]{2,1,0:T(8,128)S(1)} %get-tuple-element.21.trig_ref, f32[3,1152,128]{2,1,0:T(8,128)S(1)} %get-tuple-element.22.refs_0_), custom_call_target="tpu_custom_call" | custom-call | tf_op jit(solution)/shard_map/late_edges/pallas_call | solution.py:417
  7.3 1.9 %collective-permute-start = (f32[2,576,128]{2,1,0:T(8,128)S(1)}, f32[2,576,128]{2,1,0:T(8,128)S(1)}, u32[]{:S(2)}, u32[]{:S(2)}) collective-permute-start(f32[2,576,128]{2,1,0:T(8,128)S(1)} %get-tuple-element.23), channel_id=1, source_target_pairs={{1,2},{3,4},{5,6},{7,8},{9,10},{11,12},{13,14},{2,1},{4,3},{6,5},{... | collective-permute-start | bytes 1769480 | tf_op jit(solution)/shard_map/ppermute | solution.py:404
  9.3 0.1 collective-permute-start.2
  9.3 0.0 copy-start
  9.3 0.0 copy-start.1
  9.4 0.0 copy-start.2
  9.4 2.4 %local_rows.2.local_ref = f32[3,1152,128]{2,1,0:T(8,128)S(1)} custom-call(s32[3,128]{1,0:T(4,128)S(1)} %get-tuple-element.20.sea_ref, f32[3,72,128]{2,1,0:T(8,128)S(1)} %get-tuple-element.21.trig_ref, f32[3,1152,128]{2,1,0:T(8,128)S(1)} %get-tuple-element.26.refs_0_), custom_call_target="tpu_custom_call" | custom-call | flops 30000001024 | tf_op jit(solution)/shard_map/local_rows/pallas_call | solution.py:417
  11.8 7.6 %collective-permute-done.1.cross_ref = f32[1,576,128]{2,1,0:T(8,128)S(1)} collective-permute-done((f32[1,576,128]{2,1,0:T(8,128)S(1)}, f32[1,576,128]{2,1,0:T(8,128)S(1)}, u32[]{:S(2)}, u32[]{:S(2)}) %collective-permute-start.1) | collective-permute-done | bytes 294944 | tf_op jit(solution)/shard_map/ppermute | solution.py:404
  19.4 0.0 collective-permute-done.2.inner_ref
  19.4 0.0 copy-done
  19.4 0.0 copy-done.1
  19.4 0.0 copy-done.2
  19.4 4.0 %far_rows.2 = (f32[1,1152,128]{2,1,0:T(8,128)S(1)}, f32[2,1152,128]{2,1,0:T(8,128)S(1)}) custom-call(s32[1]{0:T(128)} %bitcast.odd_ref, s32[3,128]{1,0:T(4,128)S(1)} %get-tuple-element.20.sea_ref, s32[3,128]{1,0:T(4,128)S(1)} %copy-done.1, f32[3,128]{1,0:T(4,128)S(1)} %copy-done.2, f32[3,72,128]{2,1,0:T(8,128)S(1)} %get-tuple-element.21.trig_ref, ...), custom_call_target="tpu_custom_call" | custom-call | tf_op jit(solution)/shard_map/far_rows/pallas_call | solution.py:417
  23.4 2.3 %collective-permute-done.late_ref = f32[2,576,128]{2,1,0:T(8,128)S(1)} collective-permute-done((f32[2,576,128]{2,1,0:T(8,128)S(1)}, f32[2,576,128]{2,1,0:T(8,128)S(1)}, u32[]{:S(2)}, u32[]{:S(2)}) %collective-permute-start) | collective-permute-done | bytes 589856 | tf_op jit(solution)/shard_map/ppermute | solution.py:404
  25.7 3.6 %near_rows.2 = (f32[2,1152,128]{2,1,0:T(8,128)S(1)}, f32[1,576,128]{2,1,0:T(8,128)S(1)}) custom-call(s32[1]{0:T(128)} %bitcast.odd_ref, s32[3,128]{1,0:T(4,128)S(1)} %get-tuple-element.20.sea_ref, s32[3,128]{1,0:T(4,128)S(1)} %copy-done.1, f32[3,128]{1,0:T(4,128)S(1)} %copy-done.2, f32[3,72,128]{2,1,0:T(8,128)S(1)} %get-tuple-element.21.trig_ref, ...), custom_call_target="tpu_custom_call" | custom-call | tf_op jit(solution)/shard_map/near_rows/pallas_call | solution.py:417
  29.3 4.4 %collective-permute-start.4 = (f32[1,576,128]{2,1,0:T(8,128)S(1)}, f32[1,576,128]{2,1,0:T(8,128)S(1)}, u32[]{:S(2)}, u32[]{:S(2)}) collective-permute-start(f32[1,576,128]{2,1,0:T(8,128)S(1)} %get-tuple-element.31), channel_id=1, source_target_pairs={{1,2},{3,4},{5,6},{7,8},{9,10},{11,12},{13,14},{2,1},{4,3},{6,5},{... | collective-permute-start | bytes 884744 | tf_op jit(solution)/shard_map/ppermute | solution.py:404
  33.7 0.9 %late_edges.3 = (f32[2,576,128]{2,1,0:T(8,128)S(1)}, f32[3,576,128]{2,1,0:T(8,128)S(1)}) custom-call(s32[1]{0:T(128)} %bitcast.odd_ref, s32[3,128]{1,0:T(4,128)S(1)} %get-tuple-element.20.sea_ref, f32[3,72,128]{2,1,0:T(8,128)S(1)} %get-tuple-element.21.trig_ref, f32[2,1152,128]{2,1,0:T(8,128)S(1)} %get-tuple-element.29.refs_0_, ...), custom_call_target="tpu_custom_call" | custom-call | tf_op jit(solution)/shard_map/late_edges/pallas_call | solution.py:417
  34.6 1.9 %collective-permute-start.3 = (f32[2,576,128]{2,1,0:T(8,128)S(1)}, f32[2,576,128]{2,1,0:T(8,128)S(1)}, u32[]{:S(2)}, u32[]{:S(2)}) collective-permute-start(f32[2,576,128]{2,1,0:T(8,128)S(1)} %get-tuple-element.30), channel_id=1, source_target_pairs={{1,2},{3,4},{5,6},{7,8},{9,10},{11,12},{13,14},{2,1},{4,3},{6,5},{... | collective-permute-start | bytes 1769480 | tf_op jit(solution)/shard_map/ppermute | solution.py:404
  36.5 0.1 collective-permute-start.5
  36.6 2.4 %local_rows.3.local_ref = f32[3,1152,128]{2,1,0:T(8,128)S(1)} custom-call(s32[3,128]{1,0:T(4,128)S(1)} %get-tuple-element.20.sea_ref, f32[3,72,128]{2,1,0:T(8,128)S(1)} %get-tuple-element.21.trig_ref, f32[2,1152,128]{2,1,0:T(8,128)S(1)} %get-tuple-element.29.refs_0_, f32[1,1152,128]{2,1,0:T(8,128)S(1)} %get-tuple-element.28.far_ref.refs_1_), custom_call_target="tpu_custom_call" | custom-call | flops 30000001024 | tf_op jit(solution)/shard_map/local_rows/pallas_call | solution.py:417
  39.0 2.4 %collective-permute-done.4.cross_ref = f32[1,576,128]{2,1,0:T(8,128)S(1)} collective-permute-done((f32[1,576,128]{2,1,0:T(8,128)S(1)}, f32[1,576,128]{2,1,0:T(8,128)S(1)}, u32[]{:S(2)}, u32[]{:S(2)}) %collective-permute-start.4) | collective-permute-done | bytes 294944 | tf_op jit(solution)/shard_map/ppermute | solution.py:404
  41.4 0.0 collective-permute-done.5.inner_ref
  41.4 3.9 %far_rows.3 = (f32[1,1152,128]{2,1,0:T(8,128)S(1)}, f32[2,1152,128]{2,1,0:T(8,128)S(1)}) custom-call(s32[1]{0:T(128)} %bitcast.odd_ref, s32[3,128]{1,0:T(4,128)S(1)} %get-tuple-element.20.sea_ref, s32[3,128]{1,0:T(4,128)S(1)} %copy-done.1, f32[3,128]{1,0:T(4,128)S(1)} %copy-done.2, f32[3,72,128]{2,1,0:T(8,128)S(1)} %get-tuple-element.21.trig_ref, ...), custom_call_target="tpu_custom_call" | custom-call | tf_op jit(solution)/shard_map/far_rows/pallas_call | solution.py:417
  45.3 2.4 %collective-permute-done.3.late_ref = f32[2,576,128]{2,1,0:T(8,128)S(1)} collective-permute-done((f32[2,576,128]{2,1,0:T(8,128)S(1)}, f32[2,576,128]{2,1,0:T(8,128)S(1)}, u32[]{:S(2)}, u32[]{:S(2)}) %collective-permute-start.3) | collective-permute-done | bytes 589856 | tf_op jit(solution)/shard_map/ppermute | solution.py:404
  47.7 4.3 %near_rows.3 = f32[3,1152,128]{2,1,0:T(8,128)} custom-call(s32[1]{0:T(128)} %bitcast.odd_ref, s32[3,128]{1,0:T(4,128)S(1)} %get-tuple-element.20.sea_ref, s32[3,128]{1,0:T(4,128)S(1)} %copy-done.1, f32[3,128]{1,0:T(4,128)S(1)} %copy-done.2, f32[3,72,128]{2,1,0:T(8,128)S(1)} %get-tuple-element.21.trig_ref, bf16[1152,1152]{1,0:T(8,128)(2,1)S(1)} %copy-done, ...), custom_call_target="tpu_custom_call" | custom-call | tf_op jit(solution)/shard_map/near_rows/pallas_call | solution.py:417
Async XLA Ops:
  1.7 17.7 %collective-permute-start.1 = (f32[1,576,128]{2,1,0:T(8,128)S(1)}, f32[1,576,128]{2,1,0:T(8,128)S(1)}, u32[]{:S(2)}, u32[]{:S(2)}) collective-permute-start(f32[1,576,128]{2,1,0:T(8,128)S(1)} %get-tuple-element.24), channel_id=1, source_target_pairs={{1,2},{3,4},{5,6},{7,8},{9,10},{11,12},{13,14},{2,1},{4,3},{6,5},{... | collective-permute-start | bytes 884744 | tf_op jit(solution)/shard_map/ppermute | solution.py:404
  7.3 18.4 %collective-permute-start = (f32[2,576,128]{2,1,0:T(8,128)S(1)}, f32[2,576,128]{2,1,0:T(8,128)S(1)}, u32[]{:S(2)}, u32[]{:S(2)}) collective-permute-start(f32[2,576,128]{2,1,0:T(8,128)S(1)} %get-tuple-element.23), channel_id=1, source_target_pairs={{1,2},{3,4},{5,6},{7,8},{9,10},{11,12},{13,14},{2,1},{4,3},{6,5},{... | collective-permute-start | bytes 1769480 | tf_op jit(solution)/shard_map/ppermute | solution.py:404
  9.3 10.1 %collective-permute-start.2 = (f32[3,576,128]{2,1,0:T(8,128)S(1)}, f32[3,576,128]{2,1,0:T(8,128)S(1)}, u32[]{:S(2)}, u32[]{:S(2)}) collective-permute-start(f32[3,576,128]{2,1,0:T(8,128)S(1)} %get-tuple-element.25), channel_id=1, source_target_pairs={{0,1},{2,3},{4,5},{6,7},{8,9},{10,11},{12,13},{14,15},{1,0},{3,2},... | collective-permute-start | bytes 2654216 | tf_op jit(solution)/shard_map/ppermute | solution.py:404
  9.3 10.0 %copy-start = (bf16[1152,1152]{1,0:T(8,128)(2,1)S(1)}, bf16[1152,1152]{1,0:T(8,128)(2,1)}, u32[]{:S(2)}) copy-start(bf16[1152,1152]{1,0:T(8,128)(2,1)} %matrix_ref.7) | copy-start | bytes 7962628
  9.3 10.0 %copy-start.1 = (s32[3,128]{1,0:T(4,128)S(1)}, s32[3,128]{1,0:T(4,128)}, u32[]{:S(2)}) copy-start(s32[3,128]{1,0:T(4,128)} %ice_ref.7) | copy-start | bytes 4612
  9.4 10.0 %copy-start.2 = (f32[3,128]{1,0:T(4,128)S(1)}, f32[3,128]{1,0:T(4,128)}, u32[]{:S(2)}) copy-start(f32[3,128]{1,0:T(4,128)} %wind_ref.7) | copy-start | bytes 4612
  29.3 12.1 %collective-permute-start.4 = (f32[1,576,128]{2,1,0:T(8,128)S(1)}, f32[1,576,128]{2,1,0:T(8,128)S(1)}, u32[]{:S(2)}, u32[]{:S(2)}) collective-permute-start(f32[1,576,128]{2,1,0:T(8,128)S(1)} %get-tuple-element.31), channel_id=1, source_target_pairs={{1,2},{3,4},{5,6},{7,8},{9,10},{11,12},{13,14},{2,1},{4,3},{6,5},{... | collective-permute-start | bytes 884744 | tf_op jit(solution)/shard_map/ppermute | solution.py:404
  34.6 13.1 %collective-permute-start.3 = (f32[2,576,128]{2,1,0:T(8,128)S(1)}, f32[2,576,128]{2,1,0:T(8,128)S(1)}, u32[]{:S(2)}, u32[]{:S(2)}) collective-permute-start(f32[2,576,128]{2,1,0:T(8,128)S(1)} %get-tuple-element.30), channel_id=1, source_target_pairs={{1,2},{3,4},{5,6},{7,8},{9,10},{11,12},{13,14},{2,1},{4,3},{6,5},{... | collective-permute-start | bytes 1769480 | tf_op jit(solution)/shard_map/ppermute | solution.py:404
  36.5 4.9 %collective-permute-start.5 = (f32[3,576,128]{2,1,0:T(8,128)S(1)}, f32[3,576,128]{2,1,0:T(8,128)S(1)}, u32[]{:S(2)}, u32[]{:S(2)}) collective-permute-start(f32[3,576,128]{2,1,0:T(8,128)S(1)} %get-tuple-element.32), channel_id=1, source_target_pairs={{0,1},{2,3},{4,5},{6,7},{8,9},{10,11},{12,13},{14,15},{1,0},{3,2},... | collective-permute-start | bytes 2654216 | tf_op jit(solution)/shard_map/ppermute | solution.py:404

commit v8 on v6

--- a/solution.py
+++ b/solution.py
@@ -28,7 +28,8 @@
 CHUNKS = 4
 EAST = (True, False, False, True)
 INWARD = (True, True, False, False)
-NEAR = SUBSTEPS - 1
+EARLY = 2
+NEAR = SUBSTEPS - EARLY
 
 
 def source_row(row):
@@ -122,27 +123,54 @@
     return out
 
 
-def edges(q, coefficients, rows, seas):
+def edges(q, coefficients, rows, seas, number):
     found = [rows[-1]]
-    rows, seas = rows[-SUBSTEPS:], seas[-SUBSTEPS:]
-    for _ in range(SUBSTEPS - 1):
+    rows, seas = rows[-number:], seas[-number:]
+    for _ in range(number - 1):
         rows = substep(q, coefficients, rows, seas, False)
         seas = seas[1:]
         found.append(rows[-1])
     return found
 
 
-def first_two(q, coefficients, seas, halo):
+def shares(q, coefficients, seas, halo):
     staying, along, across = coefficients
-    first = seas[0] * (across * halo[0])
-    beside_first = beside(q, first)
-    second = seas[1] * (across * first)
-    beside_second = beside(q, seas[1]) * (across * beside_first)
-    first = seas[0] * (staying * first + along * beside_first + across * halo[1])
-    after_two = second
-    second = seas[1] * (staying * second + along * beside_second + across * first)
-    first = seas[0] * (staying * first + along * beside(q, first) + across * halo[2])
-    return first, second, after_two
+    rows = []
+    for j in range(SUBSTEPS):
+        near = [None if value is None else beside(q, value) if known is None else known for value, known in rows]
+        new = []
+        for i in range(j + 1):
+            own = rows[i][0] if i < len(rows) else None
+            upstream = rows[i - 1][0] if i else halo[j]
+            value = known = None
+            if own is not None:
+                value = staying * own + along * near[i]
+            if upstream is not None:
+                value = across * upstream if value is None else value + across * upstream
+                if i and own is None and j + 1 < SUBSTEPS:
+                    known = beside(q, seas[i]) * (across * near[i - 1])
+            new.append((None if value is None else seas[i] * value, known))
+        rows = new
+    return [value for value, _ in rows]
+
+
+def with_shares(q, values, part):
+    values = list(values)
+    for i, value in enumerate(part):
+        r = i if INWARD[q] else len(values) - 1 - i
+        if value is not None and 0 <= r < len(values):
+            values[r] = values[r] + value
+    return values
+
+
+def outward_messages(block, row, count, seas, trig_ref, refs, start=0):
+    places = [(ref, j) for ref in refs for j in range(ref.shape[0])]
+    for q, coefficients in enumerate(block_coefficients(trig_ref, block)):
+        if not INWARD[q]:
+            rows = flow(q, [row(r, quadrant_at(block, q)) for r in range(count)])
+            found = edges(q, coefficients, rows, flow(q, seas), start + len(places))
+            for (ref, j), value in zip(places, found[start:]):
+                put(ref, j, half_at(block, q), value)
 
 
 def reader(row_refs):
@@ -150,8 +178,9 @@
         whole, = row_refs
         return whole.shape, lambda r, at: get(whole, r, at)
     near, far = row_refs
-    shape = (NEAR + far.shape[0],) + tuple(far.shape[1:])
-    return shape, lambda r, at: get(near, r, at) if r < NEAR else get(far, r - NEAR, at)
+    number = near.shape[0]
+    shape = (number + far.shape[0],) + tuple(far.shape[1:])
+    return shape, lambda r, at: get(near, r, at) if r < number else get(far, r - number, at)
 
 
 def spread_all(ref, count):
@@ -165,12 +194,6 @@
             out_ref[r, tile_at(odd, block, t), :] = tile
 
 
-def first_message(block, near_ref, cross_ref):
-    for q in range(QUADRANTS):
-        if not INWARD[q]:
-            cross_ref[0, half_at(block, q), :] = near_ref[0, quadrant_at(block, q), :]
-
-
 def first_kernel(odd_ref, f_hbm, sea_hbm, trig_hbm, f_ref, sea_ref, trig_ref, cross_ref, f_raw, sea_raw, trig_raw, sem, block_sem):
     count, _, width = f_ref.shape
     odd = odd_ref[0]
@@ -180,19 +203,10 @@
         return pltpu.make_async_copy(f_hbm.at[:, at, :], f_raw.at[:, at, :], block_sem.at[block])
 
     small = [pltpu.make_async_copy(sea_hbm, sea_raw, sem.at[0]), pltpu.make_async_copy(trig_hbm, trig_raw, sem.at[1])]
+    for copy in small:
+        copy.start()
     for block in range(BLOCKS):
         block_copy(block).start()
-    for copy in small:
-        copy.start()
-    iota = sublanes(width)
-
-    def body(block, carry):
-        block_copy(block).wait()
-        put_in_order(odd, block, lambda r, at: f_raw[counted(odd, r, count), at, :], f_ref, range(count), iota)
-        first_message(block, f_ref, cross_ref)
-        return carry
-
-    lax.fori_loop(0, BLOCKS, body, 0)
     for copy in small:
         copy.wait()
     for r in range(count):
@@ -200,6 +214,16 @@
     for i in range(2):
         trig_ref[i] = trig_raw[counted(odd, i, 2)]
     trig_ref[2] = trig_raw[2]
+    iota = sublanes(width)
+    seas = spread_all(sea_ref, count)
+
+    def body(block, carry):
+        block_copy(block).wait()
+        put_in_order(odd, block, lambda r, at: f_raw[counted(odd, r, count), at, :], f_ref, range(count), iota)
+        outward_messages(block, lambda r, at: get(f_ref, r, at), count, seas, trig_ref, [cross_ref])
+        return carry
+
+    lax.fori_loop(0, BLOCKS, body, 0)
 
 
 def late_kernel(sea_ref, trig_ref, *refs):
@@ -208,15 +232,29 @@
     seas = spread_all(sea_ref, count)
 
     def body(block, carry):
+        outward_messages(block, row, count, seas, trig_ref, [cross_ref], EARLY)
         for q, coefficients in enumerate(block_coefficients(trig_ref, block)):
-            rows = flow(q, [row(r, quadrant_at(block, q)) for r in range(count)])
-            found = edges(q, coefficients, rows, flow(q, seas))
             if INWARD[q]:
-                for j in range(SUBSTEPS):
-                    put(inner_ref, j, half_at(block, q), found[j])
-            else:
-                for j in range(1, SUBSTEPS):
-                    put(cross_ref, j - 1, half_at(block, q), found[j])
+                rows = flow(q, [row(r, quadrant_at(block, q)) for r in range(count)])
+                for j, value in enumerate(edges(q, coefficients, rows, flow(q, seas), SUBSTEPS)):
+                    put(inner_ref, j, half_at(block, q), value)
+        return carry
+
+    lax.fori_loop(0, BLOCKS, body, 0)
+
+
+def outward_kernel(sea_ref, trig_ref, inner_ref, local_ref, out_ref):
+    count = local_ref.shape[0]
+    seas = spread_all(sea_ref, count)
+
+    def body(block, carry):
+        for q, coefficients in enumerate(block_coefficients(trig_ref, block)):
+            if not INWARD[q]:
+                at, half = quadrant_at(block, q), half_at(block, q)
+                halo = [get(inner_ref, j, half) for j in range(SUBSTEPS)]
+                values = [get(local_ref, r, at) for r in range(count)]
+                for r, value in enumerate(with_shares(q, values, shares(q, coefficients, flow(q, seas), halo))):
+                    put(out_ref, r, half, value)
         return carry
 
     lax.fori_loop(0, BLOCKS, body, 0)
@@ -280,34 +318,28 @@
     return total
 
 
-def far_kernel(last, odd_ref, sea_ref, ice_ref, wind_ref, trig_ref, matrix_ref, cross_ref, inner_ref, local_ref,
-               far_ref, near_ref, f_acc, b_acc, moved):
-    count, _, width = local_ref.shape
+def far_kernel(last, odd_ref, sea_ref, ice_ref, wind_ref, trig_ref, matrix_ref, cross_ref, outward_ref, local_ref,
+               far_ref, part_ref, f_acc, b_acc, moved):
+    (count, _, width), near, early = local_ref.shape, part_ref.shape[0], cross_ref.shape[0]
     iota = sublanes(width)
     odd = odd_ref[0]
     seas = spread_all(sea_ref, count)
-    rows = range(NEAR, count)
+    rows = range(near, count)
 
     def advance(block, sums):
         for q, coefficients in enumerate(block_coefficients(trig_ref, block)):
-            at = quadrant_at(block, q)
-            across = coefficients[2]
+            at, half = quadrant_at(block, q), half_at(block, q)
             if INWARD[q]:
-                value = get(cross_ref, 0, half_at(block, q))
-                for r in range(SUBSTEPS):
-                    value = seas[r] * (across * value)
-                for r in rows:
-                    put(moved, r - NEAR, at, get(local_ref, r, at) + value if r == NEAR else get(local_ref, r, at))
+                halo = [get(cross_ref, j, half) if j < early else None for j in range(SUBSTEPS)]
+                values = [get(local_ref, r, at) for r in range(count)]
+                values = with_shares(q, values, shares(q, coefficients, seas, halo))
             else:
-                halo = [get(inner_ref, j, half_at(block, q)) for j in range(SUBSTEPS)]
-                first, second, after_two = first_two(q, coefficients, flow(q, seas), halo)
-                third = seas[count - 3] * (across * after_two)
-                for r, value in enumerate([None] * (count - 3) + [third, second, first]):
-                    value = get(local_ref, r, at) if value is None else get(local_ref, r, at) + value
-                    if r < NEAR:
-                        put(near_ref, r, half_at(block, q), value)
-                    else:
-                        put(moved, r - NEAR, at, value)
+                values = [get(outward_ref, r, half) for r in range(count)]
+            for r, value in enumerate(values):
+                if r < near:
+                    put(part_ref, r, at, value)
+                else:
+                    put(moved, r - near, at, value)
         return tuple(hold(odd, block, i, moved, f_acc, b_acc, iota, total) for i, total in enumerate(sums))
 
     zero = jnp.zeros((SUB, width), jnp.float32)
@@ -325,52 +357,54 @@
     lax.fori_loop(0, BLOCKS, finish, 0)
 
 
-def near_kernel(last, odd_ref, sea_ref, ice_ref, wind_ref, trig_ref, matrix_ref, cross_in, late_in, local_ref, part_ref, far_ref, *refs):
+def near_kernel(last, odd_ref, sea_ref, ice_ref, wind_ref, trig_ref, matrix_ref, late_ref, part_ref, far_ref, *refs):
     if last:
         out_ref, f_acc, b_acc, moved, sem = refs
     else:
-        out_ref, cross_ref, f_acc, b_acc, moved = refs
-    count, _, width = local_ref.shape
+        out_ref, message_ref, f_acc, b_acc, moved = refs
+    near, late, (_, _, width) = part_ref.shape[0], late_ref.shape[0], far_ref.shape
+    count = near + far_ref.shape[0]
     iota = sublanes(width)
     odd = odd_ref[0]
     seas = spread_all(sea_ref, count)
     if last:
-        copies = [pltpu.make_async_copy(far_ref.at[i], out_ref.at[counted(odd, NEAR + i, count)], sem.at[NEAR * CHUNKS + i])
-                  for i in range(count - NEAR)]
+        copies = [pltpu.make_async_copy(far_ref.at[i], out_ref.at[counted(odd, near + i, count)], sem.at[near * CHUNKS + i])
+                  for i in range(count - near)]
         for copy in copies:
             copy.start()
 
     def advance(block, sums):
         for q, coefficients in enumerate(block_coefficients(trig_ref, block)):
-            at, half = quadrant_at(block, q), half_at(block, q)
+            at = quadrant_at(block, q)
+            values = [get(part_ref, r, at) for r in range(near)]
             if INWARD[q]:
-                halo = [get(cross_in, 0, half)] + [get(late_in, j, half) for j in range(SUBSTEPS - 1)]
-                for r, value in enumerate(first_two(q, coefficients, seas, halo)[:NEAR]):
-                    put(moved, r, at, get(local_ref, r, at) + value)
-            else:
-                for r in range(NEAR):
-                    put(moved, r, at, get(part_ref, r, half))
+                halo = [None] * (SUBSTEPS - late) + [get(late_ref, j, half_at(block, q)) for j in range(late)]
+                values = with_shares(q, values, shares(q, coefficients, seas, halo))
+            for r, value in enumerate(values):
+                put(moved, r, at, value)
         return tuple(hold(odd, block, i, moved, f_acc, b_acc, iota, total) for i, total in enumerate(sums))
 
     zero = jnp.zeros((SUB, width), jnp.float32)
-    sums = lax.fori_loop(0, BLOCKS, advance, (zero,) * NEAR)
+    sums = lax.fori_loop(0, BLOCKS, advance, (zero,) * near)
     if last:
         def ready(c, at):
-            for r in range(NEAR):
+            for r in range(near):
                 copy = pltpu.make_async_copy(f_acc.at[at, pl.ds(r * width, width)], out_ref.at[counted(odd, r, count), at, :],
-                                             sem.at[NEAR * c + r])
+                                             sem.at[near * c + r])
                 copy.start()
                 copies.append(copy)
 
-        source_steps(odd, range(NEAR), sums, sea_ref, ice_ref, wind_ref, matrix_ref, f_acc, b_acc, ready)
+        source_steps(odd, range(near), sums, sea_ref, ice_ref, wind_ref, matrix_ref, f_acc, b_acc, ready)
         for copy in copies:
             copy.wait()
         return
-    source_steps(odd, range(NEAR), sums, sea_ref, ice_ref, wind_ref, matrix_ref, f_acc, b_acc)
+    source_steps(odd, range(near), sums, sea_ref, ice_ref, wind_ref, matrix_ref, f_acc, b_acc)
+
+    _, row = reader((out_ref, far_ref))
 
     def finish(block, carry):
-        put_in_order(odd, block, lambda r, at: f_acc[at, r * width:(r + 1) * width], out_ref, range(NEAR), iota)
-        first_message(block, out_ref, cross_ref)
+        put_in_order(odd, block, lambda r, at: f_acc[at, r * width:(r + 1) * width], out_ref, range(near), iota)
+        outward_messages(block, row, count, seas, trig_ref, [message_ref])
         return carry
 
     lax.fori_loop(0, BLOCKS, finish, 0)
@@ -414,21 +448,22 @@
     whole = jax.ShapeDtypeStruct((count, K, width), jnp.float32)
     operands = [pltpu.with_memory_space_constraint(x, pltpu.HBM) for x in (f, sea_mask, trig)]
     f, sea, trig, cross = call(
-        first_kernel, "first_edges", operands, [whole, sea_mask, trig, half(1)],
+        first_kernel, "first_edges", operands, [whole, sea_mask, trig, half(EARLY)],
         scratch=[pltpu.VMEM(x.shape, x.dtype) for x in (f, sea_mask, trig)] + [dma((2,)), dma((BLOCKS,))], in_space=hbm)
     rows = (f,)
     masks = (sea, ice_mask, wind, trig, source_matrix)
     for step in range(STEPS):
         last = step == STEPS - 1
         cross = swap(cross, outer_pairs)
-        late, inner = call(late_kernel, "late_edges", (sea, trig) + rows, [half(SUBSTEPS - 1), half(SUBSTEPS)], scalar=False)
+        late, inner = call(late_kernel, "late_edges", (sea, trig) + rows, [half(NEAR), half(SUBSTEPS)], scalar=False)
         late = swap(late, outer_pairs)
         inner = swap(inner, inner_pairs)
         local, = call(local_kernel, "local_rows", (sea, trig) + rows, [whole], scalar=False, cost=30000000000)
-        far, part = call(functools.partial(far_kernel, last), "far_rows", masks + (cross, inner, local),
-                         [(count - NEAR, K, width), half(NEAR)], count - NEAR)
-        outs = [whole] if last else [(NEAR, K, width), half(1)]
-        result = call(functools.partial(near_kernel, last), "near_rows", masks + (cross, late, local, part, far), outs, NEAR,
+        outward, = call(outward_kernel, "outward_rows", (sea, trig, inner, local), [half(count)], scalar=False)
+        far, part = call(functools.partial(far_kernel, last), "far_rows", masks + (cross, outward, local),
+                         [(count - NEAR, K, width), (NEAR, K, width)], count - NEAR)
+        outs = [whole] if last else [(NEAR, K, width), half(EARLY)]
+        result = call(functools.partial(near_kernel, last), "near_rows", masks + (late, part, far), outs, NEAR,
                       scratch=[dma((NEAR * CHUNKS + count - NEAR,))] if last else (), out_space=hbm if last else vmem)
         if last:
             return jnp.transpose(result[0], (1, 0, 2))

time: 52.6 us -> 50.3 us (0.956)
  waiting for transfers between devices: 15.5 us -> 12.8 us
    ppermute x6, waiting for transfers between devices: 15.5 us -> 12.8 us  [swap(): return lax.ppermute(value, 'comp', pairs + [(j, i) for i, j in pairs])]
    pallas_call x9 -> x11, Pallas kernels: 23.8 us -> 24.1 us  [call(): pl.pallas_call(kernel, out_shape=outs, name=name, in_specs=[pl.BlockSpec(...]
  transfers between devices with their start and end apart: 6 -> 6, of which waited for: 4 -> 2; matrix products, arithmetic and copies ran while one was open for 0% -> 0% of each run, Pallas kernels for 26% -> 30%
where the time goes in v8:
time: 50.3 us; the launch traced here: 50.1 us
  Pallas kernels  24.1 us (48%)
  starting transfers between devices  12.9 us (26%)
  waiting for transfers between devices  12.8 us (25%)
    pallas_call x11, Pallas kernels, call(): pl.pallas_call(kernel, out_shape=outs, name=name, in_specs=[pl.BlockSpec(...  24.1 us
    ppermute x6, starting transfers between devices, swap(): return lax.ppermute(value, 'comp', pairs + [(j, i) for i, j in pairs])  12.9 us
    ppermute x6, waiting for transfers between devices, swap(): return lax.ppermute(value, 'comp', pairs + [(j, i) for i, j in pairs])  12.8 us
  transfers between devices with their start and end apart: 6, of which 2 were waited for; matrix products, arithmetic and copies ran while one was open for 0% of the time, Pallas kernels for 30%

profile of v8, /device:TPU:1, one launch (start us, length us, event | category | flops | bytes accessed | tf_op | source)
XLA Modules:
  0.0 50.1 jit_solution(14360485065933633331)
XLA Ops:
  0.0 2.0 %first_edges.1 = (f32[3,1152,128]{2,1,0:T(8,128)S(1)}, s32[3,128]{1,0:T(4,128)S(1)}, f32[3,72,128]{2,1,0:T(8,128)S(1)}, f32[2,576,128]{2,1,0:T(8,128)S(1)}) custom-call(s32[1]{0:T(128)} %bitcast.odd_ref, f32[3,1152,128]{2,1,0:T(8,128)} %bitcast.3, s32[3,128]{1,0:T(4,128)} %sea_hbm.1, f32[3,72,128]{2,1,0:T(8,128)} %constant.19.clone.trig_hbm), custom_call_target="tpu_custom_call" | custom-call | tf_op jit(solution)/shard_map/first_edges/pallas_call | solution.py:437
  2.0 4.5 %collective-permute-start.1 = (f32[2,576,128]{2,1,0:T(8,128)S(1)}, f32[2,576,128]{2,1,0:T(8,128)S(1)}, u32[]{:S(2)}, u32[]{:S(2)}) collective-permute-start(f32[2,576,128]{2,1,0:T(8,128)S(1)} %get-tuple-element.23), channel_id=1, source_target_pairs={{1,2},{3,4},{5,6},{7,8},{9,10},{11,12},{13,14},{2,1},{4,3},{6,5},{... | collective-permute-start | bytes 1769480 | tf_op jit(solution)/shard_map/ppermute | solution.py:424
  6.5 0.9 %late_edges.2 = (f32[1,576,128]{2,1,0:T(8,128)S(1)}, f32[3,576,128]{2,1,0:T(8,128)S(1)}) custom-call(s32[3,128]{1,0:T(4,128)S(1)} %get-tuple-element.19.sea_ref, f32[3,72,128]{2,1,0:T(8,128)S(1)} %get-tuple-element.20.trig_ref, f32[3,1152,128]{2,1,0:T(8,128)S(1)} %get-tuple-element.21.refs_0_), custom_call_target="tpu_custom_call" | custom-call | tf_op jit(solution)/shard_map/late_edges/pallas_call | solution.py:437
  7.4 1.9 %collective-permute-start = (f32[1,576,128]{2,1,0:T(8,128)S(1)}, f32[1,576,128]{2,1,0:T(8,128)S(1)}, u32[]{:S(2)}, u32[]{:S(2)}) collective-permute-start(f32[1,576,128]{2,1,0:T(8,128)S(1)} %get-tuple-element.22), channel_id=1, source_target_pairs={{1,2},{3,4},{5,6},{7,8},{9,10},{11,12},{13,14},{2,1},{4,3},{6,5},{... | collective-permute-start | bytes 884744 | tf_op jit(solution)/shard_map/ppermute | solution.py:424
  9.3 0.1 collective-permute-start.2
  9.4 2.4 %local_rows.2.local_ref = f32[3,1152,128]{2,1,0:T(8,128)S(1)} custom-call(s32[3,128]{1,0:T(4,128)S(1)} %get-tuple-element.19.sea_ref, f32[3,72,128]{2,1,0:T(8,128)S(1)} %get-tuple-element.20.trig_ref, f32[3,1152,128]{2,1,0:T(8,128)S(1)} %get-tuple-element.21.refs_0_), custom_call_target="tpu_custom_call" | custom-call | flops 30000001024 | tf_op jit(solution)/shard_map/local_rows/pallas_call | solution.py:437
  11.8 0.0 copy-start
  11.8 0.0 copy-start.1
  11.8 0.0 copy-start.2
  11.9 0.0 collective-permute-done.2.inner_ref
  11.9 0.8 %outward_rows.2.outward_ref = f32[3,576,128]{2,1,0:T(8,128)S(1)} custom-call(s32[3,128]{1,0:T(4,128)S(1)} %get-tuple-element.19.sea_ref, f32[3,72,128]{2,1,0:T(8,128)S(1)} %get-tuple-element.20.trig_ref, f32[3,576,128]{2,1,0:T(8,128)S(1)} %collective-permute-done.2.inner_ref, f32[3,1152,128]{2,1,0:T(8,128)S(1)} %local_rows.2.local_ref), custom_call_target="tpu_custom_call" | custom-call | tf_op jit(solution)/shard_map/outward_rows/pallas_call | solution.py:437
  12.6 10.2 %collective-permute-done.1.cross_ref = f32[2,576,128]{2,1,0:T(8,128)S(1)} collective-permute-done((f32[2,576,128]{2,1,0:T(8,128)S(1)}, f32[2,576,128]{2,1,0:T(8,128)S(1)}, u32[]{:S(2)}, u32[]{:S(2)}) %collective-permute-start.1) | collective-permute-done | bytes 589856 | tf_op jit(solution)/shard_map/ppermute | solution.py:424
  22.8 0.0 copy-done
  22.8 0.0 copy-done.1
  22.8 0.0 copy-done.2
  22.8 3.7 %far_rows.2 = (f32[2,1152,128]{2,1,0:T(8,128)S(1)}, f32[1,1152,128]{2,1,0:T(8,128)S(1)}) custom-call(s32[1]{0:T(128)} %bitcast.odd_ref, s32[3,128]{1,0:T(4,128)S(1)} %get-tuple-element.19.sea_ref, s32[3,128]{1,0:T(4,128)S(1)} %copy-done.1, f32[3,128]{1,0:T(4,128)S(1)} %copy-done.2, f32[3,72,128]{2,1,0:T(8,128)S(1)} %get-tuple-element.20.trig_ref, ...), custom_call_target="tpu_custom_call" | custom-call | tf_op jit(solution)/shard_map/far_rows/pallas_call | solution.py:437
  26.6 0.0 collective-permute-done.late_ref
  26.6 3.3 %near_rows.2 = (f32[1,1152,128]{2,1,0:T(8,128)S(1)}, f32[2,576,128]{2,1,0:T(8,128)S(1)}) custom-call(s32[1]{0:T(128)} %bitcast.odd_ref, s32[3,128]{1,0:T(4,128)S(1)} %get-tuple-element.19.sea_ref, s32[3,128]{1,0:T(4,128)S(1)} %copy-done.1, f32[3,128]{1,0:T(4,128)S(1)} %copy-done.2, f32[3,72,128]{2,1,0:T(8,128)S(1)} %get-tuple-element.20.trig_ref, ...), custom_call_target="tpu_custom_call" | custom-call | tf_op jit(solution)/shard_map/near_rows/pallas_call | solution.py:437
  29.9 4.4 %collective-permute-start.4 = (f32[2,576,128]{2,1,0:T(8,128)S(1)}, f32[2,576,128]{2,1,0:T(8,128)S(1)}, u32[]{:S(2)}, u32[]{:S(2)}) collective-permute-start(f32[2,576,128]{2,1,0:T(8,128)S(1)} %get-tuple-element.29), channel_id=1, source_target_pairs={{1,2},{3,4},{5,6},{7,8},{9,10},{11,12},{13,14},{2,1},{4,3},{6,5},{... | collective-permute-start | bytes 1769480 | tf_op jit(solution)/shard_map/ppermute | solution.py:424
  34.3 0.9 %late_edges.3 = (f32[1,576,128]{2,1,0:T(8,128)S(1)}, f32[3,576,128]{2,1,0:T(8,128)S(1)}) custom-call(s32[3,128]{1,0:T(4,128)S(1)} %get-tuple-element.19.sea_ref, f32[3,72,128]{2,1,0:T(8,128)S(1)} %get-tuple-element.20.trig_ref, f32[1,1152,128]{2,1,0:T(8,128)S(1)} %get-tuple-element.27.refs_0_, f32[2,1152,128]{2,1,0:T(8,128)S(1)} %get-tuple-element.26.far_ref.refs_1_), custom_call_target="tpu_custom_call" | custom-call | tf_op jit(solution)/shard_map/late_edges/pallas_call | solution.py:437
  35.2 1.9 %collective-permute-start.3 = (f32[1,576,128]{2,1,0:T(8,128)S(1)}, f32[1,576,128]{2,1,0:T(8,128)S(1)}, u32[]{:S(2)}, u32[]{:S(2)}) collective-permute-start(f32[1,576,128]{2,1,0:T(8,128)S(1)} %get-tuple-element.28), channel_id=1, source_target_pairs={{1,2},{3,4},{5,6},{7,8},{9,10},{11,12},{13,14},{2,1},{4,3},{6,5},{... | collective-permute-start | bytes 884744 | tf_op jit(solution)/shard_map/ppermute | solution.py:424
  37.1 0.1 collective-permute-start.5
  37.2 2.4 %local_rows.3.local_ref = f32[3,1152,128]{2,1,0:T(8,128)S(1)} custom-call(s32[3,128]{1,0:T(4,128)S(1)} %get-tuple-element.19.sea_ref, f32[3,72,128]{2,1,0:T(8,128)S(1)} %get-tuple-element.20.trig_ref, f32[1,1152,128]{2,1,0:T(8,128)S(1)} %get-tuple-element.27.refs_0_, f32[2,1152,128]{2,1,0:T(8,128)S(1)} %get-tuple-element.26.far_ref.refs_1_), custom_call_target="tpu_custom_call" | custom-call | flops 30000001024 | tf_op jit(solution)/shard_map/local_rows/pallas_call | solution.py:437
  39.6 0.0 collective-permute-done.5.inner_ref
  39.6 0.8 %outward_rows.3.outward_ref = f32[3,576,128]{2,1,0:T(8,128)S(1)} custom-call(s32[3,128]{1,0:T(4,128)S(1)} %get-tuple-element.19.sea_ref, f32[3,72,128]{2,1,0:T(8,128)S(1)} %get-tuple-element.20.trig_ref, f32[3,576,128]{2,1,0:T(8,128)S(1)} %collective-permute-done.5.inner_ref, f32[3,1152,128]{2,1,0:T(8,128)S(1)} %local_rows.3.local_ref), custom_call_target="tpu_custom_call" | custom-call | tf_op jit(solution)/shard_map/outward_rows/pallas_call | solution.py:437
  40.4 2.6 %collective-permute-done.4.cross_ref = f32[2,576,128]{2,1,0:T(8,128)S(1)} collective-permute-done((f32[2,576,128]{2,1,0:T(8,128)S(1)}, f32[2,576,128]{2,1,0:T(8,128)S(1)}, u32[]{:S(2)}, u32[]{:S(2)}) %collective-permute-start.4) | collective-permute-done | bytes 589856 | tf_op jit(solution)/shard_map/ppermute | solution.py:424
  43.0 3.5 %far_rows.3 = (f32[2,1152,128]{2,1,0:T(8,128)S(1)}, f32[1,1152,128]{2,1,0:T(8,128)S(1)}) custom-call(s32[1]{0:T(128)} %bitcast.odd_ref, s32[3,128]{1,0:T(4,128)S(1)} %get-tuple-element.19.sea_ref, s32[3,128]{1,0:T(4,128)S(1)} %copy-done.1, f32[3,128]{1,0:T(4,128)S(1)} %copy-done.2, f32[3,72,128]{2,1,0:T(8,128)S(1)} %get-tuple-element.20.trig_ref, ...), custom_call_target="tpu_custom_call" | custom-call | tf_op jit(solution)/shard_map/far_rows/pallas_call | solution.py:437
  46.5 0.0 collective-permute-done.3.late_ref
  46.5 3.6 %near_rows.3 = f32[3,1152,128]{2,1,0:T(8,128)} custom-call(s32[1]{0:T(128)} %bitcast.odd_ref, s32[3,128]{1,0:T(4,128)S(1)} %get-tuple-element.19.sea_ref, s32[3,128]{1,0:T(4,128)S(1)} %copy-done.1, f32[3,128]{1,0:T(4,128)S(1)} %copy-done.2, f32[3,72,128]{2,1,0:T(8,128)S(1)} %get-tuple-element.20.trig_ref, bf16[1152,1152]{1,0:T(8,128)(2,1)S(1)} %copy-done, ...), custom_call_target="tpu_custom_call" | custom-call | tf_op jit(solution)/shard_map/near_rows/pallas_call | solution.py:437
Async XLA Ops:
  2.0 20.8 %collective-permute-start.1 = (f32[2,576,128]{2,1,0:T(8,128)S(1)}, f32[2,576,128]{2,1,0:T(8,128)S(1)}, u32[]{:S(2)}, u32[]{:S(2)}) collective-permute-start(f32[2,576,128]{2,1,0:T(8,128)S(1)} %get-tuple-element.23), channel_id=1, source_target_pairs={{1,2},{3,4},{5,6},{7,8},{9,10},{11,12},{13,14},{2,1},{4,3},{6,5},{... | collective-permute-start | bytes 1769480 | tf_op jit(solution)/shard_map/ppermute | solution.py:424
  7.4 19.2 %collective-permute-start = (f32[1,576,128]{2,1,0:T(8,128)S(1)}, f32[1,576,128]{2,1,0:T(8,128)S(1)}, u32[]{:S(2)}, u32[]{:S(2)}) collective-permute-start(f32[1,576,128]{2,1,0:T(8,128)S(1)} %get-tuple-element.22), channel_id=1, source_target_pairs={{1,2},{3,4},{5,6},{7,8},{9,10},{11,12},{13,14},{2,1},{4,3},{6,5},{... | collective-permute-start | bytes 884744 | tf_op jit(solution)/shard_map/ppermute | solution.py:424
  9.3 2.5 %collective-permute-start.2 = (f32[3,576,128]{2,1,0:T(8,128)S(1)}, f32[3,576,128]{2,1,0:T(8,128)S(1)}, u32[]{:S(2)}, u32[]{:S(2)}) collective-permute-start(f32[3,576,128]{2,1,0:T(8,128)S(1)} %get-tuple-element.24), channel_id=1, source_target_pairs={{0,1},{2,3},{4,5},{6,7},{8,9},{10,11},{12,13},{14,15},{1,0},{3,2},... | collective-permute-start | bytes 2654216 | tf_op jit(solution)/shard_map/ppermute | solution.py:424
  11.8 11.0 %copy-start = (bf16[1152,1152]{1,0:T(8,128)(2,1)S(1)}, bf16[1152,1152]{1,0:T(8,128)(2,1)}, u32[]{:S(2)}) copy-start(bf16[1152,1152]{1,0:T(8,128)(2,1)} %matrix_ref.7) | copy-start | bytes 7962628
  11.8 11.0 %copy-start.1 = (s32[3,128]{1,0:T(4,128)S(1)}, s32[3,128]{1,0:T(4,128)}, u32[]{:S(2)}) copy-start(s32[3,128]{1,0:T(4,128)} %ice_ref.7) | copy-start | bytes 4612
  11.8 11.0 %copy-start.2 = (f32[3,128]{1,0:T(4,128)S(1)}, f32[3,128]{1,0:T(4,128)}, u32[]{:S(2)}) copy-start(f32[3,128]{1,0:T(4,128)} %wind_ref.7) | copy-start | bytes 4612
  29.9 13.1 %collective-permute-start.4 = (f32[2,576,128]{2,1,0:T(8,128)S(1)}, f32[2,576,128]{2,1,0:T(8,128)S(1)}, u32[]{:S(2)}, u32[]{:S(2)}) collective-permute-start(f32[2,576,128]{2,1,0:T(8,128)S(1)} %get-tuple-element.29), channel_id=1, source_target_pairs={{1,2},{3,4},{5,6},{7,8},{9,10},{11,12},{13,14},{2,1},{4,3},{6,5},{... | collective-permute-start | bytes 1769480 | tf_op jit(solution)/shard_map/ppermute | solution.py:424
  35.2 11.3 %collective-permute-start.3 = (f32[1,576,128]{2,1,0:T(8,128)S(1)}, f32[1,576,128]{2,1,0:T(8,128)S(1)}, u32[]{:S(2)}, u32[]{:S(2)}) collective-permute-start(f32[1,576,128]{2,1,0:T(8,128)S(1)} %get-tuple-element.28), channel_id=1, source_target_pairs={{1,2},{3,4},{5,6},{7,8},{9,10},{11,12},{13,14},{2,1},{4,3},{6,5},{... | collective-permute-start | bytes 884744 | tf_op jit(solution)/shard_map/ppermute | solution.py:424
  37.1 2.5 %collective-permute-start.5 = (f32[3,576,128]{2,1,0:T(8,128)S(1)}, f32[3,576,128]{2,1,0:T(8,128)S(1)}, u32[]{:S(2)}, u32[]{:S(2)}) collective-permute-start(f32[3,576,128]{2,1,0:T(8,128)S(1)} %get-tuple-element.30), channel_id=1, source_target_pairs={{0,1},{2,3},{4,5},{6,7},{8,9},{10,11},{12,13},{14,15},{1,0},{3,2},... | collective-permute-start | bytes 2654216 | tf_op jit(solution)/shard_map/ppermute | solution.py:424

commit v9 on v8

--- a/solution.py
+++ b/solution.py
@@ -25,7 +25,7 @@
 BLOCK = QUADRANTS * ARC_ROWS
 BLOCKS = K // BLOCK
 HALF = BLOCK // 2
-CHUNKS = 4
+CHUNKS = BLOCKS
 EAST = (True, False, False, True)
 INWARD = (True, True, False, False)
 EARLY = 2
@@ -55,12 +55,20 @@
     return out
 
 
-def pattern():
-    row = np.arange(ARC_ROWS)
-    theta = 2.0 * np.pi * (row % ARC + 0.5) / NDIR
-    slower = 0.6 * 0.65 / (NFREQ - 1) * (row // ARC)
-    table = np.stack([np.cos(theta), np.sin(theta), slower]).astype(np.float32)
-    return jnp.asarray(np.ascontiguousarray(np.broadcast_to(table[:, :, None], (3, ARC_ROWS, 128))))
+def pattern(width):
+    row = lax.broadcasted_iota(jnp.int32, (ARC_ROWS, width), 0)
+    angle = [2.0 * np.pi * (d + 0.5) / NDIR for d in range(ARC)]
+    frequency = jnp.zeros((ARC_ROWS, width), jnp.int32)
+    for f in range(1, SUB):
+        frequency = jnp.where(row >= f * ARC, f, frequency)
+    direction = row - ARC * frequency
+    tables = []
+    for values in (np.cos(angle), np.sin(angle)):
+        table = jnp.full((ARC_ROWS, width), float(values[0]), jnp.float32)
+        for d in range(1, ARC):
+            table = jnp.where(direction == d, float(values[d]), table)
+        tables.append(table)
+    return tables + [(0.6 * 0.65 / (NFREQ - 1)) * frequency.astype(jnp.float32)]
 
 
 def sublanes(width):
@@ -85,7 +93,7 @@
 
 
 def block_coefficients(trig_ref, block):
-    frequency = (block * SUB).astype(jnp.float32)
+    frequency = jnp.float32(block * SUB)
     fastest = 0.6 * (0.35 + (0.65 / (NFREQ - 1)) * ((NFREQ - 1) - frequency))
     cosine, sine, slower = (trig_ref[i].reshape(ARC, SUB, -1) for i in range(3))
     one, other = (fastest - slower) * cosine, (fastest - slower) * sine
@@ -194,44 +202,54 @@
             out_ref[r, tile_at(odd, block, t), :] = tile
 
 
-def first_kernel(odd_ref, f_hbm, sea_hbm, trig_hbm, f_ref, sea_ref, trig_ref, cross_ref, f_raw, sea_raw, trig_raw, sem, block_sem):
-    count, _, width = f_ref.shape
+def first_kernel(odd_ref, f_hbm, sea_hbm, f_ref, rest_ref, sea_ref, trig_ref, cross_ref, f_raw, sea_raw, sem, block_sem):
+    count, _, width = f_hbm.shape
     odd = odd_ref[0]
 
     def block_copy(block):
         at = pl.ds(pl.multiple_of(block * BLOCK, BLOCK), BLOCK)
-        return pltpu.make_async_copy(f_hbm.at[:, at, :], f_raw.at[:, at, :], block_sem.at[block])
-
-    small = [pltpu.make_async_copy(sea_hbm, sea_raw, sem.at[0]), pltpu.make_async_copy(trig_hbm, trig_raw, sem.at[1])]
-    for copy in small:
-        copy.start()
+        return pltpu.make_async_copy(f_hbm.at[pl.ds(odd * (count - EARLY), EARLY), at, :], f_raw.at[:, at, :], block_sem.at[block])
+
+    sea_copy = pltpu.make_async_copy(sea_hbm, sea_raw, sem.at[0])
+    rest_copy = pltpu.make_async_copy(f_hbm.at[pl.ds((1 - odd) * EARLY, count - EARLY)], rest_ref, sem.at[1])
+    sea_copy.start()
     for block in range(BLOCKS):
         block_copy(block).start()
-    for copy in small:
-        copy.wait()
+    rest_copy.start()
+    cosine, sine, slower = pattern(width)
+    trig_ref[0] = jnp.where(odd == 1, sine, cosine)
+    trig_ref[1] = jnp.where(odd == 1, cosine, sine)
+    trig_ref[2] = slower
+    sea_copy.wait()
     for r in range(count):
         sea_ref[r:r + 1, :] = sea_raw[pl.ds(counted(odd, r, count), 1), :]
-    for i in range(2):
-        trig_ref[i] = trig_raw[counted(odd, i, 2)]
-    trig_ref[2] = trig_raw[2]
     iota = sublanes(width)
-    seas = spread_all(sea_ref, count)
+    seas = spread_all(sea_ref, EARLY)
 
     def body(block, carry):
         block_copy(block).wait()
-        put_in_order(odd, block, lambda r, at: f_raw[counted(odd, r, count), at, :], f_ref, range(count), iota)
-        outward_messages(block, lambda r, at: get(f_ref, r, at), count, seas, trig_ref, [cross_ref])
+        put_in_order(odd, block, lambda r, at: f_raw[counted(odd, r, EARLY), at, :], f_ref, range(EARLY), iota)
+        outward_messages(block, lambda r, at: get(f_ref, r, at), EARLY, seas, trig_ref, [cross_ref])
         return carry
 
     lax.fori_loop(0, BLOCKS, body, 0)
-
-
-def late_kernel(sea_ref, trig_ref, *refs):
-    cross_ref, inner_ref = refs[-2:]
-    (count, _, _), row = reader(refs[:-2])
+    rest_copy.wait()
+
+
+def late_kernel(first, odd_ref, sea_ref, trig_ref, *refs):
+    if first:
+        early_ref, raw_ref, cross_ref, inner_ref, rest_ref = refs
+        own = early_ref, rest_ref
+        iota, left = sublanes(raw_ref.shape[2]), raw_ref.shape[0]
+    else:
+        *own, cross_ref, inner_ref = refs
+    (count, _, _), row = reader(own)
+    odd = odd_ref[0]
     seas = spread_all(sea_ref, count)
 
     def body(block, carry):
+        if first:
+            put_in_order(odd, block, lambda r, at: raw_ref[counted(odd, r, left), at, :], rest_ref, range(left), iota)
         outward_messages(block, row, count, seas, trig_ref, [cross_ref], EARLY)
         for q, coefficients in enumerate(block_coefficients(trig_ref, block)):
             if INWARD[q]:
@@ -344,17 +362,14 @@
 
     zero = jnp.zeros((SUB, width), jnp.float32)
     sums = lax.fori_loop(0, BLOCKS, advance, (zero,) * len(rows))
-    source_steps(odd, rows, sums, sea_ref, ice_ref, wind_ref, matrix_ref, f_acc, b_acc)
-    if last:
-        for i in range(len(rows)):
-            far_ref[i] = f_acc[:, i * width:(i + 1) * width]
-        return
-
-    def finish(block, carry):
-        put_in_order(odd, block, lambda r, at: f_acc[at, r * width:(r + 1) * width], far_ref, range(len(rows)), iota)
-        return carry
-
-    lax.fori_loop(0, BLOCKS, finish, 0)
+    def ready(block, at):
+        if last:
+            for i in range(len(rows)):
+                far_ref[i, at, :] = f_acc[at, i * width:(i + 1) * width]
+        else:
+            put_in_order(odd, block, lambda r, at: f_acc[at, r * width:(r + 1) * width], far_ref, range(len(rows)), iota)
+
+    source_steps(odd, rows, sums, sea_ref, ice_ref, wind_ref, matrix_ref, f_acc, b_acc, ready)
 
 
 def near_kernel(last, odd_ref, sea_ref, ice_ref, wind_ref, trig_ref, matrix_ref, late_ref, part_ref, far_ref, *refs):
@@ -398,16 +413,13 @@
         for copy in copies:
             copy.wait()
         return
-    source_steps(odd, range(near), sums, sea_ref, ice_ref, wind_ref, matrix_ref, f_acc, b_acc)
-
     _, row = reader((out_ref, far_ref))
 
-    def finish(block, carry):
+    def finish(block, at):
         put_in_order(odd, block, lambda r, at: f_acc[at, r * width:(r + 1) * width], out_ref, range(near), iota)
         outward_messages(block, row, count, seas, trig_ref, [message_ref])
-        return carry
-
-    lax.fori_loop(0, BLOCKS, finish, 0)
+
+    source_steps(odd, range(near), sums, sea_ref, ice_ref, wind_ref, matrix_ref, f_acc, b_acc, finish)
 
 
 def on_device(spectrum, sea_mask, ice_mask, wind, source_matrix):
@@ -416,7 +428,7 @@
     assert comps == K and count >= SUBSTEPS and size % 2 == 0
     odd = (lax.axis_index("comp") % 2).astype(jnp.int32).reshape(1)
     f = jnp.transpose(spectrum, (1, 0, 2))
-    trig = pattern()
+    trig = jax.ShapeDtypeStruct((3, ARC_ROWS, width), jnp.float32)
     outer_pairs = [(i, i + 1) for i in range(1, size - 1, 2)]
     inner_pairs = [(i, i + 1) for i in range(0, size, 2)]
 
@@ -446,16 +458,20 @@
         return (number, K // 2, width)
 
     whole = jax.ShapeDtypeStruct((count, K, width), jnp.float32)
-    operands = [pltpu.with_memory_space_constraint(x, pltpu.HBM) for x in (f, sea_mask, trig)]
-    f, sea, trig, cross = call(
-        first_kernel, "first_edges", operands, [whole, sea_mask, trig, half(EARLY)],
-        scratch=[pltpu.VMEM(x.shape, x.dtype) for x in (f, sea_mask, trig)] + [dma((2,)), dma((BLOCKS,))], in_space=hbm)
-    rows = (f,)
+    rest = (count - EARLY, K, width)
+    operands = [pltpu.with_memory_space_constraint(x, pltpu.HBM) for x in (f, sea_mask)]
+    f, raw, sea, trig, cross = call(
+        first_kernel, "first_edges", operands, [(EARLY, K, width), rest, sea_mask, trig, half(EARLY)],
+        scratch=[pltpu.VMEM((EARLY, K, width), jnp.float32), pltpu.VMEM(sea_mask.shape, sea_mask.dtype), dma((2,)), dma((BLOCKS,))],
+        in_space=hbm)
+    rows = (f, raw)
     masks = (sea, ice_mask, wind, trig, source_matrix)
     for step in range(STEPS):
-        last = step == STEPS - 1
+        first, last = step == 0, step == STEPS - 1
         cross = swap(cross, outer_pairs)
-        late, inner = call(late_kernel, "late_edges", (sea, trig) + rows, [half(NEAR), half(SUBSTEPS)], scalar=False)
+        late, inner, *more = call(functools.partial(late_kernel, first), "late_edges", (sea, trig) + rows,
+                                  [half(NEAR), half(SUBSTEPS)] + [rest] * first)
+        rows = (f, *more) if first else rows
         late = swap(late, outer_pairs)
         inner = swap(inner, inner_pairs)
         local, = call(local_kernel, "local_rows", (sea, trig) + rows, [whole], scalar=False, cost=30000000000)

time: 50.3 us -> 49.4 us (0.982)
  Pallas kernels: 24.1 us -> 23.3 us
    pallas_call x11, Pallas kernels: 24.1 us -> 23.3 us  [call(): pl.pallas_call(kernel, out_shape=outs, name=name, in_specs=[pl.BlockSpec(...]
  transfers between devices with their start and end apart: 6 -> 6, of which waited for: 2 -> 2; matrix products, arithmetic and copies ran while one was open for 0% -> 0% of each run, Pallas kernels for 30% -> 31%
where the time goes in v9:
time: 49.4 us; the launch traced here: 49.2 us
  Pallas kernels  23.3 us (47%)
  starting transfers between devices  12.9 us (26%)
  waiting for transfers between devices  12.8 us (26%)
    pallas_call x11, Pallas kernels, call(): pl.pallas_call(kernel, out_shape=outs, name=name, in_specs=[pl.BlockSpec(...  23.3 us
    ppermute x6, starting transfers between devices, swap(): return lax.ppermute(value, 'comp', pairs + [(j, i) for i, j in pairs])  12.9 us
    ppermute x6, waiting for transfers between devices, swap(): return lax.ppermute(value, 'comp', pairs + [(j, i) for i, j in pairs])  12.8 us
  transfers between devices with their start and end apart: 6, of which 2 were waited for; matrix products, arithmetic and copies ran while one was open for 0% of the time, Pallas kernels for 31%

profile of v9, /device:TPU:1, one launch (start us, length us, event | category | flops | bytes accessed | tf_op | source)
XLA Modules:
  0.0 49.2 jit_solution(2902096796601773144)
XLA Ops:
  0.0 1.6 %first_edges.1 = (f32[2,1152,128]{2,1,0:T(8,128)S(1)}, f32[1,1152,128]{2,1,0:T(8,128)S(1)}, s32[3,128]{1,0:T(4,128)S(1)}, f32[3,72,128]{2,1,0:T(8,128)S(1)}, f32[2,576,128]{2,1,0:T(8,128)S(1)}) custom-call(s32[1]{0:T(128)} %bitcast.odd_ref, f32[3,1152,128]{2,1,0:T(8,128)} %bitcast.3, s32[3,128]{1,0:T(4,128)} %sea_hbm.1), custom_call_target="tpu_custom_call" | custom-call | tf_op jit(solution)/shard_map/first_edges/pallas_call | solution.py:449
  1.6 4.5 %collective-permute-start.1 = (f32[2,576,128]{2,1,0:T(8,128)S(1)}, f32[2,576,128]{2,1,0:T(8,128)S(1)}, u32[]{:S(2)}, u32[]{:S(2)}) collective-permute-start(f32[2,576,128]{2,1,0:T(8,128)S(1)} %get-tuple-element.26), channel_id=1, source_target_pairs={{1,2},{3,4},{5,6},{7,8},{9,10},{11,12},{13,14},{2,1},{4,3},{6,5},{... | collective-permute-start | bytes 1769480 | tf_op jit(solution)/shard_map/ppermute | solution.py:436
  6.1 0.9 %late_edges.2 = (f32[1,576,128]{2,1,0:T(8,128)S(1)}, f32[3,576,128]{2,1,0:T(8,128)S(1)}, f32[1,1152,128]{2,1,0:T(8,128)S(1)}) custom-call(s32[1]{0:T(128)} %bitcast.odd_ref, s32[3,128]{1,0:T(4,128)S(1)} %get-tuple-element.21.sea_ref, f32[3,72,128]{2,1,0:T(8,128)S(1)} %get-tuple-element.22.trig_ref, f32[2,1152,128]{2,1,0:T(8,128)S(1)} %get-tuple-element.23.refs_0_, ...), custom_call_target="tpu_custom_call" | custom-call | tf_op jit(solution)/shard_map/late_edges/pallas_call | solution.py:449
  7.0 1.9 %collective-permute-start = (f32[1,576,128]{2,1,0:T(8,128)S(1)}, f32[1,576,128]{2,1,0:T(8,128)S(1)}, u32[]{:S(2)}, u32[]{:S(2)}) collective-permute-start(f32[1,576,128]{2,1,0:T(8,128)S(1)} %get-tuple-element.25), channel_id=1, source_target_pairs={{1,2},{3,4},{5,6},{7,8},{9,10},{11,12},{13,14},{2,1},{4,3},{6,5},{... | collective-permute-start | bytes 884744 | tf_op jit(solution)/shard_map/ppermute | solution.py:436
  8.9 0.1 collective-permute-start.2
  9.0 2.4 %local_rows.2.local_ref = f32[3,1152,128]{2,1,0:T(8,128)S(1)} custom-call(s32[3,128]{1,0:T(4,128)S(1)} %get-tuple-element.21.sea_ref, f32[3,72,128]{2,1,0:T(8,128)S(1)} %get-tuple-element.22.trig_ref, f32[2,1152,128]{2,1,0:T(8,128)S(1)} %get-tuple-element.23.refs_0_, f32[1,1152,128]{2,1,0:T(8,128)S(1)} %get-tuple-element.28.refs_1_), custom_call_target="tpu_custom_call" | custom-call | flops 30000001024 | tf_op jit(solution)/shard_map/local_rows/pallas_call | solution.py:449
  11.4 0.0 copy-start
  11.4 0.0 copy-start.1
  11.4 0.0 copy-start.2
  11.4 0.0 collective-permute-done.2.inner_ref
  11.5 0.8 %outward_rows.2.outward_ref = f32[3,576,128]{2,1,0:T(8,128)S(1)} custom-call(s32[3,128]{1,0:T(4,128)S(1)} %get-tuple-element.21.sea_ref, f32[3,72,128]{2,1,0:T(8,128)S(1)} %get-tuple-element.22.trig_ref, f32[3,576,128]{2,1,0:T(8,128)S(1)} %collective-permute-done.2.inner_ref, f32[3,1152,128]{2,1,0:T(8,128)S(1)} %local_rows.2.local_ref), custom_call_target="tpu_custom_call" | custom-call | tf_op jit(solution)/shard_map/outward_rows/pallas_call | solution.py:449
  12.2 10.2 %collective-permute-done.1.cross_ref = f32[2,576,128]{2,1,0:T(8,128)S(1)} collective-permute-done((f32[2,576,128]{2,1,0:T(8,128)S(1)}, f32[2,576,128]{2,1,0:T(8,128)S(1)}, u32[]{:S(2)}, u32[]{:S(2)}) %collective-permute-start.1) | collective-permute-done | bytes 589856 | tf_op jit(solution)/shard_map/ppermute | solution.py:436
  22.4 0.0 copy-done
  22.4 0.0 copy-done.1
  22.4 0.0 copy-done.2
  22.4 3.6 %far_rows.2 = (f32[2,1152,128]{2,1,0:T(8,128)S(1)}, f32[1,1152,128]{2,1,0:T(8,128)S(1)}) custom-call(s32[1]{0:T(128)} %bitcast.odd_ref, s32[3,128]{1,0:T(4,128)S(1)} %get-tuple-element.21.sea_ref, s32[3,128]{1,0:T(4,128)S(1)} %copy-done.1, f32[3,128]{1,0:T(4,128)S(1)} %copy-done.2, f32[3,72,128]{2,1,0:T(8,128)S(1)} %get-tuple-element.22.trig_ref, ...), custom_call_target="tpu_custom_call" | custom-call | tf_op jit(solution)/shard_map/far_rows/pallas_call | solution.py:449
  26.0 0.0 collective-permute-done.late_ref
  26.1 2.9 %near_rows.2 = (f32[1,1152,128]{2,1,0:T(8,128)S(1)}, f32[2,576,128]{2,1,0:T(8,128)S(1)}) custom-call(s32[1]{0:T(128)} %bitcast.odd_ref, s32[3,128]{1,0:T(4,128)S(1)} %get-tuple-element.21.sea_ref, s32[3,128]{1,0:T(4,128)S(1)} %copy-done.1, f32[3,128]{1,0:T(4,128)S(1)} %copy-done.2, f32[3,72,128]{2,1,0:T(8,128)S(1)} %get-tuple-element.22.trig_ref, ...), custom_call_target="tpu_custom_call" | custom-call | tf_op jit(solution)/shard_map/near_rows/pallas_call | solution.py:449
  29.0 4.4 %collective-permute-start.4 = (f32[2,576,128]{2,1,0:T(8,128)S(1)}, f32[2,576,128]{2,1,0:T(8,128)S(1)}, u32[]{:S(2)}, u32[]{:S(2)}) collective-permute-start(f32[2,576,128]{2,1,0:T(8,128)S(1)} %get-tuple-element.33), channel_id=1, source_target_pairs={{1,2},{3,4},{5,6},{7,8},{9,10},{11,12},{13,14},{2,1},{4,3},{6,5},{... | collective-permute-start | bytes 1769480 | tf_op jit(solution)/shard_map/ppermute | solution.py:436
  33.4 0.9 %late_edges.3 = (f32[1,576,128]{2,1,0:T(8,128)S(1)}, f32[3,576,128]{2,1,0:T(8,128)S(1)}) custom-call(s32[1]{0:T(128)} %bitcast.odd_ref, s32[3,128]{1,0:T(4,128)S(1)} %get-tuple-element.21.sea_ref, f32[3,72,128]{2,1,0:T(8,128)S(1)} %get-tuple-element.22.trig_ref, f32[1,1152,128]{2,1,0:T(8,128)S(1)} %get-tuple-element.31.refs_0_, ...), custom_call_target="tpu_custom_call" | custom-call | tf_op jit(solution)/shard_map/late_edges/pallas_call | solution.py:449
  34.3 1.9 %collective-permute-start.3 = (f32[1,576,128]{2,1,0:T(8,128)S(1)}, f32[1,576,128]{2,1,0:T(8,128)S(1)}, u32[]{:S(2)}, u32[]{:S(2)}) collective-permute-start(f32[1,576,128]{2,1,0:T(8,128)S(1)} %get-tuple-element.32), channel_id=1, source_target_pairs={{1,2},{3,4},{5,6},{7,8},{9,10},{11,12},{13,14},{2,1},{4,3},{6,5},{... | collective-permute-start | bytes 884744 | tf_op jit(solution)/shard_map/ppermute | solution.py:436
  36.2 0.1 collective-permute-start.5
  36.3 2.4 %local_rows.3.local_ref = f32[3,1152,128]{2,1,0:T(8,128)S(1)} custom-call(s32[3,128]{1,0:T(4,128)S(1)} %get-tuple-element.21.sea_ref, f32[3,72,128]{2,1,0:T(8,128)S(1)} %get-tuple-element.22.trig_ref, f32[1,1152,128]{2,1,0:T(8,128)S(1)} %get-tuple-element.31.refs_0_, f32[2,1152,128]{2,1,0:T(8,128)S(1)} %get-tuple-element.30.far_ref.refs_1_), custom_call_target="tpu_custom_call" | custom-call | flops 30000001024 | tf_op jit(solution)/shard_map/local_rows/pallas_call | solution.py:449
  38.7 0.0 collective-permute-done.5.inner_ref
  38.7 0.8 %outward_rows.3.outward_ref = f32[3,576,128]{2,1,0:T(8,128)S(1)} custom-call(s32[3,128]{1,0:T(4,128)S(1)} %get-tuple-element.21.sea_ref, f32[3,72,128]{2,1,0:T(8,128)S(1)} %get-tuple-element.22.trig_ref, f32[3,576,128]{2,1,0:T(8,128)S(1)} %collective-permute-done.5.inner_ref, f32[3,1152,128]{2,1,0:T(8,128)S(1)} %local_rows.3.local_ref), custom_call_target="tpu_custom_call" | custom-call | tf_op jit(solution)/shard_map/outward_rows/pallas_call | solution.py:449
  39.5 2.6 %collective-permute-done.4.cross_ref = f32[2,576,128]{2,1,0:T(8,128)S(1)} collective-permute-done((f32[2,576,128]{2,1,0:T(8,128)S(1)}, f32[2,576,128]{2,1,0:T(8,128)S(1)}, u32[]{:S(2)}, u32[]{:S(2)}) %collective-permute-start.4) | collective-permute-done | bytes 589856 | tf_op jit(solution)/shard_map/ppermute | solution.py:436
  42.1 3.5 %far_rows.3 = (f32[2,1152,128]{2,1,0:T(8,128)S(1)}, f32[1,1152,128]{2,1,0:T(8,128)S(1)}) custom-call(s32[1]{0:T(128)} %bitcast.odd_ref, s32[3,128]{1,0:T(4,128)S(1)} %get-tuple-element.21.sea_ref, s32[3,128]{1,0:T(4,128)S(1)} %copy-done.1, f32[3,128]{1,0:T(4,128)S(1)} %copy-done.2, f32[3,72,128]{2,1,0:T(8,128)S(1)} %get-tuple-element.22.trig_ref, ...), custom_call_target="tpu_custom_call" | custom-call | tf_op jit(solution)/shard_map/far_rows/pallas_call | solution.py:449
  45.6 0.0 collective-permute-done.3.late_ref
  45.6 3.6 %near_rows.3 = f32[3,1152,128]{2,1,0:T(8,128)} custom-call(s32[1]{0:T(128)} %bitcast.odd_ref, s32[3,128]{1,0:T(4,128)S(1)} %get-tuple-element.21.sea_ref, s32[3,128]{1,0:T(4,128)S(1)} %copy-done.1, f32[3,128]{1,0:T(4,128)S(1)} %copy-done.2, f32[3,72,128]{2,1,0:T(8,128)S(1)} %get-tuple-element.22.trig_ref, bf16[1152,1152]{1,0:T(8,128)(2,1)S(1)} %copy-done, ...), custom_call_target="tpu_custom_call" | custom-call | tf_op jit(solution)/shard_map/near_rows/pallas_call | solution.py:449
Async XLA Ops:
  1.6 20.8 %collective-permute-start.1 = (f32[2,576,128]{2,1,0:T(8,128)S(1)}, f32[2,576,128]{2,1,0:T(8,128)S(1)}, u32[]{:S(2)}, u32[]{:S(2)}) collective-permute-start(f32[2,576,128]{2,1,0:T(8,128)S(1)} %get-tuple-element.26), channel_id=1, source_target_pairs={{1,2},{3,4},{5,6},{7,8},{9,10},{11,12},{13,14},{2,1},{4,3},{6,5},{... | collective-permute-start | bytes 1769480 | tf_op jit(solution)/shard_map/ppermute | solution.py:436
  7.0 19.0 %collective-permute-start = (f32[1,576,128]{2,1,0:T(8,128)S(1)}, f32[1,576,128]{2,1,0:T(8,128)S(1)}, u32[]{:S(2)}, u32[]{:S(2)}) collective-permute-start(f32[1,576,128]{2,1,0:T(8,128)S(1)} %get-tuple-element.25), channel_id=1, source_target_pairs={{1,2},{3,4},{5,6},{7,8},{9,10},{11,12},{13,14},{2,1},{4,3},{6,5},{... | collective-permute-start | bytes 884744 | tf_op jit(solution)/shard_map/ppermute | solution.py:436
  8.9 2.5 %collective-permute-start.2 = (f32[3,576,128]{2,1,0:T(8,128)S(1)}, f32[3,576,128]{2,1,0:T(8,128)S(1)}, u32[]{:S(2)}, u32[]{:S(2)}) collective-permute-start(f32[3,576,128]{2,1,0:T(8,128)S(1)} %get-tuple-element.27), channel_id=1, source_target_pairs={{0,1},{2,3},{4,5},{6,7},{8,9},{10,11},{12,13},{14,15},{1,0},{3,2},... | collective-permute-start | bytes 2654216 | tf_op jit(solution)/shard_map/ppermute | solution.py:436
  11.4 11.0 %copy-start = (bf16[1152,1152]{1,0:T(8,128)(2,1)S(1)}, bf16[1152,1152]{1,0:T(8,128)(2,1)}, u32[]{:S(2)}) copy-start(bf16[1152,1152]{1,0:T(8,128)(2,1)} %matrix_ref.7) | copy-start | bytes 7962628
  11.4 11.0 %copy-start.1 = (s32[3,128]{1,0:T(4,128)S(1)}, s32[3,128]{1,0:T(4,128)}, u32[]{:S(2)}) copy-start(s32[3,128]{1,0:T(4,128)} %ice_ref.7) | copy-start | bytes 4612
  11.4 11.0 %copy-start.2 = (f32[3,128]{1,0:T(4,128)S(1)}, f32[3,128]{1,0:T(4,128)}, u32[]{:S(2)}) copy-start(f32[3,128]{1,0:T(4,128)} %wind_ref.7) | copy-start | bytes 4612
  29.0 13.1 %collective-permute-start.4 = (f32[2,576,128]{2,1,0:T(8,128)S(1)}, f32[2,576,128]{2,1,0:T(8,128)S(1)}, u32[]{:S(2)}, u32[]{:S(2)}) collective-permute-start(f32[2,576,128]{2,1,0:T(8,128)S(1)} %get-tuple-element.33), channel_id=1, source_target_pairs={{1,2},{3,4},{5,6},{7,8},{9,10},{11,12},{13,14},{2,1},{4,3},{6,5},{... | collective-permute-start | bytes 1769480 | tf_op jit(solution)/shard_map/ppermute | solution.py:436
  34.3 11.3 %collective-permute-start.3 = (f32[1,576,128]{2,1,0:T(8,128)S(1)}, f32[1,576,128]{2,1,0:T(8,128)S(1)}, u32[]{:S(2)}, u32[]{:S(2)}) collective-permute-start(f32[1,576,128]{2,1,0:T(8,128)S(1)} %get-tuple-element.32), channel_id=1, source_target_pairs={{1,2},{3,4},{5,6},{7,8},{9,10},{11,12},{13,14},{2,1},{4,3},{6,5},{... | collective-permute-start | bytes 884744 | tf_op jit(solution)/shard_map/ppermute | solution.py:436
  36.2 2.5 %collective-permute-start.5 = (f32[3,576,128]{2,1,0:T(8,128)S(1)}, f32[3,576,128]{2,1,0:T(8,128)S(1)}, u32[]{:S(2)}, u32[]{:S(2)}) collective-permute-start(f32[3,576,128]{2,1,0:T(8,128)S(1)} %get-tuple-element.34), channel_id=1, source_target_pairs={{0,1},{2,3},{4,5},{6,7},{8,9},{10,11},{12,13},{14,15},{1,0},{3,2},... | collective-permute-start | bytes 2654216 | tf_op jit(solution)/shard_map/ppermute | solution.py:436

commit v10 on v9

--- a/solution.py
+++ b/solution.py
@@ -141,11 +141,11 @@
     return found
 
 
-def shares(q, coefficients, seas, halo):
+def shares(beside_of, coefficients, seas, halo):
     staying, along, across = coefficients
     rows = []
     for j in range(SUBSTEPS):
-        near = [None if value is None else beside(q, value) if known is None else known for value, known in rows]
+        near = [None if value is None else beside_of(value) if known is None else known for value, known in rows]
         new = []
         for i in range(j + 1):
             own = rows[i][0] if i < len(rows) else None
@@ -156,10 +156,25 @@
             if upstream is not None:
                 value = across * upstream if value is None else value + across * upstream
                 if i and own is None and j + 1 < SUBSTEPS:
-                    known = beside(q, seas[i]) * (across * near[i - 1])
+                    known = beside_of(seas[i]) * (across * near[i - 1])
             new.append((None if value is None else seas[i] * value, known))
         rows = new
     return [value for value, _ in rows]
+
+
+def inward_shares(trig_ref, block, seas, halo):
+    pair = [q for q in range(QUADRANTS) if INWARD[q]]
+    coefficients = block_coefficients(trig_ref, block)
+    stacked = [jnp.stack([coefficients[q][i] for q in pair]) for i in range(3)]
+
+    def beside_of(value):
+        if value.ndim == 2:
+            return jnp.stack([beside(q, value)[None] for q in pair])
+        return jnp.stack([beside(q, value[i]) for i, q in enumerate(pair)])
+
+    found = shares(beside_of, stacked, seas, [None if refs is None else jnp.stack([get(*refs, half_at(block, q)) for q in pair])
+                                              for refs in halo])
+    return {q: [None if value is None else value[i] for value in found] for i, q in enumerate(pair)}
 
 
 def with_shares(q, values, part):
@@ -271,7 +286,7 @@
                 at, half = quadrant_at(block, q), half_at(block, q)
                 halo = [get(inner_ref, j, half) for j in range(SUBSTEPS)]
                 values = [get(local_ref, r, at) for r in range(count)]
-                for r, value in enumerate(with_shares(q, values, shares(q, coefficients, flow(q, seas), halo))):
+                for r, value in enumerate(with_shares(q, values, shares(functools.partial(beside, q), coefficients, flow(q, seas), halo))):
                     put(out_ref, r, half, value)
         return carry
 
@@ -345,12 +360,12 @@
     rows = range(near, count)
 
     def advance(block, sums):
-        for q, coefficients in enumerate(block_coefficients(trig_ref, block)):
+        halo = [(cross_ref, j) if j < early else None for j in range(SUBSTEPS)]
+        inward = inward_shares(trig_ref, block, seas, halo)
+        for q in range(QUADRANTS):
             at, half = quadrant_at(block, q), half_at(block, q)
             if INWARD[q]:
-                halo = [get(cross_ref, j, half) if j < early else None for j in range(SUBSTEPS)]
-                values = [get(local_ref, r, at) for r in range(count)]
-                values = with_shares(q, values, shares(q, coefficients, seas, halo))
+                values = with_shares(q, [get(local_ref, r, at) for r in range(count)], inward[q])
             else:
                 values = [get(outward_ref, r, half) for r in range(count)]
             for r, value in enumerate(values):
@@ -361,7 +376,7 @@
         return tuple(hold(odd, block, i, moved, f_acc, b_acc, iota, total) for i, total in enumerate(sums))
 
     zero = jnp.zeros((SUB, width), jnp.float32)
-    sums = lax.fori_loop(0, BLOCKS, advance, (zero,) * len(rows))
+    sums = lax.fori_loop(0, BLOCKS, advance, (zero,) * len(rows), unroll=True)
     def ready(block, at):
         if last:
             for i in range(len(rows)):
@@ -389,18 +404,19 @@
             copy.start()
 
     def advance(block, sums):
-        for q, coefficients in enumerate(block_coefficients(trig_ref, block)):
+        halo = [None] * (SUBSTEPS - late) + [(late_ref, j) for j in range(late)]
+        inward = inward_shares(trig_ref, block, seas, halo)
+        for q in range(QUADRANTS):
             at = quadrant_at(block, q)
             values = [get(part_ref, r, at) for r in range(near)]
             if INWARD[q]:
-                halo = [None] * (SUBSTEPS - late) + [get(late_ref, j, half_at(block, q)) for j in range(late)]
-                values = with_shares(q, values, shares(q, coefficients, seas, halo))
+                values = with_shares(q, values, inward[q])
             for r, value in enumerate(values):
                 put(moved, r, at, value)
         return tuple(hold(odd, block, i, moved, f_acc, b_acc, iota, total) for i, total in enumerate(sums))
 
     zero = jnp.zeros((SUB, width), jnp.float32)
-    sums = lax.fori_loop(0, BLOCKS, advance, (zero,) * near)
+    sums = lax.fori_loop(0, BLOCKS, advance, (zero,) * near, unroll=True)
     if last:
         def ready(c, at):
             for r in range(near):

time: 49.4 us -> 48.6 us (0.984)
  Pallas kernels: 23.3 us -> 22.3 us
    pallas_call x11, Pallas kernels: 23.3 us -> 22.3 us  [call(): pl.pallas_call(kernel, out_shape=outs, name=name, in_specs=[pl.BlockSpec(...]
  transfers between devices with their start and end apart: 6 -> 6, of which waited for: 2 -> 2; matrix products, arithmetic and copies ran while one was open for 0% -> 0% of each run, Pallas kernels for 31% -> 30%
where the time goes in v10:
time: 48.6 us; the launch traced here: 48.4 us
  Pallas kernels  22.3 us (46%)
  starting transfers between devices  13.1 us (27%)
  waiting for transfers between devices  12.6 us (26%)
    pallas_call x11, Pallas kernels, call(): pl.pallas_call(kernel, out_shape=outs, name=name, in_specs=[pl.BlockSpec(...  22.3 us
    ppermute x6, starting transfers between devices, swap(): return lax.ppermute(value, 'comp', pairs + [(j, i) for i, j in pairs])  13.1 us
    ppermute x6, waiting for transfers between devices, swap(): return lax.ppermute(value, 'comp', pairs + [(j, i) for i, j in pairs])  12.6 us
  transfers between devices with their start and end apart: 6, of which 2 were waited for; matrix products, arithmetic and copies ran while one was open for 0% of the time, Pallas kernels for 30%

profile of v10, /device:TPU:1, one launch (start us, length us, event | category | flops | bytes accessed | tf_op | source)
XLA Modules:
  0.0 48.4 jit_solution(14564365247808194326)
XLA Ops:
  0.0 1.6 %first_edges.1 = (f32[2,1152,128]{2,1,0:T(8,128)S(1)}, f32[1,1152,128]{2,1,0:T(8,128)S(1)}, s32[3,128]{1,0:T(4,128)S(1)}, f32[3,72,128]{2,1,0:T(8,128)S(1)}, f32[2,576,128]{2,1,0:T(8,128)S(1)}) custom-call(s32[1]{0:T(128)} %bitcast.odd_ref, f32[3,1152,128]{2,1,0:T(8,128)} %bitcast.3, s32[3,128]{1,0:T(4,128)} %sea_hbm.1), custom_call_target="tpu_custom_call" | custom-call | tf_op jit(solution)/shard_map/first_edges/pallas_call | solution.py:465
  1.6 4.5 %collective-permute-start.1 = (f32[2,576,128]{2,1,0:T(8,128)S(1)}, f32[2,576,128]{2,1,0:T(8,128)S(1)}, u32[]{:S(2)}, u32[]{:S(2)}) collective-permute-start(f32[2,576,128]{2,1,0:T(8,128)S(1)} %get-tuple-element.26), channel_id=1, source_target_pairs={{1,2},{3,4},{5,6},{7,8},{9,10},{11,12},{13,14},{2,1},{4,3},{6,5},{... | collective-permute-start | bytes 1769480 | tf_op jit(solution)/shard_map/ppermute | solution.py:452
  6.1 0.9 %late_edges.2 = (f32[1,576,128]{2,1,0:T(8,128)S(1)}, f32[3,576,128]{2,1,0:T(8,128)S(1)}, f32[1,1152,128]{2,1,0:T(8,128)S(1)}) custom-call(s32[1]{0:T(128)} %bitcast.odd_ref, s32[3,128]{1,0:T(4,128)S(1)} %get-tuple-element.21.sea_ref, f32[3,72,128]{2,1,0:T(8,128)S(1)} %get-tuple-element.22.trig_ref, f32[2,1152,128]{2,1,0:T(8,128)S(1)} %get-tuple-element.23.refs_0_, ...), custom_call_target="tpu_custom_call" | custom-call | tf_op jit(solution)/shard_map/late_edges/pallas_call | solution.py:465
  7.0 1.9 %collective-permute-start = (f32[1,576,128]{2,1,0:T(8,128)S(1)}, f32[1,576,128]{2,1,0:T(8,128)S(1)}, u32[]{:S(2)}, u32[]{:S(2)}) collective-permute-start(f32[1,576,128]{2,1,0:T(8,128)S(1)} %get-tuple-element.25), channel_id=1, source_target_pairs={{1,2},{3,4},{5,6},{7,8},{9,10},{11,12},{13,14},{2,1},{4,3},{6,5},{... | collective-permute-start | bytes 884744 | tf_op jit(solution)/shard_map/ppermute | solution.py:452
  8.9 0.1 collective-permute-start.2
  9.0 2.4 %local_rows.2.local_ref = f32[3,1152,128]{2,1,0:T(8,128)S(1)} custom-call(s32[3,128]{1,0:T(4,128)S(1)} %get-tuple-element.21.sea_ref, f32[3,72,128]{2,1,0:T(8,128)S(1)} %get-tuple-element.22.trig_ref, f32[2,1152,128]{2,1,0:T(8,128)S(1)} %get-tuple-element.23.refs_0_, f32[1,1152,128]{2,1,0:T(8,128)S(1)} %get-tuple-element.28.refs_1_), custom_call_target="tpu_custom_call" | custom-call | flops 30000001024 | tf_op jit(solution)/shard_map/local_rows/pallas_call | solution.py:465
  11.4 0.0 copy-start
  11.4 0.0 copy-start.1
  11.4 0.0 copy-start.2
  11.4 0.0 collective-permute-done.2.inner_ref
  11.5 0.8 %outward_rows.2.outward_ref = f32[3,576,128]{2,1,0:T(8,128)S(1)} custom-call(s32[3,128]{1,0:T(4,128)S(1)} %get-tuple-element.21.sea_ref, f32[3,72,128]{2,1,0:T(8,128)S(1)} %get-tuple-element.22.trig_ref, f32[3,576,128]{2,1,0:T(8,128)S(1)} %collective-permute-done.2.inner_ref, f32[3,1152,128]{2,1,0:T(8,128)S(1)} %local_rows.2.local_ref), custom_call_target="tpu_custom_call" | custom-call | tf_op jit(solution)/shard_map/outward_rows/pallas_call | solution.py:465
  12.2 10.2 %collective-permute-done.1.cross_ref = f32[2,576,128]{2,1,0:T(8,128)S(1)} collective-permute-done((f32[2,576,128]{2,1,0:T(8,128)S(1)}, f32[2,576,128]{2,1,0:T(8,128)S(1)}, u32[]{:S(2)}, u32[]{:S(2)}) %collective-permute-start.1) | collective-permute-done | bytes 589856 | tf_op jit(solution)/shard_map/ppermute | solution.py:452
  22.4 0.0 copy-done
  22.4 0.0 copy-done.1
  22.4 0.0 copy-done.2
  22.4 3.3 %far_rows.2 = (f32[2,1152,128]{2,1,0:T(8,128)S(1)}, f32[1,1152,128]{2,1,0:T(8,128)S(1)}) custom-call(s32[1]{0:T(128)} %bitcast.odd_ref, s32[3,128]{1,0:T(4,128)S(1)} %get-tuple-element.21.sea_ref, s32[3,128]{1,0:T(4,128)S(1)} %copy-done.1, f32[3,128]{1,0:T(4,128)S(1)} %copy-done.2, f32[3,72,128]{2,1,0:T(8,128)S(1)} %get-tuple-element.22.trig_ref, ...), custom_call_target="tpu_custom_call" | custom-call | tf_op jit(solution)/shard_map/far_rows/pallas_call | solution.py:465
  25.7 0.0 collective-permute-done.late_ref
  25.7 2.8 %near_rows.2 = (f32[1,1152,128]{2,1,0:T(8,128)S(1)}, f32[2,576,128]{2,1,0:T(8,128)S(1)}) custom-call(s32[1]{0:T(128)} %bitcast.odd_ref, s32[3,128]{1,0:T(4,128)S(1)} %get-tuple-element.21.sea_ref, s32[3,128]{1,0:T(4,128)S(1)} %copy-done.1, f32[3,128]{1,0:T(4,128)S(1)} %copy-done.2, f32[3,72,128]{2,1,0:T(8,128)S(1)} %get-tuple-element.22.trig_ref, ...), custom_call_target="tpu_custom_call" | custom-call | tf_op jit(solution)/shard_map/near_rows/pallas_call | solution.py:465
  28.5 4.4 %collective-permute-start.4 = (f32[2,576,128]{2,1,0:T(8,128)S(1)}, f32[2,576,128]{2,1,0:T(8,128)S(1)}, u32[]{:S(2)}, u32[]{:S(2)}) collective-permute-start(f32[2,576,128]{2,1,0:T(8,128)S(1)} %get-tuple-element.33), channel_id=1, source_target_pairs={{1,2},{3,4},{5,6},{7,8},{9,10},{11,12},{13,14},{2,1},{4,3},{6,5},{... | collective-permute-start | bytes 1769480 | tf_op jit(solution)/shard_map/ppermute | solution.py:452
  33.0 0.9 %late_edges.3 = (f32[1,576,128]{2,1,0:T(8,128)S(1)}, f32[3,576,128]{2,1,0:T(8,128)S(1)}) custom-call(s32[1]{0:T(128)} %bitcast.odd_ref, s32[3,128]{1,0:T(4,128)S(1)} %get-tuple-element.21.sea_ref, f32[3,72,128]{2,1,0:T(8,128)S(1)} %get-tuple-element.22.trig_ref, f32[1,1152,128]{2,1,0:T(8,128)S(1)} %get-tuple-element.31.refs_0_, ...), custom_call_target="tpu_custom_call" | custom-call | tf_op jit(solution)/shard_map/late_edges/pallas_call | solution.py:465
  33.8 2.1 %collective-permute-start.3 = (f32[1,576,128]{2,1,0:T(8,128)S(1)}, f32[1,576,128]{2,1,0:T(8,128)S(1)}, u32[]{:S(2)}, u32[]{:S(2)}) collective-permute-start(f32[1,576,128]{2,1,0:T(8,128)S(1)} %get-tuple-element.32), channel_id=1, source_target_pairs={{1,2},{3,4},{5,6},{7,8},{9,10},{11,12},{13,14},{2,1},{4,3},{6,5},{... | collective-permute-start | bytes 884744 | tf_op jit(solution)/shard_map/ppermute | solution.py:452
  35.9 0.1 collective-permute-start.5
  36.0 2.4 %local_rows.3.local_ref = f32[3,1152,128]{2,1,0:T(8,128)S(1)} custom-call(s32[3,128]{1,0:T(4,128)S(1)} %get-tuple-element.21.sea_ref, f32[3,72,128]{2,1,0:T(8,128)S(1)} %get-tuple-element.22.trig_ref, f32[1,1152,128]{2,1,0:T(8,128)S(1)} %get-tuple-element.31.refs_0_, f32[2,1152,128]{2,1,0:T(8,128)S(1)} %get-tuple-element.30.far_ref.refs_1_), custom_call_target="tpu_custom_call" | custom-call | flops 30000001024 | tf_op jit(solution)/shard_map/local_rows/pallas_call | solution.py:465
  38.4 0.0 collective-permute-done.5.inner_ref
  38.4 0.8 %outward_rows.3.outward_ref = f32[3,576,128]{2,1,0:T(8,128)S(1)} custom-call(s32[3,128]{1,0:T(4,128)S(1)} %get-tuple-element.21.sea_ref, f32[3,72,128]{2,1,0:T(8,128)S(1)} %get-tuple-element.22.trig_ref, f32[3,576,128]{2,1,0:T(8,128)S(1)} %collective-permute-done.5.inner_ref, f32[3,1152,128]{2,1,0:T(8,128)S(1)} %local_rows.3.local_ref), custom_call_target="tpu_custom_call" | custom-call | tf_op jit(solution)/shard_map/outward_rows/pallas_call | solution.py:465
  39.2 2.4 %collective-permute-done.4.cross_ref = f32[2,576,128]{2,1,0:T(8,128)S(1)} collective-permute-done((f32[2,576,128]{2,1,0:T(8,128)S(1)}, f32[2,576,128]{2,1,0:T(8,128)S(1)}, u32[]{:S(2)}, u32[]{:S(2)}) %collective-permute-start.4) | collective-permute-done | bytes 589856 | tf_op jit(solution)/shard_map/ppermute | solution.py:452
  41.7 3.1 %far_rows.3 = (f32[2,1152,128]{2,1,0:T(8,128)S(1)}, f32[1,1152,128]{2,1,0:T(8,128)S(1)}) custom-call(s32[1]{0:T(128)} %bitcast.odd_ref, s32[3,128]{1,0:T(4,128)S(1)} %get-tuple-element.21.sea_ref, s32[3,128]{1,0:T(4,128)S(1)} %copy-done.1, f32[3,128]{1,0:T(4,128)S(1)} %copy-done.2, f32[3,72,128]{2,1,0:T(8,128)S(1)} %get-tuple-element.22.trig_ref, ...), custom_call_target="tpu_custom_call" | custom-call | tf_op jit(solution)/shard_map/far_rows/pallas_call | solution.py:465
  44.8 0.0 collective-permute-done.3.late_ref
  44.8 3.4 %near_rows.3 = f32[3,1152,128]{2,1,0:T(8,128)} custom-call(s32[1]{0:T(128)} %bitcast.odd_ref, s32[3,128]{1,0:T(4,128)S(1)} %get-tuple-element.21.sea_ref, s32[3,128]{1,0:T(4,128)S(1)} %copy-done.1, f32[3,128]{1,0:T(4,128)S(1)} %copy-done.2, f32[3,72,128]{2,1,0:T(8,128)S(1)} %get-tuple-element.22.trig_ref, bf16[1152,1152]{1,0:T(8,128)(2,1)S(1)} %copy-done, ...), custom_call_target="tpu_custom_call" | custom-call | tf_op jit(solution)/shard_map/near_rows/pallas_call | solution.py:465
Async XLA Ops:
  1.6 20.8 %collective-permute-start.1 = (f32[2,576,128]{2,1,0:T(8,128)S(1)}, f32[2,576,128]{2,1,0:T(8,128)S(1)}, u32[]{:S(2)}, u32[]{:S(2)}) collective-permute-start(f32[2,576,128]{2,1,0:T(8,128)S(1)} %get-tuple-element.26), channel_id=1, source_target_pairs={{1,2},{3,4},{5,6},{7,8},{9,10},{11,12},{13,14},{2,1},{4,3},{6,5},{... | collective-permute-start | bytes 1769480 | tf_op jit(solution)/shard_map/ppermute | solution.py:452
  7.0 18.7 %collective-permute-start = (f32[1,576,128]{2,1,0:T(8,128)S(1)}, f32[1,576,128]{2,1,0:T(8,128)S(1)}, u32[]{:S(2)}, u32[]{:S(2)}) collective-permute-start(f32[1,576,128]{2,1,0:T(8,128)S(1)} %get-tuple-element.25), channel_id=1, source_target_pairs={{1,2},{3,4},{5,6},{7,8},{9,10},{11,12},{13,14},{2,1},{4,3},{6,5},{... | collective-permute-start | bytes 884744 | tf_op jit(solution)/shard_map/ppermute | solution.py:452
  8.9 2.5 %collective-permute-start.2 = (f32[3,576,128]{2,1,0:T(8,128)S(1)}, f32[3,576,128]{2,1,0:T(8,128)S(1)}, u32[]{:S(2)}, u32[]{:S(2)}) collective-permute-start(f32[3,576,128]{2,1,0:T(8,128)S(1)} %get-tuple-element.27), channel_id=1, source_target_pairs={{0,1},{2,3},{4,5},{6,7},{8,9},{10,11},{12,13},{14,15},{1,0},{3,2},... | collective-permute-start | bytes 2654216 | tf_op jit(solution)/shard_map/ppermute | solution.py:452
  11.4 11.0 %copy-start = (bf16[1152,1152]{1,0:T(8,128)(2,1)S(1)}, bf16[1152,1152]{1,0:T(8,128)(2,1)}, u32[]{:S(2)}) copy-start(bf16[1152,1152]{1,0:T(8,128)(2,1)} %matrix_ref.7) | copy-start | bytes 7962628
  11.4 11.0 %copy-start.1 = (s32[3,128]{1,0:T(4,128)S(1)}, s32[3,128]{1,0:T(4,128)}, u32[]{:S(2)}) copy-start(s32[3,128]{1,0:T(4,128)} %ice_ref.7) | copy-start | bytes 4612
  11.4 11.0 %copy-start.2 = (f32[3,128]{1,0:T(4,128)S(1)}, f32[3,128]{1,0:T(4,128)}, u32[]{:S(2)}) copy-start(f32[3,128]{1,0:T(4,128)} %wind_ref.7) | copy-start | bytes 4612
  28.5 13.1 %collective-permute-start.4 = (f32[2,576,128]{2,1,0:T(8,128)S(1)}, f32[2,576,128]{2,1,0:T(8,128)S(1)}, u32[]{:S(2)}, u32[]{:S(2)}) collective-permute-start(f32[2,576,128]{2,1,0:T(8,128)S(1)} %get-tuple-element.33), channel_id=1, source_target_pairs={{1,2},{3,4},{5,6},{7,8},{9,10},{11,12},{13,14},{2,1},{4,3},{6,5},{... | collective-permute-start | bytes 1769480 | tf_op jit(solution)/shard_map/ppermute | solution.py:452
  33.8 11.0 %collective-permute-start.3 = (f32[1,576,128]{2,1,0:T(8,128)S(1)}, f32[1,576,128]{2,1,0:T(8,128)S(1)}, u32[]{:S(2)}, u32[]{:S(2)}) collective-permute-start(f32[1,576,128]{2,1,0:T(8,128)S(1)} %get-tuple-element.32), channel_id=1, source_target_pairs={{1,2},{3,4},{5,6},{7,8},{9,10},{11,12},{13,14},{2,1},{4,3},{6,5},{... | collective-permute-start | bytes 884744 | tf_op jit(solution)/shard_map/ppermute | solution.py:452
  35.9 2.5 %collective-permute-start.5 = (f32[3,576,128]{2,1,0:T(8,128)S(1)}, f32[3,576,128]{2,1,0:T(8,128)S(1)}, u32[]{:S(2)}, u32[]{:S(2)}) collective-permute-start(f32[3,576,128]{2,1,0:T(8,128)S(1)} %get-tuple-element.34), channel_id=1, source_target_pairs={{0,1},{2,3},{4,5},{6,7},{8,9},{10,11},{12,13},{14,15},{1,0},{3,2},... | collective-permute-start | bytes 2654216 | tf_op jit(solution)/shard_map/ppermute | solution.py:452
